TPU v7x, 256 devices: a whole 4x4x8 slice. The times are simulated.
256 devices in a mesh: tm: 64 (over x_lo, y, z), head: 4 (over x_hi, core).
Axes of the slice: x: 4 (x_hi: 2, x_lo: 2; x = x_hi * 2 + x_lo), y: 4, z: 8, core: 2. Of those that a mesh axis runs over, the one named last changes fastest.
Arguments:
- frames_in: bfloat16 [256, 256, 512], P('tm'), may hold values from -6 to 6
- norm_gain: float32 [512], replicated, may hold values from 0.1 to 1.9
- w_qkv: bfloat16 [512, 3, 512], P(None, None, 'head'), may hold values from -0.25 to 0.25
- qk_scale: float32 [8], P('head'), may hold values from 0.5 to 4
- w_out: bfloat16 [512, 512], P('head'), may hold values from -0.25 to 0.25
- w_act: float32 [2, 512, 4], P(None, 'head'), may hold values from -3 to 3
- action_codes: int32 [256], P('tm'), may hold values from 0 to 999
- episode_ids: int32 [256], replicated, may hold values from 0 to 3, never falling along the last dimension, each value on 1 to 128 neighbouring positions
- cotangent: bfloat16 [256, 256, 512], P('tm', None, 'head'), may hold values from -6 to 6
- action_cotangent: float32 [256, 4], P('tm'), may hold values from -192 to 192
Outputs:
- encoded: bfloat16 [256, 256, 512], P('tm', None, 'head')
- quant_gap: float32 [256, 4], P('tm')
- grad_frames: bfloat16 [256, 256, 512], P('tm', None, 'head')
- grad_gain: float32 [512], P('head')
- grad_qkv: float32 [512, 3, 512], P(None, None, 'head')
- grad_qk_scale: float32 [8], P('head')
- grad_out: float32 [512, 512], P('head')
- grad_act: float32 [2, 512, 4], P(None, 'head')
Inputs may be any that keep to these rules, and one draw needn't show every extreme that they name: `action_codes`: each frame's action code; digit l in the radix 8, 5, 5, 5, lowest first, picks the level of dimension l. `episode_ids`: never falls from one frame to the next; each episode is one run of 1 to 128 frames, and one run is exactly 128 frames long.
All inputs are finite; a program needn't handle non-finite values.
Results may differ from a plain program's by a relative error of at most 0.025.
Values may be sent and summed in bfloat16 or wider, within the bound.
No kernel may reach another device: no remote copies, remote signals or barrier semaphores. Data moves between devices by JAX's collectives and lax.ppermute only.
A program may use at most 64 MiB of HBM per device.

v0:
```python
import math

import jax
import jax.numpy as jnp
import numpy as np
from jax import lax
from jax.sharding import PartitionSpec as P

LAG = 16


EPS = 1e-06
HIGHEST = lax.Precision.HIGHEST
CONTRACT_LAST = (((1,), (1,)), ((), ()))
CONTRACT_FIRST = (((0,), (0,)), ((), ()))


def passed_along(value, axis, steps):
    count = lax.axis_size(axis)
    leading, last = (max(0, -steps), min(count, count - steps))
    return lax.ppermute(value, axis, [(source, source + steps) for source in range(leading, last)])


def level_tables():
    sizes_list = [8.0, 5.0, 5.0, 5.0]
    half_list = [(count - 1.0) * (1.0 - 0.001) / 2.0 for count in sizes_list]
    offset_list = [0.5 if int(count) % 2 == 0 else 0.0 for count in sizes_list]
    shift_list = [
        0.5 * math.log((half_list[i] + offset_list[i]) / (half_list[i] - offset_list[i]))
        for i in range(4)
    ]
    width_list = [float(int(count) // 2) for count in sizes_list]
    return (np.array(half_list), np.array(offset_list), np.array(shift_list), np.array(width_list))


def code_values(action_codes, widths):
    bases = jnp.array([1, 8, 40, 200], dtype=jnp.int32)
    radices = jnp.array([8, 5, 5, 5], dtype=jnp.int32)
    digits = action_codes[:, None] // bases[None, :] % radices[None, :]
    return (digits.astype(jnp.float32) - widths) / widths


def rms_scale(values):
    return lax.rsqrt(jnp.mean(values * values, axis=-1, keepdims=True) + EPS)


def local(
    frames_in,
    norm_gain,
    w_qkv,
    qk_scale,
    w_out,
    w_act,
    action_codes,
    episode_ids,
    cotangent,
    action_cotangent,
):
    frames_local, patches, width = frames_in.shape
    heads_local = qk_scale.shape[0]
    channels = w_out.shape[0]
    head_dim = channels // heads_local
    share = cotangent.shape[2]
    tm_count = lax.axis_size("tm")
    total_frames = frames_local * tm_count
    patch_share = patches // tm_count
    token_count = total_frames * patches
    col_start = lax.axis_index("head") * share
    reach = LAG // frames_local
    floats = frames_in.astype(jnp.float32)
    inverse = rms_scale(floats)
    normed = (floats * inverse * norm_gain).astype(jnp.bfloat16)
    normed_flat = normed.reshape(-1, width)
    qkv_flat = w_qkv.reshape(width, 3 * channels)
    projected = jnp.dot(normed_flat, qkv_flat, preferred_element_type=jnp.float32)
    projected = projected.reshape(frames_local, patches, 3, heads_local, head_dim)
    query_raw = projected[:, :, 0]
    keys_raw = projected[:, :, 1]
    query_inv = rms_scale(query_raw)
    keys_inv = rms_scale(keys_raw)
    query = (query_raw * query_inv).astype(jnp.bfloat16).reshape(frames_local, patches, channels)
    keys = (keys_raw * keys_inv).astype(jnp.bfloat16).reshape(frames_local, patches, channels)
    values = projected[:, :, 2].astype(jnp.bfloat16).reshape(frames_local, patches, channels)
    query_patch, keys_patch, values_patch = (
        lax.all_to_all(query, "tm", split_axis=1, concat_axis=0, tiled=True),
        lax.all_to_all(keys, "tm", split_axis=1, concat_axis=0, tiled=True),
        lax.all_to_all(values, "tm", split_axis=1, concat_axis=0, tiled=True),
    )
    patch_shape = (total_frames, patch_share, heads_local, head_dim)
    query_patch = query_patch.reshape(patch_shape)
    keys_patch = keys_patch.reshape(patch_shape)
    values_patch = values_patch.reshape(patch_shape)
    order = jnp.arange(total_frames, dtype=jnp.int32)
    visible = jnp.logical_and(
        episode_ids[:, None] == episode_ids[None, :], order[None, :] <= order[:, None]
    )
    factor = qk_scale * (1.0 / math.sqrt(head_dim))
    dots = jnp.einsum(
        "tphd,uphd->phtu", query_patch, keys_patch, preferred_element_type=jnp.float32
    )
    scores = dots * factor[None, :, None, None]
    weights = jnp.where(visible[None, None], jnp.exp(scores), 0.0)
    probs = weights / jnp.sum(weights, axis=-1, keepdims=True)
    rounded = probs.astype(jnp.bfloat16)
    attended_patch = jnp.einsum(
        "phtu,uphd->tphd", rounded, values_patch, preferred_element_type=jnp.float32
    ).astype(jnp.bfloat16)
    attended = lax.all_to_all(
        attended_patch.reshape(total_frames, patch_share, channels),
        "tm",
        split_axis=0,
        concat_axis=1,
        tiled=True,
    )
    attended_flat = attended.reshape(-1, channels)
    partial_sums = jnp.dot(attended_flat, w_out, preferred_element_type=jnp.float32).reshape(
        frames_local, patches, width
    )
    branch = lax.psum_scatter(
        partial_sums.astype(jnp.bfloat16), "head", scatter_dimension=2, tiled=True
    ).astype(jnp.float32)
    floats_share = lax.dynamic_slice_in_dim(floats, col_start, share, 2)
    encoded = (floats_share + branch).astype(jnp.bfloat16)
    pooled = jnp.sum(encoded, axis=1, dtype=jnp.float32) / patches
    partner = passed_along(pooled, "tm", -reach)
    latent_part = jnp.dot(pooled, w_act[0], precision=HIGHEST) + jnp.dot(
        partner, w_act[1], precision=HIGHEST
    )
    latent = lax.psum(latent_part, "head")
    half_level, offsets, shifts, widths = level_tables()
    curve = jnp.tanh(latent + shifts)
    bounded = (curve * half_level - offsets) / widths
    quant_gap = code_values(action_codes, widths) - bounded
    grad_latent = action_cotangent * (half_level / widths) * (1.0 - curve * curve)
    grad_act_part = jnp.stack(
        [
            jnp.dot(pooled.T, grad_latent, precision=HIGHEST),
            jnp.dot(partner.T, grad_latent, precision=HIGHEST),
        ]
    )
    own_part = jnp.dot(grad_latent, w_act[0].T, precision=HIGHEST)
    partner_part = jnp.dot(grad_latent, w_act[1].T, precision=HIGHEST)
    moved_part = passed_along(partner_part, "tm", reach)
    grad_pooled = (own_part + moved_part) / patches
    upstream = (cotangent.astype(jnp.float32) + grad_pooled[:, None, :]).astype(jnp.bfloat16)
    upstream_flat = upstream.reshape(-1, share)
    piece = lax.all_gather(upstream_flat, "head", axis=1, tiled=True)
    grad_attn = lax.dot_general(piece, w_out, CONTRACT_LAST, preferred_element_type=jnp.float32)
    block = lax.dot_general(
        attended_flat, piece, CONTRACT_FIRST, preferred_element_type=jnp.float32
    )
    grad_weights = block
    grad_attn, grad_weights = (grad_attn, grad_weights)
    grad_attended = grad_attn.astype(jnp.bfloat16).reshape(frames_local, patches, channels)
    grad_patch = lax.all_to_all(
        grad_attended, "tm", split_axis=1, concat_axis=0, tiled=True
    ).reshape(patch_shape)
    grad_probs = jnp.einsum(
        "tphd,uphd->phtu", grad_patch, values_patch, preferred_element_type=jnp.float32
    )
    grad_values = jnp.einsum(
        "phtu,tphd->uphd", rounded, grad_patch, preferred_element_type=jnp.float32
    ).astype(jnp.bfloat16)
    grad_scores = probs * (grad_probs - jnp.sum(grad_probs * probs, axis=-1, keepdims=True))
    scale_part = jnp.sum(grad_scores * dots, axis=(0, 2, 3))
    grad_rounded = grad_scores.astype(jnp.bfloat16)
    head_factor = factor[None, None, :, None]
    grad_query_normed = head_factor * jnp.einsum(
        "phtu,uphd->tphd", grad_rounded, keys_patch, preferred_element_type=jnp.float32
    )
    grad_keys_normed = head_factor * jnp.einsum(
        "phtu,tphd->uphd", grad_rounded, query_patch, preferred_element_type=jnp.float32
    )
    query_back = (
        grad_query_normed
        - query_patch * jnp.mean(grad_query_normed * query_patch, axis=-1, keepdims=True)
    ).astype(jnp.bfloat16)
    keys_back = (
        grad_keys_normed
        - keys_patch * jnp.mean(grad_keys_normed * keys_patch, axis=-1, keepdims=True)
    ).astype(jnp.bfloat16)
    flat_shape = (total_frames, patch_share, channels)
    query_home, keys_home, values_home = (
        lax.all_to_all(
            query_back.reshape(flat_shape), "tm", split_axis=0, concat_axis=1, tiled=True
        ),
        lax.all_to_all(
            keys_back.reshape(flat_shape), "tm", split_axis=0, concat_axis=1, tiled=True
        ),
        lax.all_to_all(
            grad_values.reshape(flat_shape), "tm", split_axis=0, concat_axis=1, tiled=True
        ),
    )
    head_shape = (frames_local, patches, heads_local, head_dim)
    grad_query = query_inv * query_home.reshape(head_shape).astype(jnp.float32)
    grad_keys = keys_inv * keys_home.reshape(head_shape).astype(jnp.float32)
    grad_vals = values_home.reshape(head_shape).astype(jnp.float32)
    grad_projected = (
        jnp.stack([grad_query, grad_keys, grad_vals], axis=2)
        .astype(jnp.bfloat16)
        .reshape(-1, 3 * channels)
    )
    grad_qkv_part = lax.dot_general(
        normed_flat, grad_projected, CONTRACT_FIRST, preferred_element_type=jnp.float32
    ).reshape(width, 3, channels)
    grad_normed_part = lax.dot_general(
        grad_projected, qkv_flat, CONTRACT_LAST, preferred_element_type=jnp.float32
    )
    gain_share = lax.dynamic_slice_in_dim(norm_gain, col_start, share, 0)
    cubed = inverse * inverse * inverse
    grad_normed = (
        lax.psum(grad_normed_part.astype(jnp.bfloat16), "head")
        .astype(jnp.float32)
        .reshape(frames_local, patches, width)
    )
    row_dot = jnp.mean(norm_gain * grad_normed * floats, axis=-1, keepdims=True)
    grad_share = lax.dynamic_slice_in_dim(grad_normed, col_start, share, 2)
    grad_floats = inverse * gain_share * grad_share - floats_share * cubed * row_dot
    gain_part = jnp.sum(grad_share * floats_share * inverse, axis=(0, 1))
    grad_frames = (upstream.astype(jnp.float32) + grad_floats).astype(jnp.bfloat16)
    summed = lax.psum((grad_qkv_part, grad_weights, grad_act_part, gain_part, scale_part), "tm")
    norm_factor = 1.0 / math.sqrt(token_count)
    grad_qkv = summed[0] * norm_factor
    grad_out = summed[1] * norm_factor
    grad_act = summed[2] * (1.0 / math.sqrt(total_frames))
    grad_gain = summed[3] * norm_factor
    grad_qk_scale = summed[4] * (norm_factor / math.sqrt(head_dim))
    return (encoded, quant_gap, grad_frames, grad_gain, grad_qkv, grad_qk_scale, grad_out, grad_act)


def solution(mesh):
    in_specs = (
        P("tm", None, None),
        P(),
        P(None, None, "head"),
        P("head"),
        P("head", None),
        P(None, "head", None),
        P("tm"),
        P(),
        P("tm", None, "head"),
        P("tm", None),
    )
    out_specs = (
        P("tm", None, "head"),
        P("tm", None),
        P("tm", None, "head"),
        P("head"),
        P(None, None, "head"),
        P("head"),
        P("head", None),
        P(None, "head", None),
    )
    return jax.shard_map(local, mesh=mesh, in_specs=in_specs, out_specs=out_specs, check_vma=False)
```

profile of v0, /device:TPU:2, one launch (start us, length us, event | category | flops | bytes accessed | tf_op | source)
XLA Modules:
  0.0 1116.1 jit_solution(5522380472147891418)
XLA Ops:
  15.1 13.2 %all-to-all-start.1 = ((bf16[4,256,128]{2,0,1:T(4,128)(2,1)}), bf16[4,256,128]{2,0,1:T(4,128)(2,1)S(1)}, u32[]{:S(2)}, u32[]{:S(2)}) async-start(bf16[4,256,128]{2,0,1:T(4,128)(2,1)} %copy.150), calls=%async_computation.1 | async-start | bytes 524288 | tf_op jit(solution)/shard_map/all_to_all | solution.py:85
  30.3 11.4 %all-to-all-done.1 = bf16[4,256,128]{2,0,1:T(4,128)(2,1)S(1)} async-done(((bf16[4,256,128]{2,0,1:T(4,128)(2,1)}), bf16[4,256,128]{2,0,1:T(4,128)(2,1)S(1)}, u32[]{:S(2)}, u32[]{:S(2)}) %all-to-all-start.1) | async-done | bytes 262176 | tf_op jit(solution)/shard_map/all_to_all | solution.py:85
  41.7 4.9 all-to-all-start
  48.2 11.0 all-to-all-done
  59.2 4.9 all-to-all-start.2
  68.0 8.2 all-to-all-done.2
  82.5 16.4 %all_to_all.102 = bf16[256,4,128]{2,1,0:T(4,128)(2,1)S(1)} all-to-all(bf16[256,4,128]{2,1,0:T(4,128)(2,1)S(1)} %copy.160), channel_id=1, replica_groups=mesh['tm'=64,'head'=4] {'tm'}, dimensions={0} | all-to-all | bytes 524288 | tf_op jit(solution)/shard_map/all_to_all | solution.py:108
  106.1 29.5 %reduce-scatter.4.cloned.1.call-done = bf16[128,1024]{1,0:T(8,128)(2,1)} async-done(((bf16[512,1024]{1,0:T(8,128)(2,1)}), bf16[128,1024]{1,0:T(8,128)(2,1)}) %reduce-scatter.4.cloned.1.call-update) | async-done | bytes 262160
  138.8 10.7 collective-permute-start
  150.9 7.2 psum.49
  159.2 6.0 collective-permute-start.1
  165.3 6.8 collective-permute-done.1
  173.0 20.2 %all-gather.2.cloned.1.call-done = bf16[1024,512]{1,0:T(8,128)(2,1)} async-done(((bf16[1024,128]{1,0:T(8,128)(2,1)}), bf16[1024,512]{1,0:T(8,128)(2,1)}) %all-gather.2.cloned.1.call-update) | async-done | bytes 1048592 | tf_op jit(solution)/shard_map/all_gather | solution.py:147
  195.2 25.1 %all_to_all.103 = bf16[4,256,128]{2,0,1:T(4,128)(2,1)S(1)} all-to-all(bf16[4,256,128]{2,0,1:T(4,128)(2,1)S(1)} %copy.163), channel_id=1, replica_groups=mesh['tm'=64,'head'=4] {'tm'}, dimensions={1} | all-to-all | bytes 524288 | tf_op jit(solution)/shard_map/all_to_all | solution.py:155
  227.3 5.7 all-to-all-start.7
  233.0 3.6 multiply_reduce_fusion
  239.6 5.5 all-to-all-done.7
  245.1 6.0 all-to-all-start.5
  255.2 7.8 all-to-all-done.5
  263.0 5.8 all-to-all-start.6
  275.0 5.6 all-to-all-done.6
  294.8 597.3 %all-reduce.7.cloned.1.call-done = (f32[512,3,128]{2,0,1:T(8,128)}, f32[128,512]{1,0:T(8,128)}) async-done(((f32[512,3,128]{2,0,1:T(8,128)}, f32[128,512]{1,0:T(8,128)}), (f32[512,3,128]{2,0,1:T(8,128)}, f32[128,512]{1,0:T(8,128)})) %all-reduce.7.cloned.1.call-update) | async-done | bytes 1048592 | tf_op jit(solution)/shard_map/psum | solution.py:221
  894.1 48.0 %all-reduce.5.cloned.1.call-done = bf16[4,256,512]{2,1,0:T(8,128)(2,1)} async-done(((bf16[4,256,512]{2,1,0:T(8,128)(2,1)}), bf16[4,256,512]{2,1,0:T(8,128)(2,1)}) %all-reduce.5.cloned.1.call-update) | async-done | bytes 1048592 | tf_op jit(solution)/shard_map/psum | solution.py:212
  947.2 160.7 %all-reduce = (f32[128]{0:T(128)S(1)}, f32[2]{0:T(128)S(1)}, f32[2,128,4]{1,2,0:T(4,128)S(1)}) all-reduce(f32[128]{0:T(128)S(1)} %get-tuple-element.19, f32[2]{0:T(128)S(1)} %copy-done.36, f32[2,128,4]{1,2,0:T(4,128)S(1)} %pad_maximum_fusion), channel_id=1, replica_groups=mesh['tm'=64,'head'=4] {'tm'}, use_global_device_ids=true, to_apply=%region_13.14 | all-reduce | flops 1154 | bytes 9232 | tf_op jit(solution)/shard_map/psum | solution.py:221
  (206 shorter events, 79.8 us)
Async XLA Ops:
  7.2 92.7 %copy-start = (bf16[128,512]{1,0:T(8,128)(2,1)S(1)}, bf16[128,512]{1,0:T(8,128)(2,1)}, u32[]{:S(2)}) copy-start(bf16[128,512]{1,0:T(8,128)(2,1)} %param.21) | copy-start | bytes 393220
  15.1 26.5 %all-to-all-start.1 = ((bf16[4,256,128]{2,0,1:T(4,128)(2,1)}), bf16[4,256,128]{2,0,1:T(4,128)(2,1)S(1)}, u32[]{:S(2)}, u32[]{:S(2)}) async-start(bf16[4,256,128]{2,0,1:T(4,128)(2,1)} %copy.150), calls=%async_computation.1 | async-start | bytes 524288 | tf_op jit(solution)/shard_map/all_to_all | solution.py:85
  41.7 17.5 %all-to-all-start = ((bf16[4,256,128]{2,0,1:T(4,128)(2,1)}), bf16[4,256,128]{2,0,1:T(4,128)(2,1)S(1)}, u32[]{:S(2)}, u32[]{:S(2)}) async-start(bf16[4,256,128]{2,0,1:T(4,128)(2,1)} %copy.147), calls=%async_computation | async-start | bytes 524288 | tf_op jit(solution)/shard_map/all_to_all | solution.py:87
  59.2 17.0 %all-to-all-start.2 = ((bf16[4,256,128]{2,0,1:T(4,128)(2,1)}), bf16[4,256,128]{2,0,1:T(4,128)(2,1)S(1)}, u32[]{:S(2)}, u32[]{:S(2)}) async-start(bf16[4,256,128]{2,0,1:T(4,128)(2,1)} %copy.153), calls=%async_computation.2 | async-start | bytes 524288 | tf_op jit(solution)/shard_map/all_to_all | solution.py:86
  64.1 71.5 %reduce-scatter.4.cloned.1.call-start = ((), (), s32[]{:S(2)}) async-start(), calls=%async_computation.11 | async-start | bytes 1310720
  104.2 89.0 %all-gather.2.cloned.1.call-start = ((), (), s32[]{:S(2)}) async-start(), calls=%async_computation.9 | async-start | bytes 1310720 | tf_op jit(solution)/shard_map/all_gather | solution.py:147
  104.3 53.8 %copy-start.37 = (f32[4,4]{1,0:T(4,128)S(1)}, f32[4,4]{1,0:T(4,128)}, u32[]{:S(2)}) copy-start(f32[4,4]{1,0:T(4,128)} %param.26) | copy-start | bytes 196
  104.3 53.8 %copy-start.41 = (f32[4]{0:T(128)S(1)}, f32[4]{0:T(128)}, u32[]{:S(2)}) copy-start(f32[4]{0:T(128)} %constant.87) | copy-start | bytes 52
  104.3 53.8 %copy-start.42 = (f32[4]{0:T(128)S(1)}, f32[4]{0:T(128)}, u32[]{:S(2)}) copy-start(f32[4]{0:T(128)} %constant.86) | copy-start | bytes 52
  104.3 53.8 %copy-start.43 = (s32[4]{0:T(128)S(1)}, s32[4]{0:T(128)}, u32[]{:S(2)}) copy-start(s32[4]{0:T(128)} %constant.84) | copy-start | bytes 52
  104.4 53.8 %copy-start.44 = (f32[4]{0:T(128)S(1)}, f32[4]{0:T(128)}, u32[]{:S(2)}) copy-start(f32[4]{0:T(128)} %constant.80) | copy-start | bytes 52
  104.4 53.8 %copy-start.45 = (f32[4]{0:T(128)S(1)}, f32[4]{0:T(128)}, u32[]{:S(2)}) copy-start(f32[4]{0:T(128)} %constant.74.clone) | copy-start | bytes 52
  104.4 53.8 %copy-start.46 = (s32[4]{0:T(128)S(1)}, s32[4]{0:T(128)}, u32[]{:S(2)}) copy-start(s32[4]{0:T(128)} %constant.72.clone) | copy-start | bytes 52
  104.4 53.8 %copy-start.47 = (f32[4]{0:T(128)S(1)}, f32[4]{0:T(128)}, u32[]{:S(2)}) copy-start(f32[4]{0:T(128)} %constant.69.clone) | copy-start | bytes 52
  104.4 53.8 %copy-start.48 = (f32[4]{0:T(128)S(1)}, f32[4]{0:T(128)}, u32[]{:S(2)}) copy-start(f32[4]{0:T(128)} %constant.68.clone) | copy-start | bytes 52
  104.4 67.8 %copy-start.12 = (bf16[4,256,128]{2,1,0:T(8,128)(2,1)S(1)}, bf16[4,256,128]{2,1,0:T(8,128)(2,1)}, u32[]{:S(2)}) copy-start(bf16[4,256,128]{2,1,0:T(8,128)(2,1)} %param.25) | copy-start | bytes 786436
  138.8 12.0 %collective-permute-start = (f32[4,128]{1,0:T(4,128)S(1)}, f32[4,128]{1,0:T(4,128)S(1)}, u32[]{:S(2)}, u32[]{:S(2)}) collective-permute-start(f32[4,128]{1,0:T(4,128)S(1)} %broadcast_multiply_fusion.8), channel_id=1, source_target_pairs={{16,0},{20,4},{24,8},{28,12},{32,16},{36,20},{40,24},{44,28},{48,3... | collective-permute-start | bytes 6152 | tf_op jit(solution)/shard_map/ppermute | solution.py:21
  159.1 61.2 %copy-start.26 = (f32[4,4]{1,0:T(4,128)}, f32[4,4]{1,0:T(4,128)S(1)}, u32[]{:S(2)}) copy-start(f32[4,4]{1,0:T(4,128)S(1)} %get-tuple-element.25) | copy-start | bytes 196
  159.2 12.9 %collective-permute-start.1 = (f32[4,128]{1,0:T(4,128)S(1)}, f32[4,128]{1,0:T(4,128)S(1)}, u32[]{:S(2)}, u32[]{:S(2)}) collective-permute-start(f32[4,128]{1,0:T(4,128)S(1)} %fusion.25), channel_id=1, source_target_pairs={{0,16},{4,20},{8,24},{12,28},{16,32},{20,36},{24,40},{28,44},{32,4... | collective-permute-start | bytes 6152 | tf_op jit(solution)/shard_map/ppermute | solution.py:21
  227.3 17.8 %all-to-all-start.7 = ((bf16[256,4,128]{2,1,0:T(4,128)(2,1)}), bf16[256,4,128]{2,1,0:T(4,128)(2,1)}, u32[]{:S(2)}, u32[]{:S(2)}) async-start(bf16[256,4,128]{2,1,0:T(4,128)(2,1)} %copy.184), calls=%async_computation.7 | async-start | bytes 524288 | tf_op jit(solution)/shard_map/all_to_all | solution.py:190
  245.1 17.8 %all-to-all-start.5 = ((bf16[256,4,128]{2,1,0:T(4,128)(2,1)}), bf16[256,4,128]{2,1,0:T(4,128)(2,1)}, u32[]{:S(2)}, u32[]{:S(2)}) async-start(bf16[256,4,128]{2,1,0:T(4,128)(2,1)} %copy.171), calls=%async_computation.5 | async-start | bytes 524288 | tf_op jit(solution)/shard_map/all_to_all | solution.py:184
  263.0 17.6 %all-to-all-start.6 = ((bf16[256,4,128]{2,1,0:T(4,128)(2,1)}), bf16[256,4,128]{2,1,0:T(4,128)(2,1)}, u32[]{:S(2)}, u32[]{:S(2)}) async-start(bf16[256,4,128]{2,1,0:T(4,128)(2,1)} %copy.178), calls=%async_computation.6 | async-start | bytes 524288 | tf_op jit(solution)/shard_map/all_to_all | solution.py:187
  268.8 623.3 %all-reduce.7.cloned.1.call-start = ((), (), s32[]{:S(2)}) async-start(), calls=%async_computation.12 | async-start | bytes 2097152 | tf_op jit(solution)/shard_map/psum | solution.py:221
  292.4 649.6 %all-reduce.5.cloned.1.call-start = ((), (), s32[]{:S(2)}) async-start(), calls=%async_computation.10 | async-start | bytes 2097152 | tf_op jit(solution)/shard_map/psum | solution.py:212
  (37 other events, 370.1 us)
Sparse Core Ops, SparseCore 0:
  104.4 31.1 reduce-scatter.3
  173.2 20.0 all-gather.1
  292.6 599.4 all-reduce.6
  894.5 47.4 all-reduce.4
where the time goes:
time: 1120 us
  waiting for transfers between devices  752 us (67%)
  blocking collectives  210 us (19%)
  starting transfers between devices  57.5 us (5%)
  local copies, waits for them, and re-layouts  34.8 us (3%)
  other arithmetic  28 us (2%)
  matrix products  19.1 us (2%)
  between operations  14.8 us (1%)
    psum x1, waiting for transfers between devices, local(): lax.psum((grad_qkv_part, grad_weights, grad_act_part, gain_part, scale_pa...  597 us
    psum x1, blocking collectives, local(): lax.psum((grad_qkv_part, grad_weights, grad_act_part, gain_part, scale_pa...  161 us
    psum x1, waiting for transfers between devices, local(): lax.psum(grad_normed_part.astype(jnp.bfloat16), 'head').astype(jnp.float32)  48 us
    unnamed x5, waiting for transfers between devices  29.5 us
    all_to_all x1, blocking collectives, local(): lax.all_to_all(grad_attended, 'tm', split_axis=1, concat_axis=0, tiled=True)  25.1 us
  transfers between devices with their start and end apart: 12, of which 12 were waited for; matrix products, arithmetic and copies ran while one was open for 3% of the time, Pallas kernels for 0%

commit v1 on v0

v1 whole, which is shorter than its diff:
```python
import math

import jax
import jax.numpy as jnp
import numpy as np
from jax import lax
from jax.sharding import Mesh
from jax.sharding import PartitionSpec as P

LAG = 16
EPS = 1e-06
HIGHEST = lax.Precision.HIGHEST
TM = ("xl", "y", "z")
YZ = ("y", "z")
bf16 = jnp.bfloat16
f32 = jnp.float32


def swap(value, axis):
    return lax.ppermute(value, axis, [(0, 1), (1, 0)])


def ordered(own, other, index, axis):
    first = jnp.where(index == 0, own, other)
    second = jnp.where(index == 0, other, own)
    return jnp.stack([first, second], axis=axis)


def pick(value, index, axis):
    return lax.dynamic_index_in_dim(value, index, axis, keepdims=False)


def after(value, *earlier):
    return lax.optimization_barrier((value, *earlier))[0]


def level_tables():
    sizes_list = [8.0, 5.0, 5.0, 5.0]
    half_list = [(count - 1.0) * (1.0 - 0.001) / 2.0 for count in sizes_list]
    offset_list = [0.5 if int(count) % 2 == 0 else 0.0 for count in sizes_list]
    shift_list = [
        0.5 * math.log((half_list[i] + offset_list[i]) / (half_list[i] - offset_list[i]))
        for i in range(4)
    ]
    width_list = [float(int(count) // 2) for count in sizes_list]
    return tuple(
        np.array(v, np.float32)[:, None] for v in (half_list, offset_list, shift_list, width_list)
    )


def rms_scale(values):
    return lax.rsqrt(jnp.mean(values * values, axis=-1, keepdims=True) + EPS)


def dot(a, b, ca, cb, **kw):
    return lax.dot_general(a, b, (((ca,), (cb,)), ((), ())), preferred_element_type=f32, **kw)


def local(
    frames_in,
    norm_gain,
    w_qkv,
    qk_scale,
    w_out,
    w_act,
    action_codes,
    episode_ids,
    cotangent,
    action_cotangent,
):
    fl, patches, width = frames_in.shape
    share = cotangent.shape[2]
    n_tm = lax.axis_size("xl") * lax.axis_size("y") * lax.axis_size("z")
    n_yz = lax.axis_size("y") * lax.axis_size("z")
    frames = fl * n_tm
    group = patches // 4
    tokens = frames * patches
    hd = 64
    xl, xh, core = lax.axis_index("xl"), lax.axis_index("xh"), lax.axis_index("core")
    block = xh * 2 + core
    tm = lax.axis_index(TM)

    sent = lax.dynamic_slice_in_dim(frames_in, block * group, group, 1).transpose(1, 0, 2)
    x_own = lax.all_to_all(sent, TM, 0, 0, tiled=True)
    x_own = x_own.reshape(frames, width)
    x_other = swap(x_own, "core")

    w_both = ordered(w_qkv, swap(w_qkv, "xh"), xh, 2).reshape(width, 3 * 2 * share)
    wo_both = ordered(w_out, swap(w_out, "xh"), xh, 0).reshape(2 * share, width)
    scale_both = ordered(qk_scale, swap(qk_scale, "xh"), xh, 0).reshape(4)
    act = w_act.transpose(0, 2, 1).reshape(8, share)
    act = ordered(act, swap(act, "core"), core, 0)
    act = ordered(act, swap(act, "xh"), xh, 0).reshape(4, 8, share)
    act = act.transpose(1, 0, 2).reshape(8, width)
    ac_t = action_cotangent.T
    ac_t = ordered(ac_t, swap(ac_t, "xl"), xl, 0)

    cot = cotangent.reshape(fl, 2, 2, group, share)
    got = swap(pick(cot, 1 - core, 2), "core")
    cot = ordered(pick(cot, core, 2), got, core, 3)
    got = swap(pick(cot, 1 - xh, 1), "xh")
    cot = ordered(pick(cot, xh, 1), got, xh, 2).reshape(fl, group, width)
    cot = after(cot.transpose(1, 0, 2), x_own)
    cot_own = lax.all_to_all(cot, TM, 0, 0, tiled=True).reshape(frames, width)
    cot_other = swap(cot_own, "core")

    x_two = jnp.stack([x_own, x_other])
    floats = x_two.astype(f32)
    inverse = rms_scale(floats)
    normed = (floats * inverse * norm_gain).astype(bf16)
    normed_flat = normed.reshape(2 * frames, width)
    projected = jnp.dot(normed_flat, w_both, preferred_element_type=f32)
    projected = projected.reshape(2, frames, 3, 4, hd)
    query_raw, keys_raw = projected[:, :, 0], projected[:, :, 1]
    query_inv, keys_inv = rms_scale(query_raw), rms_scale(keys_raw)
    query = (query_raw * query_inv).astype(bf16)
    keys = (keys_raw * keys_inv).astype(bf16)
    values = projected[:, :, 2].astype(bf16)
    order = jnp.arange(frames, dtype=jnp.int32)
    visible = jnp.logical_and(
        episode_ids[:, None] == episode_ids[None, :], order[None, :] <= order[:, None]
    )
    factor = scale_both * (1.0 / math.sqrt(hd))
    dots = jnp.einsum("pthd,puhd->phtu", query, keys, preferred_element_type=f32)
    scores = dots * factor[None, :, None, None]
    weights = jnp.where(visible[None, None], jnp.exp(scores), 0.0)
    probs = weights / jnp.sum(weights, axis=-1, keepdims=True)
    rounded = probs.astype(bf16)
    attended = jnp.einsum("phtu,puhd->pthd", rounded, values, preferred_element_type=f32)
    attended = attended.astype(bf16).reshape(2, frames, 2 * share)

    act_out = dot(act, wo_both.astype(f32), 1, 1, precision=HIGHEST)
    pooled_att = attended[0].astype(f32) + attended[1].astype(f32)
    terms = dot(act_out, pooled_att, 1, 1, precision=HIGHEST)
    terms = terms + dot(act, floats[0], 1, 1, precision=HIGHEST)
    terms = terms * (1.0 / patches)
    part = terms[:4] + jnp.pad(terms[4:, LAG:], ((0, 0), (0, LAG)))
    for axis in ("core", "xh", "xl"):
        part = part + swap(part, axis)
    part = part.reshape(4, 2, frames // 2)
    packed = jnp.concatenate(
        [part.reshape(8, frames // 2), jnp.pad(ac_t.reshape(8, fl), ((0, 0), (0, frames // 2 - fl)))]
    )
    packed = after(packed, cot_own)
    packed = jnp.broadcast_to(packed[None], (n_yz, 16, frames // 2))
    packed = lax.all_to_all(packed, YZ, 0, 0, tiled=True)
    latent = jnp.sum(packed[:, :8], axis=0).reshape(4, frames)
    ac_all = packed[:, 8:, :fl].reshape(n_yz, 2, 4, fl).transpose(2, 1, 0, 3).reshape(4, frames)

    half_level, offsets, shifts, widths = level_tables()
    curve = jnp.tanh(latent + shifts)
    bounded = (curve * half_level - offsets) / widths
    bases = jnp.array([1, 8, 40, 200], dtype=jnp.int32)[:, None]
    radices = jnp.array([8, 5, 5, 5], dtype=jnp.int32)[:, None]
    digits = action_codes[None, :] // bases % radices
    bounded_own = lax.dynamic_slice_in_dim(bounded, tm * fl, fl, 1)
    quant_gap = ((digits.astype(f32) - widths) / widths - bounded_own).T
    grad_latent = ac_all * (half_level / widths) * (1.0 - curve * curve)
    moved = jnp.pad(grad_latent[:, : frames - LAG], ((0, 0), (LAG, 0)))
    grad_eight = jnp.concatenate([grad_latent, moved])
    grad_pooled = dot(grad_eight, act, 0, 0, precision=HIGHEST) * (1.0 / patches)

    branch = jnp.dot(
        attended.reshape(2 * frames, 2 * share), wo_both, preferred_element_type=f32
    ).reshape(2, frames, width)
    got = swap(branch[1].astype(bf16), "core").astype(f32)
    encoded_own = (floats[0] + (branch[0] + got)).astype(bf16)

    def home(value, *earlier):
        value = after(value.reshape(n_tm, fl, width), *earlier)
        value = lax.all_to_all(value, TM, 0, 0, tiled=True)
        value = value.reshape(group, fl, 2, 2, share)
        got = swap(pick(value, 1 - xh, 2), "xh")
        value = ordered(pick(value, xh, 2), got, xh, 0)
        got = swap(pick(value, 1 - core, 3), "core")
        value = ordered(pick(value, core, 3), got, core, 1)
        return value.transpose(3, 0, 1, 2, 4).reshape(fl, patches, share)

    encoded = home(encoded_own, latent)

    upstream = (
        jnp.stack([cot_own, cot_other]).astype(f32) + grad_pooled[None]
    ).astype(bf16)
    upstream_flat = upstream.reshape(2 * frames, width)
    attended_flat = attended.reshape(2 * frames, 2 * share)
    grad_out_part = dot(attended_flat, upstream_flat, 0, 0)
    grad_att = dot(upstream_flat, wo_both, 1, 1).astype(bf16).reshape(2, frames, 4, hd)
    grad_probs = jnp.einsum("pthd,puhd->phtu", grad_att, values, preferred_element_type=f32)
    grad_values = jnp.einsum("phtu,pthd->puhd", rounded, grad_att, preferred_element_type=f32)
    grad_scores = probs * (grad_probs - jnp.sum(grad_probs * probs, axis=-1, keepdims=True))
    grad_rounded = grad_scores.astype(bf16)
    grad_query = jnp.einsum("phtu,puhd->pthd", grad_rounded, keys, preferred_element_type=f32)
    grad_keys = jnp.einsum("phtu,pthd->puhd", grad_rounded, query, preferred_element_type=f32)
    query_mean = jnp.mean(grad_query * query, axis=-1, keepdims=True)
    keys_mean = jnp.mean(grad_keys * keys, axis=-1, keepdims=True)
    scale_part = jnp.sum(query_mean, axis=(0, 1, 3)) * hd
    head_factor = factor[None, None, :, None]
    grad_query = head_factor * query_inv * (grad_query - query * query_mean)
    grad_keys = head_factor * keys_inv * (grad_keys - keys * keys_mean)
    grad_projected = jnp.stack(
        [grad_query.astype(bf16), grad_keys.astype(bf16), grad_values.astype(bf16)], axis=2
    ).reshape(2 * frames, 6 * share)
    grad_qkv_part = dot(normed_flat, grad_projected, 0, 0)
    grad_normed = dot(grad_projected, w_both, 1, 1).reshape(2, frames, width)
    got = swap(grad_normed[1].astype(bf16), "core").astype(f32)
    grad_normed = grad_normed[0] + got
    inv_own = inverse[0]
    scaled = norm_gain * grad_normed
    row_dot = jnp.mean(scaled * floats[0], axis=-1, keepdims=True)
    grad_floats = inv_own * scaled - floats[0] * (inv_own * inv_own * inv_own * row_dot)
    gain_part = jnp.sum(grad_normed * floats[0] * inv_own, axis=0)
    frames_own = (upstream[0].astype(f32) + grad_floats).astype(bf16)
    grad_frames = home(frames_own, encoded)

    qkv_blocks = grad_qkv_part.astype(bf16).reshape(2, n_yz, width // 2 // n_yz, 3, 2, share)
    out_blocks = grad_out_part.astype(bf16).reshape(2, 2, n_yz, share // 2 // n_yz, 4, share)
    act_part = dot(grad_eight, encoded_own.astype(f32), 1, 0, precision=HIGHEST)
    small = jnp.concatenate([act_part, gain_part[None]]).reshape(9, 2, 2, share)
    small = pick(small, core, 2) + swap(pick(small, 1 - core, 2), "core")
    scale_row = jnp.pad(scale_part.reshape(1, 2, 2), ((0, 0), (0, 0), (0, share - 2)))
    small = jnp.concatenate([small, scale_row])
    small_mine = pick(small, xh, 1) + swap(pick(small, 1 - xh, 1), "xh")
    small_mine = small_mine + swap(small_mine, "xl")
    qkv_mine = pick(qkv_blocks, xh, 4).astype(f32) + swap(pick(qkv_blocks, 1 - xh, 4), "xh").astype(f32)
    out_mine = pick(out_blocks, xh, 0).astype(f32) + swap(pick(out_blocks, 1 - xh, 0), "xh").astype(f32)
    rows = width // 2 // n_yz * 3
    rows_out = share // 2 // n_yz * 4
    grads = jnp.concatenate(
        [qkv_mine.reshape(2, n_yz, rows, share), out_mine.reshape(2, n_yz, rows_out, share)], axis=2
    ).astype(bf16)
    grads = pick(grads, xl, 0).astype(f32) + swap(pick(grads, 1 - xl, 0), "xl").astype(f32)

    def high_low(value):
        high = value.astype(bf16)
        return high, (value - high.astype(f32)).astype(bf16)

    high, low = high_low(small_mine)
    small_rows = jnp.pad(jnp.concatenate([high, low]), ((0, n_yz - 20), (0, 0)))
    small_rows = jnp.pad(small_rows.reshape(n_yz, 1, share), ((0, 0), (0, 7), (0, 0)))
    grads = jnp.concatenate([grads.astype(bf16), small_rows], axis=1)
    grads = after(grads, grad_frames)
    grads = lax.all_to_all(grads, YZ, 0, 0, tiled=True)
    summed = jnp.sum(grads.astype(f32), axis=0)
    high, low = high_low(summed[-8:])
    summed = jnp.concatenate([summed[:-8].astype(bf16), high[:4], low[:4]])
    summed = jnp.broadcast_to(summed[None], (n_yz, *summed.shape))
    summed = lax.all_to_all(summed, YZ, 0, 0, tiled=True)
    both = ordered(summed, swap(summed, "xl"), xl, 0).astype(f32)
    norm_factor = 1.0 / math.sqrt(tokens)
    grad_qkv = both[:, :, :rows].reshape(width, 3, share) * norm_factor
    grad_out = both[:, :, rows : rows + rows_out].reshape(share, width) * norm_factor
    last = rows + rows_out
    small_all = summed[:, last].astype(f32) + summed[:, last + 4].astype(f32)
    small_all = small_all[:10] + small_all[10:20]
    grad_act = small_all[:8].reshape(2, 4, share).transpose(0, 2, 1) * (
        1.0 / math.sqrt(frames) / patches
    )
    grad_gain = small_all[8] * norm_factor
    grad_qk_scale = small_all[9, :2] * (norm_factor / math.sqrt(hd))
    return (encoded, quant_gap, grad_frames, grad_gain, grad_qkv, grad_qk_scale, grad_out, grad_act)


def solution(mesh):
    fine = Mesh(mesh.devices.reshape(2, 4, 8, 2, 2), ("xl", "y", "z", "xh", "core"))
    head = ("xh", "core")
    in_specs = (
        P(TM, None, None),
        P(),
        P(None, None, head),
        P(head),
        P(head, None),
        P(None, head, None),
        P(TM),
        P(),
        P(TM, None, head),
        P(TM, None),
    )
    out_specs = (
        P(TM, None, head),
        P(TM, None),
        P(TM, None, head),
        P(head),
        P(None, None, head),
        P(head),
        P(head, None),
        P(None, head, None),
    )
    return jax.shard_map(local, mesh=fine, in_specs=in_specs, out_specs=out_specs, check_vma=False)
```

time: 1120 us -> 239 us (0.21)
  waiting for transfers between devices: 752 us -> 77.2 us
  blocking collectives: 210 us -> 16.6 us
  starting transfers between devices: 57.5 us -> 79 us
  other arithmetic: 28 us -> 14.1 us
  between operations: 14.8 us -> 1.95 us
    psum x2 -> x0, waiting for transfers between devices: 645 us -> none  [the longest x1 597 us: local(): lax.psum((grad_qkv_part, grad_weights, grad_act_part, gain_part, scale_pa...]
    psum x2 -> x0, blocking collectives: 168 us -> none  [the longest x1 161 us: local(): lax.psum((grad_qkv_part, grad_weights, grad_act_part, gain_part, scale_pa...]
    unnamed x5 -> x0, waiting for transfers between devices: 29.5 us -> none
    ppermute x2 -> x26, waiting for transfers between devices: 7.99 us -> 36.7 us  [swap(): return lax.ppermute(value, axis, [(0, 1), (1, 0)])]
    all_to_all x2 -> x1, blocking collectives: 41.5 us -> 16.6 us  [local(): grads = lax.all_to_all(grads, YZ, 0, 0, tiled=True)]
    all_gather x1 -> x0, waiting for transfers between devices: 20.2 us -> none  [local(): piece = lax.all_gather(upstream_flat, 'head', axis=1, tiled=True)]
    all_to_all x6, starting transfers between devices: 40.4 us -> 51.9 us  [the longest x2 13.3 us: home(): value = lax.all_to_all(value, TM, 0, 0, tiled=True)]
    ppermute x2 -> x26, starting transfers between devices: 16.7 us -> 27.1 us  [swap(): return lax.ppermute(value, axis, [(0, 1), (1, 0)])]
  transfers between devices with their start and end apart: 12 -> 32, of which waited for: 12 -> 16; matrix products, arithmetic and copies ran while one was open for 3% -> 21% of each run, Pallas kernels for 0% -> 0%
where the time goes in v1:
time: 239 us; the launch traced here: 238 us
  starting transfers between devices  79 us (33%)
  waiting for transfers between devices  77.2 us (32%)
  local copies, waits for them, and re-layouts  34.3 us (14%)
  blocking collectives  16.6 us (7%)
  matrix products  14.3 us (6%)
  other arithmetic  14.1 us (6%)
    ppermute x26, waiting for transfers between devices, swap(): return lax.ppermute(value, axis, [(0, 1), (1, 0)])  36.7 us
    ppermute x26, starting transfers between devices, swap(): return lax.ppermute(value, axis, [(0, 1), (1, 0)])  27.1 us
    all_to_all x2, waiting for transfers between devices, home(): value = lax.all_to_all(value, TM, 0, 0, tiled=True)  25.4 us
    all_to_all x1, blocking collectives, local(): grads = lax.all_to_all(grads, YZ, 0, 0, tiled=True)  16.6 us
    all_to_all x2, starting transfers between devices, home(): value = lax.all_to_all(value, TM, 0, 0, tiled=True)  13.3 us
    all_to_all x1, starting transfers between devices, local(): x_own = lax.all_to_all(sent, TM, 0, 0, tiled=True)  13.2 us
    all_to_all x1, waiting for transfers between devices, local(): summed = lax.all_to_all(summed, YZ, 0, 0, tiled=True)  11.5 us
    all_to_all x1, starting transfers between devices, local(): cot_own = lax.all_to_all(cot, TM, 0, 0, tiled=True).reshape(frames, width)  10.8 us
  transfers between devices with their start and end apart: 32, of which 16 were waited for; matrix products, arithmetic and copies ran while one was open for 21% of the time, Pallas kernels for 0%

profile of v1, /device:TPU:2, one launch (start us, length us, event | category | flops | bytes accessed | tf_op | source)
XLA Modules:
  0.0 237.5 jit_solution(6029905269606958421)
XLA Ops:
  2.8 13.2 %all-to-all-start = ((bf16[64,4,512]{2,1,0:T(4,128)(2,1)}), bf16[64,4,512]{2,1,0:T(4,128)(2,1)S(1)}, u32[]{:S(2)}, u32[]{:S(2)}) async-start(bf16[64,4,512]{2,1,0:T(4,128)(2,1)} %bitcast.289), calls=%async_computation | async-start | bytes 524288 | tf_op jit(solution)/shard_map/all_to_all | solution.py:84
  17.2 2.2 collective-permute-start.1
  20.8 2.2 collective-permute-start.3
  23.4 8.9 %collective-permute-done.2 = f32[2]{0:T(128)S(1)} collective-permute-done((f32[2]{0:T(128)S(1)}, f32[2]{0:T(128)S(1)}, u32[]{:S(2)}, u32[]{:S(2)}) %collective-permute-start.2) | collective-permute-done | bytes 40 | tf_op jit(solution)/shard_map/ppermute | solution.py:20
  34.3 3.3 %collective-permute-done.6 = f32[2,8,128]{2,1,0:T(8,128)S(1)} collective-permute-done((f32[2,8,128]{2,1,0:T(8,128)S(1)}, f32[2,8,128]{2,1,0:T(8,128)S(1)}, u32[]{:S(2)}, u32[]{:S(2)}) %collective-permute-start.6) | collective-permute-done | bytes 8224 | tf_op jit(solution)/shard_map/ppermute | solution.py:20
  40.8 3.6 %collective-permute-done.12 = bf16[4,64,2,128]{3,2,0,1:T(2,128)(2,1)S(1)} collective-permute-done((bf16[4,64,2,128]{3,2,0,1:T(2,128)(2,1)S(1)}, bf16[4,64,2,128]{3,2,0,1:T(2,128)(2,1)S(1)}, u32[]{:S(2)}, u32[]{:S(2)}) %collective-permute-start.12) | collective-permute-done | bytes 131104 | tf_op jit(solution)/shard_map/ppermute | solution.py:20
  46.2 10.8 %all-to-all-start.1 = ((bf16[64,4,512]{2,1,0:T(4,128)(2,1)}), bf16[64,4,512]{2,1,0:T(4,128)(2,1)}, u32[]{:S(2)}, u32[]{:S(2)}) async-start(bf16[64,4,512]{2,1,0:T(4,128)(2,1)} %bitcast.48), calls=%async_computation.1 | async-start | bytes 524288 | tf_op jit(solution)/shard_map/all_to_all | solution.py:104
  67.6 2.2 collective-permute-done.8
  71.0 2.4 %collective-permute-done.9 = f32[4,256]{1,0:T(4,128)S(1)} collective-permute-done((f32[4,256]{1,0:T(4,128)S(1)}, f32[4,256]{1,0:T(4,128)S(1)}, u32[]{:S(2)}, u32[]{:S(2)}) %collective-permute-start.9) | collective-permute-done | bytes 4128 | tf_op jit(solution)/shard_map/ppermute | solution.py:20
  75.9 9.7 %all-to-all-start.2 = ((f32[32,16,128]{2,1,0:T(8,128)}), f32[32,16,128]{2,1,0:T(8,128)}, u32[]{:S(2)}, u32[]{:S(2)}) async-start(f32[32,16,128]{2,1,0:T(8,128)} %broadcast_in_dim.18), calls=%async_computation.2 | async-start | bytes 524288 | tf_op jit(solution)/shard_map/all_to_all | solution.py:146
  93.0 3.6 %all-to-all-done.2 = f32[32,16,128]{2,1,0:T(8,128)} async-done(((f32[32,16,128]{2,1,0:T(8,128)}), f32[32,16,128]{2,1,0:T(8,128)}, u32[]{:S(2)}, u32[]{:S(2)}) %all-to-all-start.2) | async-done | bytes 262176 | tf_op jit(solution)/shard_map/all_to_all | solution.py:146
  106.2 2.0 reshape.452
  110.2 2.7 %multiply_reduce_fusion = (f32[2,4,256]{2,1,0:T(4,128)S(1)}, f32[2,4,256,256]{2,3,1,0:T(8,128)S(1)}) fusion(f32[2,4,256]{2,1,0:T(4,128)S(1)} %copy-done.43, f32[2,4,256,256]{2,3,1,0:T(8,128)} %copy-done.18, f32[4]{0:T(128)S(1)} %copy-done.47, pred[256,256]{0,1:T(8,128)(4,1)S(1)} %copy-done.27, bf16[2,256,4,64]{1,3,2,0:T(8,128)(2,1)} %copy.185, ...), kind=kOutput, calls=%fused_computation.1 | convolution fusion | flops 69728256 | bytes 4801024 | tf_op jit(solution)/shard_map/pthd,puhd->phtu/dot_general | solution.py:188
  127.4 2.2 collective-permute-start.19
  131.9 7.8 %all-to-all-start.3 = ((bf16[64,4,512]{2,1,0:T(4,128)(2,1)}), bf16[64,4,512]{2,1,0:T(4,128)(2,1)S(1)}, u32[]{:S(2)}, u32[]{:S(2)}) async-start(bf16[64,4,512]{2,1,0:T(4,128)(2,1)} %reshape.421), calls=%async_computation.3 | async-start | bytes 524288 | tf_op jit(solution)/shard_map/all_to_all | solution.py:171
  140.9 12.3 %all-to-all-done.3 = bf16[64,4,512]{2,1,0:T(4,128)(2,1)S(1)} async-done(((bf16[64,4,512]{2,1,0:T(4,128)(2,1)}), bf16[64,4,512]{2,1,0:T(4,128)(2,1)S(1)}, u32[]{:S(2)}, u32[]{:S(2)}) %all-to-all-start.3) | async-done | bytes 262176 | tf_op jit(solution)/shard_map/all_to_all | solution.py:171
  157.3 2.8 %collective-permute-done.13 = bf16[64,4,2,128]{3,0,2,1:T(8,128)(2,1)S(1)} collective-permute-done((bf16[64,4,2,128]{3,0,2,1:T(8,128)(2,1)S(1)}, bf16[64,4,2,128]{3,0,2,1:T(8,128)(2,1)S(1)}, u32[]{:S(2)}, u32[]{:S(2)}) %collective-permute-start.13) | collective-permute-done | bytes 131104 | tf_op jit(solution)/shard_map/ppermute | solution.py:20
  162.7 5.5 %all-to-all-start.4 = ((bf16[64,4,512]{2,1,0:T(4,128)(2,1)}), bf16[64,4,512]{2,1,0:T(4,128)(2,1)S(1)}, u32[]{:S(2)}, u32[]{:S(2)}) async-start(bf16[64,4,512]{2,1,0:T(4,128)(2,1)} %reshape.436), calls=%async_computation.4 | async-start | bytes 524288 | tf_op jit(solution)/shard_map/all_to_all | solution.py:171
  168.4 13.1 %all-to-all-done.4 = bf16[64,4,512]{2,1,0:T(4,128)(2,1)S(1)} async-done(((bf16[64,4,512]{2,1,0:T(4,128)(2,1)}), bf16[64,4,512]{2,1,0:T(4,128)(2,1)S(1)}, u32[]{:S(2)}, u32[]{:S(2)}) %all-to-all-start.4) | async-done | bytes 262176 | tf_op jit(solution)/shard_map/all_to_all | solution.py:171
  185.0 4.6 %collective-permute-done.17 = bf16[64,4,2,128]{3,0,2,1:T(8,128)(2,1)S(1)} collective-permute-done((bf16[64,4,2,128]{3,0,2,1:T(8,128)(2,1)S(1)}, bf16[64,4,2,128]{3,0,2,1:T(8,128)(2,1)S(1)}, u32[]{:S(2)}, u32[]{:S(2)}) %collective-permute-start.17) | collective-permute-done | bytes 131104 | tf_op jit(solution)/shard_map/ppermute | solution.py:20
  192.7 16.6 %all_to_all.35 = bf16[32,40,128]{2,1,0:T(8,128)(2,1)S(1)} all-to-all(bf16[32,40,128]{2,1,0:T(8,128)(2,1)S(1)} %copy.199), channel_id=1, replica_groups=mesh['xl'=2,'y'=4,'z'=8,'xh'=2,'core'=2] {'y','z'}, dimensions={0} | all-to-all | bytes 655360 | tf_op jit(solution)/shard_map/all_to_all | solution.py:242
  210.2 4.9 %all-to-all-start.6 = ((bf16[32,40,128]{2,1,0:T(8,128)(2,1)}), bf16[32,40,128]{2,1,0:T(8,128)(2,1)S(1)}, u32[]{:S(2)}, u32[]{:S(2)}) async-start(bf16[32,40,128]{2,1,0:T(8,128)(2,1)} %broadcast_in_dim.19), calls=%async_computation.6 | async-start | bytes 655360 | tf_op jit(solution)/shard_map/all_to_all | solution.py:247
  216.2 11.5 %all-to-all-done.6 = bf16[32,40,128]{2,1,0:T(8,128)(2,1)S(1)} async-done(((bf16[32,40,128]{2,1,0:T(8,128)(2,1)}), bf16[32,40,128]{2,1,0:T(8,128)(2,1)S(1)}, u32[]{:S(2)}, u32[]{:S(2)}) %all-to-all-start.6) | async-done | bytes 327712 | tf_op jit(solution)/shard_map/all_to_all | solution.py:247
  230.1 5.2 %collective-permute-done.25 = bf16[32,40,128]{2,1,0:T(8,128)(2,1)S(1)} collective-permute-done((bf16[32,40,128]{2,1,0:T(8,128)(2,1)S(1)}, bf16[32,40,128]{2,1,0:T(8,128)(2,1)S(1)}, u32[]{:S(2)}, u32[]{:S(2)}) %collective-permute-start.25) | collective-permute-done | bytes 327712 | tf_op jit(solution)/shard_map/ppermute | solution.py:20
  (306 shorter events, 82.1 us)
Async XLA Ops:
  2.8 43.0 %all-to-all-start = ((bf16[64,4,512]{2,1,0:T(4,128)(2,1)}), bf16[64,4,512]{2,1,0:T(4,128)(2,1)S(1)}, u32[]{:S(2)}, u32[]{:S(2)}) async-start(bf16[64,4,512]{2,1,0:T(4,128)(2,1)} %bitcast.289), calls=%async_computation | async-start | bytes 524288 | tf_op jit(solution)/shard_map/all_to_all | solution.py:84
  17.2 28.9 %collective-permute-start.1 = (bf16[512,3,128]{0,2,1:T(8,128)(2,1)S(1)}, bf16[512,3,128]{0,2,1:T(8,128)(2,1)S(1)}, u32[]{:S(2)}, u32[]{:S(2)}) collective-permute-start(bf16[512,3,128]{0,2,1:T(8,128)(2,1)S(1)} %copy.163), channel_id=1, source_target_pairs={{0,2},{2,0},{1,3},{3,1},{4,6},{6,4},{5,7},{7,5},{8,10},{10,8},{9,1... | collective-permute-start | bytes 1179656 | tf_op jit(solution)/shard_map/ppermute | solution.py:20
  19.4 12.9 %collective-permute-start.2 = (f32[2]{0:T(128)S(1)}, f32[2]{0:T(128)S(1)}, u32[]{:S(2)}, u32[]{:S(2)}) collective-permute-start(f32[2]{0:T(128)S(1)} %copy-done.49), channel_id=1, source_target_pairs={{0,2},{2,0},{1,3},{3,1},{4,6},{6,4},{5,7},{7,5},{8,10},{10,8},{9,1... | collective-permute-start | bytes 32 | tf_op jit(solution)/shard_map/ppermute | solution.py:20
  20.8 11.5 %collective-permute-start.5 = (f32[8,128]{1,0:T(8,128)S(1)}, f32[8,128]{1,0:T(8,128)S(1)}, u32[]{:S(2)}, u32[]{:S(2)}) collective-permute-start(f32[8,128]{1,0:T(8,128)S(1)} %bitcast.346), channel_id=1, source_target_pairs={{0,1},{1,0},{2,3},{3,2},{4,5},{5,4},{6,7},{7,6},{8,9},{9,8},{10,11... | collective-permute-start | bytes 12296 | tf_op jit(solution)/shard_map/ppermute | solution.py:20
  20.8 18.9 %collective-permute-start.3 = (bf16[128,512]{1,0:T(8,128)(2,1)S(1)}, bf16[128,512]{1,0:T(8,128)(2,1)S(1)}, u32[]{:S(2)}, u32[]{:S(2)}) collective-permute-start(bf16[128,512]{1,0:T(8,128)(2,1)S(1)} %copy-done.31), channel_id=1, source_target_pairs={{0,2},{2,0},{1,3},{3,1},{4,6},{6,4},{5,7},{7,5},{8,10},{10,8},{9,1... | collective-permute-start | bytes 393224 | tf_op jit(solution)/shard_map/ppermute | solution.py:20
  23.0 14.6 %collective-permute-start.11 = (bf16[4,2,64,128]{3,2,1,0:T(8,128)(2,1)S(1)}, bf16[4,2,64,128]{3,2,1,0:T(8,128)(2,1)S(1)}, u32[]{:S(2)}, u32[]{:S(2)}) collective-permute-start(bf16[4,2,64,128]{3,2,1,0:T(8,128)(2,1)S(1)} %dynamic-slice_bitcast_fusion.1), channel_id=1, source_target_pairs={{0,1},{1,0},{2,3},{3,2},{4,5},{5,4},{6,7},{7,6},{8,9},{9,8},{10,11... | collective-permute-start | bytes 393224 | tf_op jit(solution)/shard_map/ppermute | solution.py:20
  37.8 6.6 %collective-permute-start.12 = (bf16[4,64,2,128]{3,2,0,1:T(2,128)(2,1)S(1)}, bf16[4,64,2,128]{3,2,0,1:T(2,128)(2,1)S(1)}, u32[]{:S(2)}, u32[]{:S(2)}) collective-permute-start(bf16[4,64,2,128]{3,2,0,1:T(2,128)(2,1)S(1)} %bitcast.330), channel_id=1, source_target_pairs={{0,2},{2,0},{1,3},{3,1},{4,6},{6,4},{5,7},{7,5},{8,10},{10,8},{9,1... | collective-permute-start | bytes 393224 | tf_op jit(solution)/shard_map/ppermute | solution.py:20
  45.9 11.2 %collective-permute-start = (bf16[256,512]{1,0:T(8,128)(2,1)S(1)}, bf16[256,512]{1,0:T(8,128)(2,1)S(1)}, u32[]{:S(2)}, u32[]{:S(2)}) collective-permute-start(bf16[256,512]{1,0:T(8,128)(2,1)S(1)} %reshape.418), channel_id=1, source_target_pairs={{0,1},{1,0},{2,3},{3,2},{4,5},{5,4},{6,7},{7,6},{8,9},{9,8},{10,11... | collective-permute-start | bytes 786440 | tf_op jit(solution)/shard_map/ppermute | solution.py:20
  46.2 27.2 %all-to-all-start.1 = ((bf16[64,4,512]{2,1,0:T(4,128)(2,1)}), bf16[64,4,512]{2,1,0:T(4,128)(2,1)}, u32[]{:S(2)}, u32[]{:S(2)}) async-start(bf16[64,4,512]{2,1,0:T(4,128)(2,1)} %bitcast.48), calls=%async_computation.1 | async-start | bytes 524288 | tf_op jit(solution)/shard_map/all_to_all | solution.py:104
  75.9 20.8 %all-to-all-start.2 = ((f32[32,16,128]{2,1,0:T(8,128)}), f32[32,16,128]{2,1,0:T(8,128)}, u32[]{:S(2)}, u32[]{:S(2)}) async-start(f32[32,16,128]{2,1,0:T(8,128)} %broadcast_in_dim.18), calls=%async_computation.2 | async-start | bytes 524288 | tf_op jit(solution)/shard_map/all_to_all | solution.py:146
  89.7 40.2 %collective-permute-start.4 = (bf16[256,512]{1,0:T(8,128)(2,1)}, bf16[256,512]{1,0:T(8,128)(2,1)}, u32[]{:S(2)}, u32[]{:S(2)}) collective-permute-start(bf16[256,512]{1,0:T(8,128)(2,1)} %slice.231), channel_id=1, source_target_pairs={{0,1},{1,0},{2,3},{3,2},{4,5},{5,4},{6,7},{7,6},{8,9},{9,8},{10,11... | collective-permute-start | bytes 786440 | tf_op jit(solution)/shard_map/ppermute | solution.py:20
  90.8 12.2 %collective-permute-start.15 = (bf16[256,512]{1,0:T(8,128)(2,1)}, bf16[256,512]{1,0:T(8,128)(2,1)}, u32[]{:S(2)}, u32[]{:S(2)}) collective-permute-start(bf16[256,512]{1,0:T(8,128)(2,1)} %reshape.428), channel_id=1, source_target_pairs={{0,1},{1,0},{2,3},{3,2},{4,5},{5,4},{6,7},{7,6},{8,9},{9,8},{10,11... | collective-permute-start | bytes 786440 | tf_op jit(solution)/shard_map/ppermute | solution.py:20
  120.7 47.6 %collective-permute-start.20 = (bf16[2,32,2,4,128]{4,3,2,1,0:T(4,128)(2,1)}, bf16[2,32,2,4,128]{4,3,2,1,0:T(4,128)(2,1)S(1)}, u32[]{:S(2)}, u32[]{:S(2)}) collective-permute-start(bf16[2,32,2,4,128]{4,3,2,1,0:T(4,128)(2,1)} %dynamic-slice_bitcast_fusion), channel_id=1, source_target_pairs={{0,2},{2,0},{1,3},{3,1},{4,6},{6,4},{5,7},{7,5},{8,10},{10,8},{9,1... | collective-permute-start | bytes 393224 | tf_op jit(solution)/shard_map/ppermute | solution.py:20
  127.4 56.1 %collective-permute-start.19 = (bf16[2,32,8,3,128]{4,1,3,2,0:T(8,128)(2,1)S(1)}, bf16[2,32,8,3,128]{4,1,3,2,0:T(8,128)(2,1)S(1)}, u32[]{:S(2)}, u32[]{:S(2)}) collective-permute-start(bf16[2,32,8,3,128]{4,1,3,2,0:T(8,128)(2,1)S(1)} %bitcast.318), channel_id=1, source_target_pairs={{0,2},{2,0},{1,3},{3,1},{4,6},{6,4},{5,7},{7,5},{8,10},{10,8},{9,1... | collective-permute-start | bytes 1179656 | tf_op jit(solution)/shard_map/ppermute | solution.py:20
  131.9 21.4 %all-to-all-start.3 = ((bf16[64,4,512]{2,1,0:T(4,128)(2,1)}), bf16[64,4,512]{2,1,0:T(4,128)(2,1)S(1)}, u32[]{:S(2)}, u32[]{:S(2)}) async-start(bf16[64,4,512]{2,1,0:T(4,128)(2,1)} %reshape.421), calls=%async_computation.3 | async-start | bytes 524288 | tf_op jit(solution)/shard_map/all_to_all | solution.py:171
  140.0 15.3 %collective-permute-start.22 = (f32[9,2,128]{2,0,1:T(8,128)S(1)}, f32[9,2,128]{2,0,1:T(8,128)S(1)}, u32[]{:S(2)}, u32[]{:S(2)}) collective-permute-start(f32[9,2,128]{2,0,1:T(8,128)S(1)} %fusion.51), channel_id=1, source_target_pairs={{0,1},{1,0},{2,3},{3,2},{4,5},{5,4},{6,7},{7,6},{8,9},{9,8},{10,11... | collective-permute-start | bytes 27656 | tf_op jit(solution)/shard_map/ppermute | solution.py:20
  153.6 6.6 %collective-permute-start.13 = (bf16[64,4,2,128]{3,0,2,1:T(8,128)(2,1)S(1)}, bf16[64,4,2,128]{3,0,2,1:T(8,128)(2,1)S(1)}, u32[]{:S(2)}, u32[]{:S(2)}) collective-permute-start(bf16[64,4,2,128]{3,0,2,1:T(8,128)(2,1)S(1)} %bitcast.329), channel_id=1, source_target_pairs={{0,2},{2,0},{1,3},{3,1},{4,6},{6,4},{5,7},{7,5},{8,10},{10,8},{9,1... | collective-permute-start | bytes 393224 | tf_op jit(solution)/shard_map/ppermute | solution.py:20
  155.3 5.2 %collective-permute-start.23 = (f32[10,128]{1,0:T(8,128)S(1)}, f32[10,128]{1,0:T(8,128)S(1)}, u32[]{:S(2)}, u32[]{:S(2)}) collective-permute-start(f32[10,128]{1,0:T(8,128)S(1)} %fusion.59), channel_id=1, source_target_pairs={{0,2},{2,0},{1,3},{3,1},{4,6},{6,4},{5,7},{7,5},{8,10},{10,8},{9,1... | collective-permute-start | bytes 15368 | tf_op jit(solution)/shard_map/ppermute | solution.py:20
  160.6 7.8 %collective-permute-start.24 = (f32[10,128]{1,0:T(8,128)S(1)}, f32[10,128]{1,0:T(8,128)S(1)}, u32[]{:S(2)}, u32[]{:S(2)}) collective-permute-start(f32[10,128]{1,0:T(8,128)S(1)} %fusion.62), channel_id=1, source_target_pairs={{0,128},{128,0},{1,129},{129,1},{2,130},{130,2},{3,131},{131,3},{4... | collective-permute-start | bytes 15368 | tf_op jit(solution)/shard_map/ppermute | solution.py:20
  162.7 18.8 %all-to-all-start.4 = ((bf16[64,4,512]{2,1,0:T(4,128)(2,1)}), bf16[64,4,512]{2,1,0:T(4,128)(2,1)S(1)}, u32[]{:S(2)}, u32[]{:S(2)}) async-start(bf16[64,4,512]{2,1,0:T(4,128)(2,1)} %reshape.436), calls=%async_computation.4 | async-start | bytes 524288 | tf_op jit(solution)/shard_map/all_to_all | solution.py:171
  181.8 7.8 %collective-permute-start.17 = (bf16[64,4,2,128]{3,0,2,1:T(8,128)(2,1)S(1)}, bf16[64,4,2,128]{3,0,2,1:T(8,128)(2,1)S(1)}, u32[]{:S(2)}, u32[]{:S(2)}) collective-permute-start(bf16[64,4,2,128]{3,0,2,1:T(8,128)(2,1)S(1)} %bitcast.328), channel_id=1, source_target_pairs={{0,2},{2,0},{1,3},{3,1},{4,6},{6,4},{5,7},{7,5},{8,10},{10,8},{9,1... | collective-permute-start | bytes 393224 | tf_op jit(solution)/shard_map/ppermute | solution.py:20
  183.6 7.9 %collective-permute-start.21 = (bf16[32,32,128]{2,0,1:T(8,128)(2,1)S(1)}, bf16[32,32,128]{2,0,1:T(8,128)(2,1)S(1)}, u32[]{:S(2)}, u32[]{:S(2)}) collective-permute-start(bf16[32,32,128]{2,0,1:T(8,128)(2,1)S(1)} %fusion.28), channel_id=1, source_target_pairs={{0,128},{128,0},{1,129},{129,1},{2,130},{130,2},{3,131},{131,3},{4... | collective-permute-start | bytes 786440 | tf_op jit(solution)/shard_map/ppermute | solution.py:20
  210.2 17.5 %all-to-all-start.6 = ((bf16[32,40,128]{2,1,0:T(8,128)(2,1)}), bf16[32,40,128]{2,1,0:T(8,128)(2,1)S(1)}, u32[]{:S(2)}, u32[]{:S(2)}) async-start(bf16[32,40,128]{2,1,0:T(8,128)(2,1)} %broadcast_in_dim.19), calls=%async_computation.6 | async-start | bytes 655360 | tf_op jit(solution)/shard_map/all_to_all | solution.py:247
  228.2 7.1 %collective-permute-start.25 = (bf16[32,40,128]{2,1,0:T(8,128)(2,1)S(1)}, bf16[32,40,128]{2,1,0:T(8,128)(2,1)S(1)}, u32[]{:S(2)}, u32[]{:S(2)}) collective-permute-start(bf16[32,40,128]{2,1,0:T(8,128)(2,1)S(1)} %all-to-all-done.6), channel_id=1, source_target_pairs={{0,128},{128,0},{1,129},{129,1},{2,130},{130,2},{3,131},{131,3},{4... | collective-permute-start | bytes 983048 | tf_op jit(solution)/shard_map/ppermute | solution.py:20
  (66 other events, 565.9 us)

commit v2 on v1

v2 whole, which is shorter than its diff:
```python
import math

import jax
import jax.numpy as jnp
import numpy as np
from jax import lax
from jax.experimental import pallas as pl
from jax.experimental.pallas import tpu as pltpu
from jax.sharding import Mesh
from jax.sharding import PartitionSpec as P

LAG = 16
EPS = 1e-06
HIGHEST = lax.Precision.HIGHEST
TM = ("xl", "y", "z")
YZ = ("y", "z")
bf16 = jnp.bfloat16
f32 = jnp.float32
FORWARD_FLOPS = 1_000
BACKWARD_FLOPS = 5_000_000_000


def swap(value, axis):
    return lax.ppermute(value, axis, [(0, 1), (1, 0)])


def ordered(own, other, index, axis):
    first = jnp.where(index == 0, own, other)
    second = jnp.where(index == 0, other, own)
    return jnp.stack([first, second], axis=axis)


def pick(value, index, axis):
    return lax.dynamic_index_in_dim(value, index, axis, keepdims=False)


def after(value, *earlier):
    return lax.optimization_barrier((value, *earlier))[0]


HALF = [(n - 1.0) * (1.0 - 0.001) / 2.0 for n in (8.0, 5.0, 5.0, 5.0)]
OFFSET = [0.5, 0.0, 0.0, 0.0]
WIDTH = [4.0, 2.0, 2.0, 2.0]
SHIFT = [0.5 * math.log((a + b) / (a - b)) for a, b in zip(HALF, OFFSET)]


def by_level(values, shape):
    row = lax.broadcasted_iota(jnp.int32, shape, 0)
    return jnp.where(row == 0, values[0], values[1]).astype(f32)


def dot(a, b, ca, cb, **kw):
    return lax.dot_general(a, b, (((ca,), (cb,)), ((), ())), preferred_element_type=f32, **kw)


def per_head(values, first):
    one = jnp.sum(jnp.where(first, values, 0.0), axis=-1, keepdims=True)
    two = jnp.sum(jnp.where(first, 0.0, values), axis=-1, keepdims=True)
    return one, two


def attention_forward(b, scale, normed, w, ids_row, ids_col, qkv, invs, probs, attended):
    frames, share = qkv.shape[2:]
    hd = share // 2
    first = first_lanes(frames, share)
    t = lax.broadcasted_iota(jnp.int32, (frames, frames), 0)
    u = lax.broadcasted_iota(jnp.int32, (frames, frames), 1)
    visible = jnp.logical_and(ids_col[...] == ids_row[...], u <= t)
    for p in range(2):
        raw = dot(normed[p], w[...], 1, 0)
        parts = []
        for k in range(2):
            one = raw[:, k * share : (k + 1) * share]
            sums = per_head(one * one, first)
            inv0 = lax.rsqrt(sums[0] * (1.0 / hd) + EPS)
            inv1 = lax.rsqrt(sums[1] * (1.0 / hd) + EPS)
            invs[p, :, k * 2 : k * 2 + 1] = inv0
            invs[p, :, k * 2 + 1 : k * 2 + 2] = inv1
            parts.append((one * jnp.where(first, inv0, inv1)).astype(bf16))
        parts.append(raw[:, 2 * share :].astype(bf16))
        query, keys, values = parts
        for k in range(3):
            qkv[p, k] = parts[k]
        mixed = None
        zero = jnp.zeros_like(keys)
        for h in range(2):
            mask = first if h == 0 else jnp.logical_not(first)
            dots = dot(query, jnp.where(mask, keys, zero), 1, 1)
            weights = jnp.where(visible, jnp.exp(dots * (scale[b * 2 + h] * (1.0 / math.sqrt(hd)))), 0.0)
            prob = weights / jnp.sum(weights, axis=-1, keepdims=True)
            probs[p, h] = prob
            one = dot(prob.astype(bf16), jnp.where(mask, values, zero), 1, 0)
            mixed = one if mixed is None else mixed + one
        attended[p] = mixed.astype(bf16)


def forward_kernel(
    scale, x_own, x_other, gain, w_own, w_other, wo_own, wo_other, act, ids_row, ids_col,
    normed, qkv0, qkv1, invs0, invs1, probs0, probs1, attended0, attended1, enc_part, branch_other, part8,
):
    frames = x_own.shape[0]
    for p in range(2):
        x = (x_own, x_other)[p][...].astype(f32)
        inverse = lax.rsqrt(jnp.mean(x * x, axis=-1, keepdims=True) + EPS)
        normed[p] = (x * inverse * gain[...]).astype(bf16)
    attention_forward(0, scale, normed, w_own, ids_row, ids_col, qkv0, invs0, probs0, attended0)
    attention_forward(1, scale, normed, w_other, ids_row, ids_col, qkv1, invs1, probs1, attended1)
    x = x_own[...].astype(f32)
    for p in range(2):
        branch = dot(attended0[p], wo_own[...], 1, 0) + dot(attended1[p], wo_other[...], 1, 0)
        if p == 0:
            enc_part[...] = x + branch
        else:
            branch_other[...] = branch.astype(bf16)
    terms = dot(act[...], x, 1, 1, precision=HIGHEST)
    for wo, att in ((wo_own, attended0), (wo_other, attended1)):
        act_out = dot(act[...], wo[...].astype(f32), 1, 1, precision=HIGHEST)
        terms = terms + dot(act_out, att[0].astype(f32) + att[1].astype(f32), 1, 1, precision=HIGHEST)
    terms = terms * (1.0 / 256.0)
    moved = pltpu.roll(terms, frames - LAG, 1)
    moved = jnp.where(lax.broadcasted_iota(jnp.int32, moved.shape, 1) < frames - LAG, moved, 0.0)
    part = terms[:4] + moved[4:]
    part8[0:4] = part[:, : frames // 2]
    part8[4:8] = part[:, frames // 2 :]


def attention_back(b, scale, up, wo, qkv, invs, probs, gp, first):
    share = wo.shape[0]
    hd = share // 2
    sums = [None, None]
    factor = jnp.where(
        first[:1], scale[b * 2] * (1.0 / math.sqrt(hd)), scale[b * 2 + 1] * (1.0 / math.sqrt(hd))
    )
    for p in range(2):
        query, keys, values = qkv[p, 0], qkv[p, 1], qkv[p, 2]
        zero = jnp.zeros_like(keys)
        grad_att = dot(up[p], wo[...], 1, 1).astype(bf16)
        grad_q = grad_k = grad_v = None
        for h in range(2):
            mask = first if h == 0 else jnp.logical_not(first)
            grad_probs = dot(grad_att, jnp.where(mask, values, zero), 1, 1)
            prob = probs[p, h]
            inner = jnp.sum(grad_probs * prob, axis=-1, keepdims=True)
            grad_scores = (prob * (grad_probs - inner)).astype(bf16)
            one = dot(grad_scores, jnp.where(mask, keys, zero), 1, 0)
            grad_q = one if grad_q is None else grad_q + one
            one = dot(grad_scores, jnp.where(mask, query, zero), 0, 0)
            grad_k = one if grad_k is None else grad_k + one
            one = dot(prob.astype(bf16), jnp.where(mask, grad_att, zero), 0, 0)
            grad_v = one if grad_v is None else grad_v + one
        for k in range(2):
            grad, base = ((grad_q, query), (grad_k, keys))[k]
            base = base.astype(f32)
            one, two = per_head(grad * base, first)
            if k == 0:
                one_sum, two_sum = jnp.sum(one, axis=0, keepdims=True), jnp.sum(two, axis=0, keepdims=True)
                sums[0] = one_sum if sums[0] is None else sums[0] + one_sum
                sums[1] = two_sum if sums[1] is None else sums[1] + two_sum
            mean = jnp.where(first, one, two) * (1.0 / hd)
            inv = jnp.where(first, invs[p, :, 2 * k : 2 * k + 1], invs[p, :, 2 * k + 1 : 2 * k + 2])
            gp[p, :, k * share : (k + 1) * share] = (factor * inv * (grad - base * mean)).astype(bf16)
        gp[p, :, 2 * share : 3 * share] = grad_v.astype(bf16)
    lane = lax.broadcasted_iota(jnp.int32, (1, share), 1)
    return jnp.where(lane == 0, sums[0], 0.0) + jnp.where(lane == 1, sums[1], 0.0)


def weight_grads(target, normed, gp, up, attended):
    split = gp.shape[2]
    qkv_part = dot(normed[0], gp[0], 0, 0) + dot(normed[1], gp[1], 0, 0)
    out_part = dot(up[0], attended[0], 0, 0) + dot(up[1], attended[1], 0, 0)
    target[:, :split] = qkv_part.astype(target.dtype)
    target[:, split:] = out_part.astype(target.dtype)


def first_lanes(frames, share):
    return lax.broadcasted_iota(jnp.int32, (frames, share), 1) < share // 2


def other_kernel(
    scale, place, packed, cot_own, cot_other, act, wo, qkv, invs, probs, attended, normed,
    bounded_out, eight_out, up, gp, grads, scale_row,
    pooled,
):
    frames, width = up.shape[1:]
    share = wo.shape[0]
    summed = jnp.sum(packed[...], axis=0)
    latent = jnp.concatenate([summed[0:4], summed[4:8]], axis=1)
    cot_act = jnp.concatenate([summed[8:12], summed[12:16]], axis=1)
    shape = latent.shape
    half, offset, widths = by_level(HALF, shape), by_level(OFFSET, shape), by_level(WIDTH, shape)
    curve = jnp.tanh(latent + by_level(SHIFT, shape))
    bounded_out[...] = (curve * half - offset) / widths
    grad_latent = cot_act * (half / widths) * (1.0 - curve * curve)
    moved = pltpu.roll(grad_latent, LAG, 1)
    moved = jnp.where(lax.broadcasted_iota(jnp.int32, shape, 1) >= LAG, moved, 0.0)
    eight = jnp.concatenate([grad_latent, moved], axis=0)
    eight_out[...] = eight
    pooled[...] = dot(eight.T, act[...], 1, 0, precision=HIGHEST) * (1.0 / 256.0)
    xh, core = place[0], place[1]
    for p in range(2):
        core_p = core if p == 0 else 1 - core
        for r in range(4):
            block_r = (xh if r < 2 else 1 - xh) * 2 + (core_p if r % 2 == 0 else 1 - core_p)
            cols = pl.ds(pl.multiple_of(block_r * share, share), share)
            cot = (cot_own, cot_other)[p][:, r * share : (r + 1) * share].astype(f32)
            up[p, :, cols] = (cot + pooled[:, cols]).astype(bf16)
    scale_row[...] = attention_back(1, scale, up, wo, qkv, invs, probs, gp, first_lanes(frames, share))
    weight_grads(grads, normed, gp, up, attended)


def own_kernel(
    scale, place, eight, up, wo, w_own, w_other, qkv, invs, probs, attended, normed, x_own, x_other,
    encoded, gp_other, scale_other,
    grads, small, normed_own, normed_other,
    gp,
):
    frames, width = x_own.shape
    share = wo.shape[0]
    scale_own = attention_back(0, scale, up, wo, qkv, invs, probs, gp, first_lanes(frames, share))
    gain_part = None
    for p in (1, 0):
        grad = dot(gp[p], w_own[...], 1, 1) + dot(gp_other[p], w_other[...], 1, 1)
        x = (x_own, x_other)[p][...].astype(f32)
        inverse = lax.rsqrt(jnp.mean(x * x, axis=-1, keepdims=True) + EPS)
        one = jnp.sum(grad * (x * inverse), axis=0, keepdims=True)
        gain_part = one if gain_part is None else gain_part + one
        if p == 0:
            normed_own[...] = grad
        else:
            normed_other[:frames] = grad.astype(bf16)
    weight_grads(grads, normed, gp, up, attended)
    act_part = dot(eight[...], encoded[...].astype(f32), 1, 0, precision=HIGHEST)
    xh, core = place[0], place[1]
    none = jnp.zeros((1, share), f32)
    for r in range(4):
        second = (xh if r < 2 else 1 - xh) == 1
        odd = (core if r % 2 == 0 else 1 - core) == 1

        def block(value):
            low = jnp.where(odd, value[:, share : 2 * share], value[:, :share])
            high = jnp.where(odd, value[:, 3 * share :], value[:, 2 * share : 3 * share])
            return jnp.where(second, high, low)

        tail = (scale_own, none, scale_other[...], none)[r]
        rows = jnp.concatenate([block(act_part), block(gain_part), tail, jnp.zeros((6, share), f32)])
        if r == 1:
            normed_other[frames:, :share] = rows.astype(bf16)
        else:
            small[r] = rows
    small[1] = jnp.zeros((16, share), f32)
    normed_other[frames:, share:] = jnp.zeros((16, width - share), bf16)


def finish_kernel(x_own, gain, grad_own, grad_got, up, encoded, out):
    x = x_own[...].astype(f32)
    frames, width = x.shape
    inverse = lax.rsqrt(jnp.mean(x * x, axis=-1, keepdims=True) + EPS)
    scaled = gain[...] * (grad_own[...] + grad_got[:frames].astype(f32))
    row_dot = jnp.mean(scaled * x, axis=-1, keepdims=True)
    grad = inverse * scaled - x * (inverse * inverse * inverse * row_dot)
    out[:, :width] = encoded[...]
    out[:, width : 2 * width] = (up[0].astype(f32) + grad).astype(bf16)


VMEM = pl.BlockSpec(memory_space=pltpu.VMEM)
SMEM = pl.BlockSpec(memory_space=pltpu.SMEM)


def call(kernel, scalars, arrays, outs, flops, scratch=()):
    return pl.pallas_call(
        kernel,
        out_shape=[jax.ShapeDtypeStruct(s, d) for s, d in outs],
        in_specs=[SMEM] * len(scalars) + [VMEM] * len(arrays),
        out_specs=[VMEM] * len(outs),
        scratch_shapes=scratch,
        compiler_params=pltpu.CompilerParams(vmem_limit_bytes=60 * 1024 * 1024),
        cost_estimate=pl.CostEstimate(flops=flops, bytes_accessed=flops // 1000, transcendentals=0),
    )(*scalars, *arrays)


def local(
    frames_in,
    norm_gain,
    w_qkv,
    qk_scale,
    w_out,
    w_act,
    action_codes,
    episode_ids,
    cotangent,
    action_cotangent,
):
    fl, patches, width = frames_in.shape
    share = cotangent.shape[2]
    n_tm = lax.axis_size("xl") * lax.axis_size("y") * lax.axis_size("z")
    n_yz = lax.axis_size("y") * lax.axis_size("z")
    frames = fl * n_tm
    group = patches // 4
    tokens = frames * patches
    hd = 64
    xl, xh, core = lax.axis_index("xl"), lax.axis_index("xh"), lax.axis_index("core")
    block = xh * 2 + core
    tm = lax.axis_index(TM)
    gain = norm_gain.reshape(1, width)

    few = jnp.concatenate(
        [w_act.transpose(0, 2, 1).reshape(8, share), jnp.pad(qk_scale[None], ((0, 7), (0, share - 2)))]
    )
    few_got = swap(few, "core")
    few = ordered(few, few_got, core, 0)

    sent = lax.dynamic_slice_in_dim(frames_in, block * group, group, 1).transpose(1, 0, 2)
    sent = after(sent, few_got)
    x_own = lax.all_to_all(sent, TM, 0, 0, tiled=True)
    x_own = x_own.reshape(frames, width)
    x_other = swap(x_own, "core")

    w_own = w_qkv.reshape(width, 3 * share)
    w_other = swap(w_own, "xh")
    wo_other = swap(after(w_out, few_got), "xh")
    place = jnp.stack([xh, core]).astype(jnp.int32)
    few_other = swap(few, "xh")
    act = ordered(few, few_other, xh, 0).reshape(4, 16, share)[:, :8]
    act = act.transpose(1, 0, 2).reshape(8, width)
    scale = jnp.concatenate([qk_scale, pick(few_other, core, 0)[8, :2]])

    cot = after(cotangent, few_got).reshape(fl, 2, 2, group, share)
    cot = jnp.concatenate([pick(cot, core, 2), swap(pick(cot, 1 - core, 2), "core")], axis=-1)
    cot = jnp.concatenate([pick(cot, xh, 1), swap(pick(cot, 1 - xh, 1), "xh")], axis=-1)
    cot = after(cot.transpose(1, 0, 2), x_own)
    cot_own = lax.all_to_all(cot, TM, 0, 0, tiled=True).reshape(frames, width)
    cot_other = swap(cot_own, "core")

    ids_row, ids_col = episode_ids[None], episode_ids[:, None]
    (
        normed, qkv0, qkv1, invs0, invs1, probs0, probs1, attended0, attended1, enc_part, branch_other, part8
    ) = call(
        forward_kernel,
        (scale,),
        (x_own, x_other, gain, w_own, w_other, w_out, wo_other, act, ids_row, ids_col),
        (
            ((2, frames, width), bf16),
            ((2, 3, frames, share), bf16),
            ((2, 3, frames, share), bf16),
            ((2, frames, 4), f32),
            ((2, frames, 4), f32),
            ((2, 2, frames, frames), f32),
            ((2, 2, frames, frames), f32),
            ((2, frames, share), bf16),
            ((2, frames, share), bf16),
            ((frames, width), f32),
            ((frames, width), bf16),
            ((8, frames // 2), f32),
        ),
        FORWARD_FLOPS,
    )

    ac_t = jnp.broadcast_to(action_cotangent.T[:, None], (4, n_tm, fl)).reshape(4, frames)
    ac_t = jnp.where(jnp.arange(frames)[None] // fl == tm, ac_t, 0.0)
    ac8 = jnp.concatenate([ac_t[:, : frames // 2], ac_t[:, frames // 2 :]])
    part8 = part8 + swap(part8, "core")
    packed = jnp.concatenate([part8, ac8])
    from_xh = swap(part8, "xh")
    from_xl = swap(packed, "xl")
    from_both = lax.ppermute(part8, ("xl", "xh"), [(0, 3), (1, 2), (2, 1), (3, 0)])
    far = jnp.concatenate([from_xh + from_both, jnp.zeros_like(ac8)])
    packed = (packed + from_xl) + far
    packed = jnp.broadcast_to(packed[None], (n_yz, 16, frames // 2))
    packed = after(packed, cot_own)
    packed = lax.all_to_all(packed, YZ, 0, 0, tiled=True)

    encoded_own = (enc_part + swap(branch_other, "core").astype(f32)).astype(bf16)

    bounded, eight, up, gp_other, grads_other, scale_other = call(
        other_kernel,
        (scale, place),
        (packed, cot_own, cot_other, act, wo_other, qkv1, invs1, probs1, attended1, normed),
        (
            ((4, frames), f32),
            ((8, frames), f32),
            ((2, frames, width), bf16),
            ((2, frames, 3 * share), bf16),
            ((width, 4 * share), bf16),
            ((1, share), f32),
        ),
        BACKWARD_FLOPS,
        scratch=[pltpu.VMEM((frames, width), f32)],
    )
    grads_got = swap(grads_other, "xh")
    grads_own, small, normed_own, normed_other = call(
        own_kernel,
        (scale, place),
        (
            eight, up, w_out, w_own, w_other, qkv0, invs0, probs0, attended0, normed, x_own, x_other,
            encoded_own, gp_other, scale_other,
        ),
        (
            ((width, 4 * share), f32),
            ((4, 16, share), f32),
            ((frames, width), f32),
            ((frames + 16, width), bf16),
        ),
        BACKWARD_FLOPS,
        scratch=[pltpu.VMEM((2, frames, 3 * share), bf16)],
    )

    normed_got = swap(normed_other, "core")
    (both_out,) = call(
        finish_kernel,
        (),
        (x_own, gain, normed_own, normed_got, up, encoded_own),
        (((frames, 2 * width), bf16),),
        10 * frames * width,
    )
    far = lax.ppermute(small[3], ("xh", "core"), [(0, 3), (1, 2), (2, 1), (3, 0)])
    small = (small[0] + normed_got[frames:, :share].astype(f32)) + (swap(small[2], "xh") + far)
    small = jnp.pad(small.astype(bf16), ((0, frames - 16), (0, 0)))
    grads = (grads_own + grads_got.astype(f32)).astype(bf16)
    both_out = jnp.concatenate([both_out, grads[:frames], grads[frames:], small], axis=1)
    home = lax.all_to_all(both_out.reshape(n_tm, fl, 4 * width + share), TM, 0, 0, tiled=True)
    summed = jnp.sum(home[:, :, 2 * width :].astype(f32), axis=0).astype(bf16)
    summed = jnp.broadcast_to(summed[None], (n_tm, *summed.shape))
    summed = lax.all_to_all(summed, TM, 0, 0, tiled=True).reshape(frames, 2 * width + share)
    home = home[:, :, : 2 * width]
    home = home.reshape(group, fl, 2, 2, 2, share)
    got = swap(pick(home, 1 - xh, 3), "xh")
    home = ordered(pick(home, xh, 3), got, xh, 0)
    got = swap(pick(home, 1 - core, 4), "core")
    home = ordered(pick(home, core, 4), got, core, 1)
    home = home.transpose(4, 3, 0, 1, 2, 5).reshape(2, fl, patches, share)
    encoded, grad_frames = home[0], home[1]

    half_level, offsets, widths = (np.array(v, np.float32)[:, None] for v in (HALF, OFFSET, WIDTH))
    bases = jnp.array([1, 8, 40, 200], dtype=jnp.int32)[:, None]
    radices = jnp.array([8, 5, 5, 5], dtype=jnp.int32)[:, None]
    digits = action_codes[None, :] // bases % radices
    bounded_own = lax.dynamic_slice_in_dim(bounded, tm * fl, fl, 1)
    quant_gap = ((digits.astype(f32) - widths) / widths - bounded_own).T

    both = jnp.concatenate([summed[:, :width], summed[:, width : 2 * width]]).astype(f32)
    norm_factor = 1.0 / math.sqrt(tokens)
    grad_qkv = both[:, : 3 * share].reshape(width, 3, share) * norm_factor
    grad_out = both[:, 3 * share : 4 * share].T * norm_factor
    small = summed[:16, 2 * width :].astype(f32)
    grad_act = small[:8].reshape(2, 4, share).transpose(0, 2, 1) * (1.0 / math.sqrt(frames) / patches)
    grad_gain = small[8] * norm_factor
    grad_qk_scale = small[9, :2] * (norm_factor / math.sqrt(hd))
    return (encoded, quant_gap, grad_frames, grad_gain, grad_qkv, grad_qk_scale, grad_out, grad_act)


def solution(mesh):
    fine = Mesh(mesh.devices.reshape(2, 4, 8, 2, 2), ("xl", "y", "z", "xh", "core"))
    head = ("xh", "core")
    in_specs = (
        P(TM, None, None),
        P(),
        P(None, None, head),
        P(head),
        P(head, None),
        P(None, head, None),
        P(TM),
        P(),
        P(TM, None, head),
        P(TM, None),
    )
    out_specs = (
        P(TM, None, head),
        P(TM, None),
        P(TM, None, head),
        P(head),
        P(None, None, head),
        P(head),
        P(head, None),
        P(None, head, None),
    )
    return jax.shard_map(local, mesh=fine, in_specs=in_specs, out_specs=out_specs, check_vma=False)
```

time: 239 us -> 181 us (0.76)
  waiting for transfers between devices: 77.2 us -> 38.2 us
  Pallas kernels: 0 us -> 23 us
  starting transfers between devices: 79 us -> 56.9 us
  blocking collectives: 16.6 us -> 37.3 us
  local copies, waits for them, and re-layouts: 34.3 us -> 16.8 us
  matrix products: 14.3 us -> 0 us
  other arithmetic: 14.1 us -> 7.17 us
    ppermute x26 -> x17, waiting for transfers between devices: 36.7 us -> 4.26 us  [swap(): return lax.ppermute(value, axis, [(0, 1), (1, 0)])]
    pallas_call x0 -> x4, Pallas kernels: none -> 23 us  [call(): pl.pallas_call(kernel, out_shape=[jax.ShapeDtypeStruct(s, d) for s, d in...]
    all_to_all x3 -> x1, waiting for transfers between devices: 36.9 us -> 15.9 us  [local(): lax.all_to_all(summed, TM, 0, 0, tiled=True)]
    all_to_all x1, blocking collectives: 16.6 us -> 37.3 us  [local(): lax.all_to_all(both_out.reshape(n_tm, fl, 4 * width + share), TM, 0, 0, t...]
    dot_general x17 -> x0, matrix products: 14.3 us -> none  [the longest x9 5.01 us: dot(): lax.dot_general(a, b, (((ca,), (cb,)), ((), ())), preferred_element_type=...]
    all_to_all x3 -> x1, starting transfers between devices: 18.2 us -> 6.17 us  [local(): lax.all_to_all(summed, TM, 0, 0, tiled=True)]
    ppermute x26 -> x17, starting transfers between devices: 27.1 us -> 15.3 us  [swap(): return lax.ppermute(value, axis, [(0, 1), (1, 0)])]
    all_to_all x1, waiting for transfers between devices: 0.01 us -> 8.21 us  [local(): x_own = lax.all_to_all(sent, TM, 0, 0, tiled=True)]
  transfers between devices with their start and end apart: 32 -> 23, of which waited for: 16 -> 9; matrix products, arithmetic and copies ran while one was open for 21% -> 8% of each run, Pallas kernels for 0% -> 9%
where the time goes in v2:
time: 181 us
  starting transfers between devices  56.9 us (31%)
  waiting for transfers between devices  38.2 us (21%)
  blocking collectives  37.3 us (21%)
  Pallas kernels  23 us (13%)
  local copies, waits for them, and re-layouts  16.8 us (9%)
  other arithmetic  7.17 us (4%)
    all_to_all x1, blocking collectives, local(): lax.all_to_all(both_out.reshape(n_tm, fl, 4 * width + share), TM, 0, 0, t...  37.3 us
    pallas_call x4, Pallas kernels, call(): pl.pallas_call(kernel, out_shape=[jax.ShapeDtypeStruct(s, d) for s, d in...  23 us
    all_to_all x1, waiting for transfers between devices, local(): lax.all_to_all(summed, TM, 0, 0, tiled=True)  15.9 us
    ppermute x17, starting transfers between devices, swap(): return lax.ppermute(value, axis, [(0, 1), (1, 0)])  15.3 us
    all_to_all x1, starting transfers between devices, local(): x_own = lax.all_to_all(sent, TM, 0, 0, tiled=True)  13.2 us
    all_to_all x1, waiting for transfers between devices, local(): packed = lax.all_to_all(packed, YZ, 0, 0, tiled=True)  9.64 us
    all_to_all x1, starting transfers between devices, local(): packed = lax.all_to_all(packed, YZ, 0, 0, tiled=True)  9.57 us
    all_to_all x1, starting transfers between devices, local(): cot_own = lax.all_to_all(cot, TM, 0, 0, tiled=True).reshape(frames, width)  8.33 us
  transfers between devices with their start and end apart: 23, of which 9 were waited for; matrix products, arithmetic and copies ran while one was open for 8% of the time, Pallas kernels for 9%

profile of v2, /device:TPU:2, one launch (start us, length us, event | category | flops | bytes accessed | tf_op | source)
XLA Modules:
  0.0 180.6 jit_solution(5195480772234602921)
XLA Ops:
  1.5 1.2 copy.73
  2.9 2.2 %collective-permute-start.3 = (bf16[512,384]{1,0:T(8,128)(2,1)S(1)}, bf16[512,384]{1,0:T(8,128)(2,1)S(1)}, u32[]{:S(2)}, u32[]{:S(2)}) collective-permute-start(bf16[512,384]{1,0:T(8,128)(2,1)S(1)} %copy.75.w_own), channel_id=1, source_target_pairs={{0,2},{2,0},{1,3},{3,1},{4,6},{6,4},{5,7},{7,5},{8,10},{10,8},{9,1... | collective-permute-start | bytes 1179656 | tf_op jit(solution)/shard_map/ppermute | solution.py:24
  7.2 1.5 collective-permute-start.1
  8.7 13.2 %all-to-all-start = ((bf16[64,4,512]{2,1,0:T(4,128)(2,1)}), bf16[64,4,512]{2,1,0:T(4,128)(2,1)S(1)}, u32[]{:S(2)}, u32[]{:S(2)}) async-start(bf16[64,4,512]{2,1,0:T(4,128)(2,1)} %bitcast.92), calls=%async_computation | async-start | bytes 524288 | tf_op jit(solution)/shard_map/all_to_all | solution.py:314
  21.9 2.2 %collective-permute-start.4 = (bf16[128,512]{1,0:T(8,128)(2,1)S(1)}, bf16[128,512]{1,0:T(8,128)(2,1)S(1)}, u32[]{:S(2)}, u32[]{:S(2)}) collective-permute-start(bf16[128,512]{1,0:T(8,128)(2,1)S(1)} %copy-done.12), channel_id=1, source_target_pairs={{0,2},{2,0},{1,3},{3,1},{4,6},{6,4},{5,7},{7,5},{8,10},{10,8},{9,1... | collective-permute-start | bytes 393224 | tf_op jit(solution)/shard_map/ppermute | solution.py:24
  25.6 1.5 collective-permute-start.10
  27.1 8.2 %all-to-all-done = bf16[64,4,512]{2,1,0:T(4,128)(2,1)S(1)} async-done(((bf16[64,4,512]{2,1,0:T(4,128)(2,1)}), bf16[64,4,512]{2,1,0:T(4,128)(2,1)S(1)}, u32[]{:S(2)}, u32[]{:S(2)}) %all-to-all-start) | async-done | bytes 262176 | tf_op jit(solution)/shard_map/all_to_all | solution.py:314
  37.1 8.3 %all-to-all-start.1 = ((bf16[64,4,512]{2,1,0:T(4,128)(2,1)}), bf16[64,4,512]{2,1,0:T(4,128)(2,1)S(1)}, u32[]{:S(2)}, u32[]{:S(2)}) async-start(bf16[64,4,512]{2,1,0:T(4,128)(2,1)} %copy.78), calls=%async_computation.1 | async-start | bytes 524288 | tf_op jit(solution)/shard_map/all_to_all | solution.py:331
  46.3 7.8 %shard_map.188 = (bf16[2,256,512]{2,1,0:T(8,128)(2,1)}, bf16[2,3,256,128]{3,2,1,0:T(8,128)(2,1)}, bf16[2,3,256,128]{3,2,1,0:T(8,128)(2,1)}, f32[2,256,4]{2,1,0:T...) custom-call(f32[4]{0:T(128)} %pad_maximum_fusion.3.scale, ...), custom_call_target="tpu_custom_call" | custom-call | flops 1000 | bytes 1 | tf_op jit(solution)/shard_map/pallas_call | solution.py:270
  54.2 1.4 collective-permute-done.5
  56.9 1.7 collective-permute-start.7
  58.6 1.4 collective-permute-start.8
  60.0 2.0 %collective-permute-done.7 = f32[8,128]{1,0:T(8,128)S(1)} collective-permute-done((f32[8,128]{1,0:T(8,128)S(1)}, f32[8,128]{1,0:T(8,128)S(1)}, u32[]{:S(2)}, u32[]{:S(2)}) %collective-permute-start.7) | collective-permute-done | bytes 4128 | tf_op jit(solution)/shard_map/ppermute | solution.py:24
  63.1 9.6 %all-to-all-start.2 = ((f32[32,16,128]{2,1,0:T(8,128)}), f32[32,16,128]{2,1,0:T(8,128)S(1)}, u32[]{:S(2)}, u32[]{:S(2)}) async-start(f32[32,16,128]{2,1,0:T(8,128)} %broadcast_in_dim.50), calls=%async_computation.2 | async-start | bytes 524288 | tf_op jit(solution)/shard_map/all_to_all | solution.py:370
  74.3 9.6 %all-to-all-done.2.packed = f32[32,16,128]{2,1,0:T(8,128)S(1)} async-done(((f32[32,16,128]{2,1,0:T(8,128)}), f32[32,16,128]{2,1,0:T(8,128)S(1)}, u32[]{:S(2)}, u32[]{:S(2)}) %all-to-all-start.2) | async-done | bytes 262176 | tf_op jit(solution)/shard_map/all_to_all | solution.py:370
  84.6 5.9 %shard_map.189 = (f32[4,256]{1,0:T(4,128)}, f32[8,256]{1,0:T(8,128)}, bf16[2,256,512]{2,1,0:T(8,128)(2,1)}, bf16[2,256,384]{2,1,0:T(8,128)(2,1)}, bf16[512,512]{1,0:T(8,128)(2,1)}, /*index=5*/f32[1,128]{1,0:T(1,128)}) custom-call(f32[4]{0:T(128)} %pad_maximum_fusion.3.scale, s32[2]{0:T(128)} %pad_add_fusion.1.place, f32[32,16,128]{2,1,0:T(8,128)} %copy-done.10, ...), custom_call_target="tpu_custom_call" | custom-call | flops 5000000000 | bytes 5000000 | tf_op jit(solution)/shard_map/pallas_call | solution.py:270
  90.5 3.1 %collective-permute-start.14 = (bf16[512,512]{1,0:T(8,128)(2,1)}, bf16[512,512]{1,0:T(8,128)(2,1)S(1)}, u32[]{:S(2)}, u32[]{:S(2)}) collective-permute-start(bf16[512,512]{1,0:T(8,128)(2,1)} %get-tuple-element.59), channel_id=1, source_target_pairs={{0,2},{2,0},{1,3},{3,1},{4,6},{6,4},{5,7},{7,5},{8,10},{10,8},{9,1... | collective-permute-start | bytes 1572872 | tf_op jit(solution)/shard_map/ppermute | solution.py:24
  93.6 6.7 %shard_map.190 = (f32[512,512]{1,0:T(8,128)}, f32[4,16,128]{2,1,0:T(8,128)}, f32[256,512]{1,0:T(8,128)}, bf16[272,512]{1,0:T(8,128)(2,1)}) custom-call(f32[4]{0:T(128)} %pad_maximum_fusion.3.scale, s32[2]{0:T(128)} %pad_add_fusion.1.place, f32[8,256]{1,0:T(8,128)} %get-tuple-element.46.eight, bf16[2,256,512]{2,1,0:T(8,128)(2,1)} %get-tuple-element.47.up, ...), custom_call_target="tpu_custom_call" | custom-call | flops 5000000000 | bytes 5000000 | tf_op jit(solution)/shard_map/pallas_call | solution.py:270
  101.5 2.9 %collective-permute-start.16 = (f32[16,128]{1,0:T(8,128)S(1)}, f32[16,128]{1,0:T(8,128)S(1)}, u32[]{:S(2)}, u32[]{:S(2)}) collective-permute-start(f32[16,128]{1,0:T(8,128)S(1)} %get-tuple-element.118), channel_id=1, source_target_pairs={{0,3},{1,2},{2,1},{3,0},{4,7},{5,6},{6,5},{7,4},{8,11},{9,10},{10,... | collective-permute-start | bytes 24584 | tf_op jit(solution)/shard_map/ppermute | solution.py:415
  105.2 2.6 %shard_map.191 = bf16[256,1024]{1,0:T(8,128)(2,1)} custom-call(bf16[256,512]{1,0:T(8,128)(2,1)} %copy-done.1, f32[1,512]{1,0:T(1,128)} %bitcast.103, f32[256,512]{1,0:T(8,128)} %get-tuple-element.56.grad_own, bf16[272,512]{1,0:T(8,128)(2,1)} %copy-done.7, bf16[2,256,512]{2,1,0:T(8,128)(2,1)} %get-tuple-element.47.up, bf16[256,512]{1,0:T(8,128)(2,1)} %add_convert_fusion.1.encoded), custom_call_target="tpu_custom_call" | custom-call | flops 1310720 | bytes 1310 | tf_op jit(solution)/shard_map/pallas_call | solution.py:270
  109.9 37.3 %all_to_all.25 = bf16[64,4,2176]{2,1,0:T(4,128)(2,1)S(1)} all-to-all(bf16[64,4,2176]{2,1,0:T(4,128)(2,1)S(1)} %reshape.129), channel_id=1, replica_groups=mesh['xl'=2,'y'=4,'z'=8,'xh'=2,'core'=2] {'xl','y','z'}, dimensions={0} | all-to-all | bytes 2228224 | tf_op jit(solution)/shard_map/all_to_all | solution.py:420
  148.0 1.6 collective-permute-start.17
  150.9 6.2 %all-to-all-start.4 = ((bf16[64,4,1152]{2,1,0:T(4,128)(2,1)}), bf16[64,4,1152]{2,1,0:T(4,128)(2,1)S(1)}, u32[]{:S(2)}, u32[]{:S(2)}) async-start(bf16[64,4,1152]{2,1,0:T(4,128)(2,1)} %broadcast_in_dim.51), calls=%async_computation.4 | async-start | bytes 1179648 | tf_op jit(solution)/shard_map/all_to_all | solution.py:423
  160.4 15.9 %all-to-all-done.4 = bf16[64,4,1152]{2,1,0:T(4,128)(2,1)S(1)} async-done(((bf16[64,4,1152]{2,1,0:T(4,128)(2,1)}), bf16[64,4,1152]{2,1,0:T(4,128)(2,1)S(1)}, u32[]{:S(2)}, u32[]{:S(2)}) %all-to-all-start.4) | async-done | bytes 589856 | tf_op jit(solution)/shard_map/all_to_all | solution.py:423
  (144 shorter events, 25.5 us)
Async XLA Ops:
  1.5 5.7 %collective-permute-start = (f32[16,128]{1,0:T(8,128)S(1)}, f32[16,128]{1,0:T(8,128)S(1)}, u32[]{:S(2)}, u32[]{:S(2)}) collective-permute-start(f32[16,128]{1,0:T(8,128)S(1)} %select_maximum_fusion), channel_id=1, source_target_pairs={{0,1},{1,0},{2,3},{3,2},{4,5},{5,4},{6,7},{7,6},{8,9},{9,8},{10,11... | collective-permute-start | bytes 24584 | tf_op jit(solution)/shard_map/ppermute | solution.py:24
  2.9 42.5 %collective-permute-start.3 = (bf16[512,384]{1,0:T(8,128)(2,1)S(1)}, bf16[512,384]{1,0:T(8,128)(2,1)S(1)}, u32[]{:S(2)}, u32[]{:S(2)}) collective-permute-start(bf16[512,384]{1,0:T(8,128)(2,1)S(1)} %copy.75.w_own), channel_id=1, source_target_pairs={{0,2},{2,0},{1,3},{3,1},{4,6},{6,4},{5,7},{7,5},{8,10},{10,8},{9,1... | collective-permute-start | bytes 1179656 | tf_op jit(solution)/shard_map/ppermute | solution.py:24
  7.2 17.1 %collective-permute-start.1 = (f32[2,16,128]{2,1,0:T(8,128)S(1)}, f32[2,16,128]{2,1,0:T(8,128)S(1)}, u32[]{:S(2)}, u32[]{:S(2)}) collective-permute-start(f32[2,16,128]{2,1,0:T(8,128)S(1)} %pad_maximum_fusion.1), channel_id=1, source_target_pairs={{0,2},{2,0},{1,3},{3,1},{4,6},{6,4},{5,7},{7,5},{8,10},{10,8},{9,1... | collective-permute-start | bytes 49160 | tf_op jit(solution)/shard_map/ppermute | solution.py:24
  8.7 26.7 %all-to-all-start = ((bf16[64,4,512]{2,1,0:T(4,128)(2,1)}), bf16[64,4,512]{2,1,0:T(4,128)(2,1)S(1)}, u32[]{:S(2)}, u32[]{:S(2)}) async-start(bf16[64,4,512]{2,1,0:T(4,128)(2,1)} %bitcast.92), calls=%async_computation | async-start | bytes 524288 | tf_op jit(solution)/shard_map/all_to_all | solution.py:314
  21.9 23.5 %collective-permute-start.4 = (bf16[128,512]{1,0:T(8,128)(2,1)S(1)}, bf16[128,512]{1,0:T(8,128)(2,1)S(1)}, u32[]{:S(2)}, u32[]{:S(2)}) collective-permute-start(bf16[128,512]{1,0:T(8,128)(2,1)S(1)} %copy-done.12), channel_id=1, source_target_pairs={{0,2},{2,0},{1,3},{3,1},{4,6},{6,4},{5,7},{7,5},{8,10},{10,8},{9,1... | collective-permute-start | bytes 393224 | tf_op jit(solution)/shard_map/ppermute | solution.py:24
  24.2 1.4 collective-permute-start.9
  25.6 10.5 %collective-permute-start.10 = (bf16[4,64,256]{2,1,0:T(8,128)(2,1)S(1)}, bf16[4,64,256]{2,1,0:T(8,128)(2,1)S(1)}, u32[]{:S(2)}, u32[]{:S(2)}) collective-permute-start(bf16[4,64,256]{2,1,0:T(8,128)(2,1)S(1)} %get-tuple-element.115), channel_id=1, source_target_pairs={{0,2},{2,0},{1,3},{3,1},{4,6},{6,4},{5,7},{7,5},{8,10},{10,8},{9,1... | collective-permute-start | bytes 393224 | tf_op jit(solution)/shard_map/ppermute | solution.py:24
  35.4 10.0 %collective-permute-start.2 = (bf16[256,512]{1,0:T(8,128)(2,1)S(1)}, bf16[256,512]{1,0:T(8,128)(2,1)S(1)}, u32[]{:S(2)}, u32[]{:S(2)}) collective-permute-start(bf16[256,512]{1,0:T(8,128)(2,1)S(1)} %reshape.121.x_own), channel_id=1, source_target_pairs={{0,1},{1,0},{2,3},{3,2},{4,5},{5,4},{6,7},{7,6},{8,9},{9,8},{10,11... | collective-permute-start | bytes 786440 | tf_op jit(solution)/shard_map/ppermute | solution.py:24
  37.1 25.1 %all-to-all-start.1 = ((bf16[64,4,512]{2,1,0:T(4,128)(2,1)}), bf16[64,4,512]{2,1,0:T(4,128)(2,1)S(1)}, u32[]{:S(2)}, u32[]{:S(2)}) async-start(bf16[64,4,512]{2,1,0:T(4,128)(2,1)} %copy.78), calls=%async_computation.1 | async-start | bytes 524288 | tf_op jit(solution)/shard_map/all_to_all | solution.py:331
  54.1 1.5 collective-permute-start.5
  56.2 5.9 %collective-permute-start.6 = (f32[16,128]{1,0:T(8,128)S(1)}, f32[16,128]{1,0:T(8,128)S(1)}, u32[]{:S(2)}, u32[]{:S(2)}) collective-permute-start(f32[16,128]{1,0:T(8,128)S(1)} %pad_maximum_fusion.2), channel_id=1, source_target_pairs={{0,128},{128,0},{1,129},{129,1},{2,130},{130,2},{3,131},{131,3},{4... | collective-permute-start | bytes 24584 | tf_op jit(solution)/shard_map/ppermute | solution.py:24
  56.9 5.1 %collective-permute-start.7 = (f32[8,128]{1,0:T(8,128)S(1)}, f32[8,128]{1,0:T(8,128)S(1)}, u32[]{:S(2)}, u32[]{:S(2)}) collective-permute-start(f32[8,128]{1,0:T(8,128)S(1)} %add.92), channel_id=1, source_target_pairs={{0,2},{2,0},{1,3},{3,1},{4,6},{6,4},{5,7},{7,5},{8,10},{10,8},{9,1... | collective-permute-start | bytes 12296 | tf_op jit(solution)/shard_map/ppermute | solution.py:24
  58.6 3.6 %collective-permute-start.8 = (f32[8,128]{1,0:T(8,128)S(1)}, f32[8,128]{1,0:T(8,128)S(1)}, u32[]{:S(2)}, u32[]{:S(2)}) collective-permute-start(f32[8,128]{1,0:T(8,128)S(1)} %add.92), channel_id=1, source_target_pairs={{0,130},{2,128},{128,2},{130,0},{1,131},{3,129},{129,3},{131,1},{4... | collective-permute-start | bytes 12296 | tf_op jit(solution)/shard_map/ppermute | solution.py:365
  60.0 13.4 %collective-permute-start.12 = (bf16[256,512]{1,0:T(8,128)(2,1)}, bf16[256,512]{1,0:T(8,128)(2,1)S(1)}, u32[]{:S(2)}, u32[]{:S(2)}) collective-permute-start(bf16[256,512]{1,0:T(8,128)(2,1)} %get-tuple-element.53), channel_id=1, source_target_pairs={{0,1},{1,0},{2,3},{3,2},{4,5},{5,4},{6,7},{7,6},{8,9},{9,8},{10,11... | collective-permute-start | bytes 786440 | tf_op jit(solution)/shard_map/ppermute | solution.py:24
  62.3 21.6 %copy-start.9 = (bf16[256,512]{1,0:T(8,128)(2,1)}, bf16[256,512]{1,0:T(8,128)(2,1)S(1)}, u32[]{:S(2)}) copy-start(bf16[256,512]{1,0:T(8,128)(2,1)S(1)} %reshape.128.cot_own) | copy-start | bytes 786436
  63.1 20.8 %all-to-all-start.2 = ((f32[32,16,128]{2,1,0:T(8,128)}), f32[32,16,128]{2,1,0:T(8,128)S(1)}, u32[]{:S(2)}, u32[]{:S(2)}) async-start(f32[32,16,128]{2,1,0:T(8,128)} %broadcast_in_dim.50), calls=%async_computation.2 | async-start | bytes 524288 | tf_op jit(solution)/shard_map/all_to_all | solution.py:370
  72.6 1.6 collective-permute-start.11
  90.5 17.9 %collective-permute-start.14 = (bf16[512,512]{1,0:T(8,128)(2,1)}, bf16[512,512]{1,0:T(8,128)(2,1)S(1)}, u32[]{:S(2)}, u32[]{:S(2)}) collective-permute-start(bf16[512,512]{1,0:T(8,128)(2,1)} %get-tuple-element.59), channel_id=1, source_target_pairs={{0,2},{2,0},{1,3},{3,1},{4,6},{6,4},{5,7},{7,5},{8,10},{10,8},{9,1... | collective-permute-start | bytes 1572872 | tf_op jit(solution)/shard_map/ppermute | solution.py:24
  100.3 4.1 %collective-permute-start.13 = (bf16[272,512]{1,0:T(8,128)(2,1)}, bf16[272,512]{1,0:T(8,128)(2,1)S(1)}, u32[]{:S(2)}, u32[]{:S(2)}) collective-permute-start(bf16[272,512]{1,0:T(8,128)(2,1)} %get-tuple-element.57), channel_id=1, source_target_pairs={{0,1},{1,0},{2,3},{3,2},{4,5},{5,4},{6,7},{7,6},{8,9},{9,8},{10,11... | collective-permute-start | bytes 835592 | tf_op jit(solution)/shard_map/ppermute | solution.py:24
  101.1 6.7 %collective-permute-start.15 = (f32[16,128]{1,0:T(8,128)S(1)}, f32[16,128]{1,0:T(8,128)S(1)}, u32[]{:S(2)}, u32[]{:S(2)}) collective-permute-start(f32[16,128]{1,0:T(8,128)S(1)} %get-tuple-element.119), channel_id=1, source_target_pairs={{0,2},{2,0},{1,3},{3,1},{4,6},{6,4},{5,7},{7,5},{8,10},{10,8},{9,1... | collective-permute-start | bytes 24584 | tf_op jit(solution)/shard_map/ppermute | solution.py:24
  101.5 6.2 %collective-permute-start.16 = (f32[16,128]{1,0:T(8,128)S(1)}, f32[16,128]{1,0:T(8,128)S(1)}, u32[]{:S(2)}, u32[]{:S(2)}) collective-permute-start(f32[16,128]{1,0:T(8,128)S(1)} %get-tuple-element.118), channel_id=1, source_target_pairs={{0,3},{1,2},{2,1},{3,0},{4,7},{5,6},{6,5},{7,4},{8,11},{9,10},{10,... | collective-permute-start | bytes 24584 | tf_op jit(solution)/shard_map/ppermute | solution.py:415
  148.0 9.1 %collective-permute-start.17 = (bf16[64,4,2,2,128]{4,0,3,2,1:T(8,128)(2,1)S(1)}, bf16[64,4,2,2,128]{4,0,3,2,1:T(8,128)(2,1)S(1)}, u32[]{:S(2)}, u32[]{:S(2)}) collective-permute-start(bf16[64,4,2,2,128]{4,0,3,2,1:T(8,128)(2,1)S(1)} %bitcast.98), channel_id=1, source_target_pairs={{0,2},{2,0},{1,3},{3,1},{4,6},{6,4},{5,7},{7,5},{8,10},{10,8},{9,1... | collective-permute-start | bytes 786440 | tf_op jit(solution)/shard_map/ppermute | solution.py:24
  150.9 25.5 %all-to-all-start.4 = ((bf16[64,4,1152]{2,1,0:T(4,128)(2,1)}), bf16[64,4,1152]{2,1,0:T(4,128)(2,1)S(1)}, u32[]{:S(2)}, u32[]{:S(2)}) async-start(bf16[64,4,1152]{2,1,0:T(4,128)(2,1)} %broadcast_in_dim.51), calls=%async_computation.4 | async-start | bytes 1179648 | tf_op jit(solution)/shard_map/all_to_all | solution.py:423
  157.2 1.6 collective-permute-start.18
  (24 other events, 134.6 us)

commit v3 on v2

--- a/solution.py
+++ b/solution.py
@@ -53,6 +53,18 @@
     return lax.dot_general(a, b, (((ca,), (cb,)), ((), ())), preferred_element_type=f32, **kw)
 
 
+def pieces(values):
+    high = values.astype(bf16).astype(f32)
+    middle = (values - high).astype(bf16).astype(f32)
+    return high, middle, (values - high - middle).astype(bf16).astype(f32)
+
+
+def dot_wide(few, many, ca, cb):
+    rows = few.shape[0]
+    out = dot(jnp.concatenate(pieces(few)).astype(bf16), many, ca, cb)
+    return out[:rows] + (out[rows : 2 * rows] + out[2 * rows :])
+
+
 def per_head(values, first):
     one = jnp.sum(jnp.where(first, values, 0.0), axis=-1, keepdims=True)
     two = jnp.sum(jnp.where(first, 0.0, values), axis=-1, keepdims=True)
@@ -61,7 +73,7 @@
 
 def attention_forward(b, scale, normed, w, ids_row, ids_col, qkv, invs, probs, attended):
     frames, share = qkv.shape[2:]
-    hd = share // 2
+    hd, mid = share // 2, frames // 2
     first = first_lanes(frames, share)
     t = lax.broadcasted_iota(jnp.int32, (frames, frames), 0)
     u = lax.broadcasted_iota(jnp.int32, (frames, frames), 1)
@@ -81,41 +93,36 @@
         query, keys, values = parts
         for k in range(3):
             qkv[p, k] = parts[k]
-        mixed = None
         zero = jnp.zeros_like(keys)
+        mixed = [None, None]
         for h in range(2):
             mask = first if h == 0 else jnp.logical_not(first)
-            dots = dot(query, jnp.where(mask, keys, zero), 1, 1)
-            weights = jnp.where(visible, jnp.exp(dots * (scale[b * 2 + h] * (1.0 / math.sqrt(hd)))), 0.0)
-            prob = weights / jnp.sum(weights, axis=-1, keepdims=True)
-            probs[p, h] = prob
-            one = dot(prob.astype(bf16), jnp.where(mask, values, zero), 1, 0)
-            mixed = one if mixed is None else mixed + one
-        attended[p] = mixed.astype(bf16)
+            keys_h, values_h = jnp.where(mask, keys, zero), jnp.where(mask, values, zero)
+            factor = scale[b * 2 + h] * (1.0 / math.sqrt(hd))
+            for k, (rows, seen) in enumerate(((slice(0, mid), mid), (slice(mid, frames), frames))):
+                dots = dot(query[rows], keys_h[:seen], 1, 1)
+                weights = jnp.where(visible[rows, :seen], jnp.exp(dots * factor), 0.0)
+                prob = weights * (1.0 / jnp.sum(weights, axis=-1, keepdims=True))
+                probs[p, h, rows, :seen] = prob
+                one = dot(prob.astype(bf16), values_h[:seen], 1, 0)
+                mixed[k] = one if mixed[k] is None else mixed[k] + one
+        attended[p] = jnp.concatenate(mixed).astype(bf16)
 
 
 def forward_kernel(
-    scale, x_own, x_other, gain, w_own, w_other, wo_own, wo_other, act, ids_row, ids_col,
-    normed, qkv0, qkv1, invs0, invs1, probs0, probs1, attended0, attended1, enc_part, branch_other, part8,
+    scale, in_own, in_other, gain, w_own, w_other, ids_row, ids_col, act, act_own, act_other,
+    normed, qkv0, qkv1, invs0, invs1, probs0, probs1, attended0, attended1, part8,
 ):
-    frames = x_own.shape[0]
+    frames = in_own.shape[1]
     for p in range(2):
-        x = (x_own, x_other)[p][...].astype(f32)
+        x = frames_of((in_own, in_other)[p]).astype(f32)
         inverse = lax.rsqrt(jnp.mean(x * x, axis=-1, keepdims=True) + EPS)
         normed[p] = (x * inverse * gain[...]).astype(bf16)
     attention_forward(0, scale, normed, w_own, ids_row, ids_col, qkv0, invs0, probs0, attended0)
     attention_forward(1, scale, normed, w_other, ids_row, ids_col, qkv1, invs1, probs1, attended1)
-    x = x_own[...].astype(f32)
-    for p in range(2):
-        branch = dot(attended0[p], wo_own[...], 1, 0) + dot(attended1[p], wo_other[...], 1, 0)
-        if p == 0:
-            enc_part[...] = x + branch
-        else:
-            branch_other[...] = branch.astype(bf16)
-    terms = dot(act[...], x, 1, 1, precision=HIGHEST)
-    for wo, att in ((wo_own, attended0), (wo_other, attended1)):
-        act_out = dot(act[...], wo[...].astype(f32), 1, 1, precision=HIGHEST)
-        terms = terms + dot(act_out, att[0].astype(f32) + att[1].astype(f32), 1, 1, precision=HIGHEST)
+    terms = dot_wide(act[...], frames_of(in_own), 1, 1)
+    for act_out, att in ((act_own, attended0), (act_other, attended1)):
+        terms = terms + (dot_wide(act_out[...], att[0], 1, 1) + dot_wide(act_out[...], att[1], 1, 1))
     terms = terms * (1.0 / 256.0)
     moved = pltpu.roll(terms, frames - LAG, 1)
     moved = jnp.where(lax.broadcasted_iota(jnp.int32, moved.shape, 1) < frames - LAG, moved, 0.0)
@@ -125,8 +132,8 @@
 
 
 def attention_back(b, scale, up, wo, qkv, invs, probs, gp, first):
-    share = wo.shape[0]
-    hd = share // 2
+    share, frames = wo.shape[0], up.shape[1]
+    hd, mid = share // 2, frames // 2
     sums = [None, None]
     factor = jnp.where(
         first[:1], scale[b * 2] * (1.0 / math.sqrt(hd)), scale[b * 2 + 1] * (1.0 / math.sqrt(hd))
@@ -135,19 +142,26 @@
         query, keys, values = qkv[p, 0], qkv[p, 1], qkv[p, 2]
         zero = jnp.zeros_like(keys)
         grad_att = dot(up[p], wo[...], 1, 1).astype(bf16)
-        grad_q = grad_k = grad_v = None
+        grad_q, low, high = [None, None], [None, None], [None, None]
+
+        def add(old, new):
+            return new if old is None else old + new
+
         for h in range(2):
             mask = first if h == 0 else jnp.logical_not(first)
-            grad_probs = dot(grad_att, jnp.where(mask, values, zero), 1, 1)
-            prob = probs[p, h]
-            inner = jnp.sum(grad_probs * prob, axis=-1, keepdims=True)
-            grad_scores = (prob * (grad_probs - inner)).astype(bf16)
-            one = dot(grad_scores, jnp.where(mask, keys, zero), 1, 0)
-            grad_q = one if grad_q is None else grad_q + one
-            one = dot(grad_scores, jnp.where(mask, query, zero), 0, 0)
-            grad_k = one if grad_k is None else grad_k + one
-            one = dot(prob.astype(bf16), jnp.where(mask, grad_att, zero), 0, 0)
-            grad_v = one if grad_v is None else grad_v + one
+            query_h, keys_h = jnp.where(mask, query, zero), jnp.where(mask, keys, zero)
+            values_h, grad_h = jnp.where(mask, values, zero), jnp.where(mask, grad_att, zero)
+            for k, (rows, seen) in enumerate(((slice(0, mid), mid), (slice(mid, frames), frames))):
+                grad_probs = dot(grad_att[rows], values_h[:seen], 1, 1)
+                prob = probs[p, h, rows, :seen]
+                inner = jnp.sum(grad_probs * prob, axis=-1, keepdims=True)
+                grad_scores = (prob * (grad_probs - inner)).astype(bf16)
+                grad_q[k] = add(grad_q[k], dot(grad_scores, keys_h[:seen], 1, 0))
+                target = (low, high)[k]
+                target[0] = add(target[0], dot(grad_scores, query_h[rows], 0, 0))
+                target[1] = add(target[1], dot(prob.astype(bf16), grad_h[rows], 0, 0))
+        grad_q = jnp.concatenate(grad_q)
+        grad_k, grad_v = (jnp.concatenate([low[j] + high[j][:mid], high[j][mid:]]) for j in range(2))
         for k in range(2):
             grad, base = ((grad_q, query), (grad_k, keys))[k]
             base = base.astype(f32)
@@ -172,13 +186,18 @@
     target[:, split:] = out_part.astype(target.dtype)
 
 
+def frames_of(home):
+    half = home.shape[2] // 2
+    return jnp.concatenate([home[0, :, :half], home[1, :, :half]], axis=1)
+
+
 def first_lanes(frames, share):
     return lax.broadcasted_iota(jnp.int32, (frames, share), 1) < share // 2
 
 
 def other_kernel(
-    scale, place, packed, cot_own, cot_other, act, wo, qkv, invs, probs, attended, normed,
-    bounded_out, eight_out, up, gp, grads, scale_row,
+    scale, packed, in_own, in_other, act, wo_own, wo, qkv, invs, probs, attended0, attended, normed,
+    bounded_out, act_part, up, gp, grads, scale_row,
     pooled,
 ):
     frames, width = up.shape[1:]
@@ -194,33 +213,39 @@
     moved = pltpu.roll(grad_latent, LAG, 1)
     moved = jnp.where(lax.broadcasted_iota(jnp.int32, shape, 1) >= LAG, moved, 0.0)
     eight = jnp.concatenate([grad_latent, moved], axis=0)
-    eight_out[...] = eight
-    pooled[...] = dot(eight.T, act[...], 1, 0, precision=HIGHEST) * (1.0 / 256.0)
-    xh, core = place[0], place[1]
+    left, right = pieces(eight), pieces(act[...])
+    pairs = ((0, 0), (0, 1), (1, 0), (1, 1), (0, 2), (2, 0))
+    lefts = jnp.concatenate([left[i] for i, _ in pairs]).T.astype(bf16)
+    rights = jnp.concatenate([right[j] for _, j in pairs]).astype(bf16)
+    pooled[...] = dot(lefts, rights, 1, 0) * (1.0 / 256.0)
+    half = width // 2
     for p in range(2):
-        core_p = core if p == 0 else 1 - core
-        for r in range(4):
-            block_r = (xh if r < 2 else 1 - xh) * 2 + (core_p if r % 2 == 0 else 1 - core_p)
-            cols = pl.ds(pl.multiple_of(block_r * share, share), share)
-            cot = (cot_own, cot_other)[p][:, r * share : (r + 1) * share].astype(f32)
+        for r in range(2):
+            cols = slice(r * half, (r + 1) * half)
+            cot = (in_own, in_other)[p][r, :, half:].astype(f32)
             up[p, :, cols] = (cot + pooled[:, cols]).astype(bf16)
     scale_row[...] = attention_back(1, scale, up, wo, qkv, invs, probs, gp, first_lanes(frames, share))
     weight_grads(grads, normed, gp, up, attended)
+    part = dot_wide(eight, frames_of(in_own), 1, 0)
+    for att, w in ((attended0, wo_own), (attended, wo)):
+        mixed = dot_wide(eight, att[0], 1, 0) + dot_wide(eight, att[1], 1, 0)
+        part = part + dot_wide(mixed, w[...], 1, 0)
+    act_part[...] = part
 
 
 def own_kernel(
-    scale, place, eight, up, wo, w_own, w_other, qkv, invs, probs, attended, normed, x_own, x_other,
-    encoded, gp_other, scale_other,
-    grads, small, normed_own, normed_other,
+    scale, place, act_part, up, wo, qkv, invs, probs, attended, normed, w_own, w_other, in_own, in_other,
+    gp_other, scale_other, attended1, wo_other,
+    grads, small, normed_own, normed_other, enc_part,
     gp,
 ):
-    frames, width = x_own.shape
+    frames, width = up.shape[1:]
     share = wo.shape[0]
     scale_own = attention_back(0, scale, up, wo, qkv, invs, probs, gp, first_lanes(frames, share))
     gain_part = None
     for p in (1, 0):
         grad = dot(gp[p], w_own[...], 1, 1) + dot(gp_other[p], w_other[...], 1, 1)
-        x = (x_own, x_other)[p][...].astype(f32)
+        x = frames_of((in_own, in_other)[p]).astype(f32)
         inverse = lax.rsqrt(jnp.mean(x * x, axis=-1, keepdims=True) + EPS)
         one = jnp.sum(grad * (x * inverse), axis=0, keepdims=True)
         gain_part = one if gain_part is None else gain_part + one
@@ -229,7 +254,12 @@
         else:
             normed_other[:frames] = grad.astype(bf16)
     weight_grads(grads, normed, gp, up, attended)
-    act_part = dot(eight[...], encoded[...].astype(f32), 1, 0, precision=HIGHEST)
+    for p in range(2):
+        branch = dot(attended[p], wo[...], 1, 0) + dot(attended1[p], wo_other[...], 1, 0)
+        if p == 0:
+            enc_part[...] = frames_of(in_own).astype(f32) + branch
+        else:
+            normed_other[frames + 16 :] = branch.astype(bf16)
     xh, core = place[0], place[1]
     none = jnp.zeros((1, share), f32)
     for r in range(4):
@@ -242,23 +272,23 @@
             return jnp.where(second, high, low)
 
         tail = (scale_own, none, scale_other[...], none)[r]
-        rows = jnp.concatenate([block(act_part), block(gain_part), tail, jnp.zeros((6, share), f32)])
+        rows = jnp.concatenate([block(act_part[...]), block(gain_part), tail, jnp.zeros((6, share), f32)])
         if r == 1:
-            normed_other[frames:, :share] = rows.astype(bf16)
+            normed_other[frames : frames + 16, :share] = rows.astype(bf16)
         else:
             small[r] = rows
     small[1] = jnp.zeros((16, share), f32)
-    normed_other[frames:, share:] = jnp.zeros((16, width - share), bf16)
-
-
-def finish_kernel(x_own, gain, grad_own, grad_got, up, encoded, out):
-    x = x_own[...].astype(f32)
+    normed_other[frames : frames + 16, share:] = jnp.zeros((16, width - share), bf16)
+
+
+def finish_kernel(in_own, gain, grad_own, grad_got, up, enc_part, out):
+    x = frames_of(in_own).astype(f32)
     frames, width = x.shape
     inverse = lax.rsqrt(jnp.mean(x * x, axis=-1, keepdims=True) + EPS)
     scaled = gain[...] * (grad_own[...] + grad_got[:frames].astype(f32))
     row_dot = jnp.mean(scaled * x, axis=-1, keepdims=True)
     grad = inverse * scaled - x * (inverse * inverse * inverse * row_dot)
-    out[:, :width] = encoded[...]
+    out[:, :width] = (enc_part[...] + grad_got[frames + 16 :].astype(f32)).astype(bf16)
     out[:, width : 2 * width] = (up[0].astype(f32) + grad).astype(bf16)
 
 
@@ -309,35 +339,33 @@
     few_got = swap(few, "core")
     few = ordered(few, few_got, core, 0)
 
-    sent = lax.dynamic_slice_in_dim(frames_in, block * group, group, 1).transpose(1, 0, 2)
-    sent = after(sent, few_got)
-    x_own = lax.all_to_all(sent, TM, 0, 0, tiled=True)
-    x_own = x_own.reshape(frames, width)
-    x_other = swap(x_own, "core")
+    cot = cotangent.reshape(fl, 2, 2, group, share)
+    cot = ordered(pick(cot, core, 2), swap(pick(cot, 1 - core, 2), "core"), core, 3)
+    sent = pick(frames_in.reshape(fl, 2, 2, group, width), core, 2)
+    sent = lax.dynamic_slice_in_dim(sent, xh * 2 * share, 2 * share, 3)
+    sent = jnp.concatenate([sent, cot.reshape(fl, 2, group, 2 * share)], axis=-1)
+    sent = sent.transpose(1, 2, 0, 3).reshape(2 * n_tm, fl, width)
+    in_own = lax.all_to_all(sent, ("xh",) + TM, 0, 0, tiled=True).reshape(2, frames, width)
+    in_other = swap(in_own, "core")
 
     w_own = w_qkv.reshape(width, 3 * share)
     w_other = swap(w_own, "xh")
-    wo_other = swap(after(w_out, few_got), "xh")
+    wo_other = swap(after(w_out, w_other), "xh")
     place = jnp.stack([xh, core]).astype(jnp.int32)
     few_other = swap(few, "xh")
     act = ordered(few, few_other, xh, 0).reshape(4, 16, share)[:, :8]
     act = act.transpose(1, 0, 2).reshape(8, width)
+    act_own = dot(act, w_out.astype(f32), 1, 1, precision=HIGHEST)
+    act_other = swap(act_own, "xh")
     scale = jnp.concatenate([qk_scale, pick(few_other, core, 0)[8, :2]])
-
-    cot = after(cotangent, few_got).reshape(fl, 2, 2, group, share)
-    cot = jnp.concatenate([pick(cot, core, 2), swap(pick(cot, 1 - core, 2), "core")], axis=-1)
-    cot = jnp.concatenate([pick(cot, xh, 1), swap(pick(cot, 1 - xh, 1), "xh")], axis=-1)
-    cot = after(cot.transpose(1, 0, 2), x_own)
-    cot_own = lax.all_to_all(cot, TM, 0, 0, tiled=True).reshape(frames, width)
-    cot_other = swap(cot_own, "core")
 
     ids_row, ids_col = episode_ids[None], episode_ids[:, None]
     (
-        normed, qkv0, qkv1, invs0, invs1, probs0, probs1, attended0, attended1, enc_part, branch_other, part8
+        normed, qkv0, qkv1, invs0, invs1, probs0, probs1, attended0, attended1, part8
     ) = call(
         forward_kernel,
         (scale,),
-        (x_own, x_other, gain, w_own, w_other, w_out, wo_other, act, ids_row, ids_col),
+        (in_own, in_other, gain, w_own, w_other, ids_row, ids_col, act, act_own, act_other),
         (
             ((2, frames, width), bf16),
             ((2, 3, frames, share), bf16),
@@ -348,8 +376,6 @@
             ((2, 2, frames, frames), f32),
             ((2, frames, share), bf16),
             ((2, frames, share), bf16),
-            ((frames, width), f32),
-            ((frames, width), bf16),
             ((8, frames // 2), f32),
         ),
         FORWARD_FLOPS,
@@ -366,18 +392,17 @@
     far = jnp.concatenate([from_xh + from_both, jnp.zeros_like(ac8)])
     packed = (packed + from_xl) + far
     packed = jnp.broadcast_to(packed[None], (n_yz, 16, frames // 2))
-    packed = after(packed, cot_own)
     packed = lax.all_to_all(packed, YZ, 0, 0, tiled=True)
 
-    encoded_own = (enc_part + swap(branch_other, "core").astype(f32)).astype(bf16)
-
-    bounded, eight, up, gp_other, grads_other, scale_other = call(
+    bounded, act_part, up, gp_other, grads_other, scale_other = call(
         other_kernel,
-        (scale, place),
-        (packed, cot_own, cot_other, act, wo_other, qkv1, invs1, probs1, attended1, normed),
+        (scale,),
+        (
+            packed, in_own, in_other, act, w_out, wo_other, qkv1, invs1, probs1, attended0, attended1, normed,
+        ),
         (
             ((4, frames), f32),
-            ((8, frames), f32),
+            ((8, width), f32),
             ((2, frames, width), bf16),
             ((2, frames, 3 * share), bf16),
             ((width, 4 * share), bf16),
@@ -387,18 +412,19 @@
         scratch=[pltpu.VMEM((frames, width), f32)],
     )
     grads_got = swap(grads_other, "xh")
-    grads_own, small, normed_own, normed_other = call(
+    grads_own, small, normed_own, normed_other, enc_part = call(
         own_kernel,
         (scale, place),
         (
-            eight, up, w_out, w_own, w_other, qkv0, invs0, probs0, attended0, normed, x_own, x_other,
-            encoded_own, gp_other, scale_other,
+            act_part, up, w_out, qkv0, invs0, probs0, attended0, normed, w_own, w_other, in_own, in_other,
+            gp_other, scale_other, attended1, wo_other,
         ),
         (
             ((width, 4 * share), f32),
             ((4, 16, share), f32),
             ((frames, width), f32),
-            ((frames + 16, width), bf16),
+            ((2 * frames + 16, width), bf16),
+            ((frames, width), f32),
         ),
         BACKWARD_FLOPS,
         scratch=[pltpu.VMEM((2, frames, 3 * share), bf16)],
@@ -408,20 +434,20 @@
     (both_out,) = call(
         finish_kernel,
         (),
-        (x_own, gain, normed_own, normed_got, up, encoded_own),
+        (in_own, gain, normed_own, normed_got, up, enc_part),
         (((frames, 2 * width), bf16),),
         10 * frames * width,
     )
     far = lax.ppermute(small[3], ("xh", "core"), [(0, 3), (1, 2), (2, 1), (3, 0)])
-    small = (small[0] + normed_got[frames:, :share].astype(f32)) + (swap(small[2], "xh") + far)
+    small = (small[0] + normed_got[frames : frames + 16, :share].astype(f32)) + (swap(small[2], "xh") + far)
     small = jnp.pad(small.astype(bf16), ((0, frames - 16), (0, 0)))
     grads = (grads_own + grads_got.astype(f32)).astype(bf16)
     both_out = jnp.concatenate([both_out, grads[:frames], grads[frames:], small], axis=1)
     home = lax.all_to_all(both_out.reshape(n_tm, fl, 4 * width + share), TM, 0, 0, tiled=True)
     summed = jnp.sum(home[:, :, 2 * width :].astype(f32), axis=0).astype(bf16)
-    summed = jnp.broadcast_to(summed[None], (n_tm, *summed.shape))
-    summed = lax.all_to_all(summed, TM, 0, 0, tiled=True).reshape(frames, 2 * width + share)
-    home = home[:, :, : 2 * width]
+    copies = jnp.broadcast_to(summed[None], (n_tm, *summed.shape))
+    summed = lax.all_to_all(copies, TM, 0, 0, tiled=True).reshape(frames, 2 * width + share)
+    home = after(home[:, :, : 2 * width], copies)
     home = home.reshape(group, fl, 2, 2, 2, share)
     got = swap(pick(home, 1 - xh, 3), "xh")
     home = ordered(pick(home, xh, 3), got, xh, 0)

time: 181 us -> 178 us (0.983)
  blocking collectives: 37.3 us -> 0 us
  waiting for transfers between devices: 38.2 us -> 71.9 us
    all_to_all x1 -> x0, blocking collectives: 37.3 us -> none  [local(): lax.all_to_all(both_out.reshape(n_tm, fl, 4 * width + share), TM, 0, 0, t...]
    all_to_all x3, waiting for transfers between devices: 24.1 us -> 55.1 us  [the longest x1 31.2 us: local(): lax.all_to_all(both_out.reshape(n_tm, fl, 4 * width + share), TM, 0, 0, t...]
    ppermute x17 -> x15, waiting for transfers between devices: 4.26 us -> 12 us  [swap(): return lax.ppermute(value, axis, [(0, 1), (1, 0)])]
    all_to_all x1, starting transfers between devices: 9.57 us -> 4.05 us  [local(): packed = lax.all_to_all(packed, YZ, 0, 0, tiled=True)]
    all_to_all x1, waiting for transfers between devices: 9.64 us -> 4.93 us  [local(): packed = lax.all_to_all(packed, YZ, 0, 0, tiled=True)]
    ppermute x17 -> x15, starting transfers between devices: 15.3 us -> 19.5 us  [swap(): return lax.ppermute(value, axis, [(0, 1), (1, 0)])]
    unnamed x55 -> x48, local copies, waits for them, and re-layouts: 8.3 us -> 6.2 us
  transfers between devices with their start and end apart: 23 -> 21, of which waited for: 9 -> 11; matrix products, arithmetic and copies ran while one was open for 8% -> 7% of each run, Pallas kernels for 9% -> 6%
where the time goes in v3:
time: 178 us; the launch traced here: 177 us
  waiting for transfers between devices  71.9 us (40%)
  starting transfers between devices  55.2 us (31%)
  Pallas kernels  22.6 us (13%)
  local copies, waits for them, and re-layouts  17 us (10%)
  other arithmetic  8.61 us (5%)
    all_to_all x1, waiting for transfers between devices, local(): lax.all_to_all(both_out.reshape(n_tm, fl, 4 * width + share), TM, 0, 0, t...  31.2 us
    pallas_call x4, Pallas kernels, call(): pl.pallas_call(kernel, out_shape=[jax.ShapeDtypeStruct(s, d) for s, d in...  22.6 us
    ppermute x15, starting transfers between devices, swap(): return lax.ppermute(value, axis, [(0, 1), (1, 0)])  19.5 us
    all_to_all x1, starting transfers between devices, local(): lax.all_to_all(sent, ('xh',) + TM, 0, 0, tiled=True)  14.5 us
    all_to_all x1, waiting for transfers between devices, local(): lax.all_to_all(copies, TM, 0, 0, tiled=True)  14.1 us
    ppermute x15, waiting for transfers between devices, swap(): return lax.ppermute(value, axis, [(0, 1), (1, 0)])  12 us
    all_to_all x1, waiting for transfers between devices, local(): lax.all_to_all(sent, ('xh',) + TM, 0, 0, tiled=True)  9.82 us
    all_to_all x1, starting transfers between devices, local(): lax.all_to_all(both_out.reshape(n_tm, fl, 4 * width + share), TM, 0, 0, t...  6.85 us
  transfers between devices with their start and end apart: 21, of which 11 were waited for; matrix products, arithmetic and copies ran while one was open for 7% of the time, Pallas kernels for 6%

profile of v3, /device:TPU:2, one launch (start us, length us, event | category | flops | bytes accessed | tf_op | source)
XLA Modules:
  0.0 176.7 jit_solution(5542636663976501056)
XLA Ops:
  4.4 2.2 %collective-permute-start.4 = (bf16[512,384]{1,0:T(8,128)(2,1)S(1)}, bf16[512,384]{1,0:T(8,128)(2,1)S(1)}, u32[]{:S(2)}, u32[]{:S(2)}) collective-permute-start(bf16[512,384]{1,0:T(8,128)(2,1)S(1)} %copy.85.w_own), channel_id=1, source_target_pairs={{0,2},{2,0},{1,3},{3,1},{4,6},{6,4},{5,7},{7,5},{8,10},{10,8},{9,1... | collective-permute-start | bytes 1179656 | tf_op jit(solution)/shard_map/ppermute | solution.py:24
  8.4 14.5 %all-to-all-start = ((bf16[128,4,512]{2,1,0:T(4,128)(2,1)}), bf16[128,4,512]{2,1,0:T(4,128)(2,1)S(1)}, u32[]{:S(2)}, u32[]{:S(2)}) async-start(bf16[128,4,512]{2,1,0:T(4,128)(2,1)} %copy.82), calls=%async_computation | async-start | bytes 1048576 | tf_op jit(solution)/shard_map/all_to_all | solution.py:348
  23.0 2.6 %collective-permute-start.2 = (f32[2,16,128]{2,1,0:T(8,128)S(1)}, f32[2,16,128]{2,1,0:T(8,128)S(1)}, u32[]{:S(2)}, u32[]{:S(2)}) collective-permute-start(f32[2,16,128]{2,1,0:T(8,128)S(1)} %pad_maximum_fusion.2), channel_id=1, source_target_pairs={{0,2},{2,0},{1,3},{3,1},{4,6},{6,4},{5,7},{7,5},{8,10},{10,8},{9,1... | collective-permute-start | bytes 49160 | tf_op jit(solution)/shard_map/ppermute | solution.py:24
  26.4 2.1 %collective-permute-done.2 = f32[2,16,128]{2,1,0:T(8,128)S(1)} collective-permute-done((f32[2,16,128]{2,1,0:T(8,128)S(1)}, f32[2,16,128]{2,1,0:T(8,128)S(1)}, u32[]{:S(2)}, u32[]{:S(2)}) %collective-permute-start.2) | collective-permute-done | bytes 16416 | tf_op jit(solution)/shard_map/ppermute | solution.py:24
  28.7 2.5 %collective-permute-start.5 = (f32[8,128]{1,0:T(8,128)S(1)}, f32[8,128]{1,0:T(8,128)S(1)}, u32[]{:S(2)}, u32[]{:S(2)}) collective-permute-start(f32[8,128]{1,0:T(8,128)S(1)} %fusion.21.act_own), channel_id=1, source_target_pairs={{0,2},{2,0},{1,3},{3,1},{4,6},{6,4},{5,7},{7,5},{8,10},{10,8},{9,1... | collective-permute-start | bytes 12296 | tf_op jit(solution)/shard_map/ppermute | solution.py:24
  31.2 9.8 %all-to-all-done = bf16[128,4,512]{2,1,0:T(4,128)(2,1)S(1)} async-done(((bf16[128,4,512]{2,1,0:T(4,128)(2,1)}), bf16[128,4,512]{2,1,0:T(4,128)(2,1)S(1)}, u32[]{:S(2)}, u32[]{:S(2)}) %all-to-all-start) | async-done | bytes 524320 | tf_op jit(solution)/shard_map/all_to_all | solution.py:348
  44.0 5.5 %shard_map.188 = (bf16[2,256,512]{2,1,0:T(8,128)(2,1)}, bf16[2,3,256,128]{3,2,1,0:T(8,128)(2,1)}, bf16[2,3,256,128]{3,2,1,0:T(8,128)(2,1)}, f32[2,256,4]{2,1,0:T...) custom-call(f32[4]{0:T(128)} %pad_maximum_fusion.4.scale, ...), custom_call_target="tpu_custom_call" | custom-call | flops 1000 | bytes 1 | tf_op jit(solution)/shard_map/pallas_call | solution.py:300
  51.6 3.4 %collective-permute-start.7 = (f32[16,128]{1,0:T(8,128)S(1)}, f32[16,128]{1,0:T(8,128)S(1)}, u32[]{:S(2)}, u32[]{:S(2)}) collective-permute-start(f32[16,128]{1,0:T(8,128)S(1)} %pad_maximum_fusion.3), channel_id=1, source_target_pairs={{0,128},{128,0},{1,129},{129,1},{2,130},{130,2},{3,131},{131,3},{4... | collective-permute-start | bytes 24584 | tf_op jit(solution)/shard_map/ppermute | solution.py:24
  55.0 1.6 collective-permute-start.9
  56.6 3.5 %collective-permute-done.8 = f32[8,128]{1,0:T(8,128)S(1)} collective-permute-done((f32[8,128]{1,0:T(8,128)S(1)}, f32[8,128]{1,0:T(8,128)S(1)}, u32[]{:S(2)}, u32[]{:S(2)}) %collective-permute-start.8) | collective-permute-done | bytes 4128 | tf_op jit(solution)/shard_map/ppermute | solution.py:24
  60.9 4.1 %all-to-all-start.1 = ((f32[32,16,128]{2,1,0:T(8,128)}), f32[32,16,128]{2,1,0:T(8,128)S(1)}, u32[]{:S(2)}, u32[]{:S(2)}) async-start(f32[32,16,128]{2,1,0:T(8,128)} %broadcast_in_dim.50), calls=%async_computation.1 | async-start | bytes 524288 | tf_op jit(solution)/shard_map/all_to_all | solution.py:395
  65.0 3.3 %collective-permute-start.10 = (bf16[128,512]{1,0:T(8,128)(2,1)S(1)}, bf16[128,512]{1,0:T(8,128)(2,1)S(1)}, u32[]{:S(2)}, u32[]{:S(2)}) collective-permute-start(bf16[128,512]{1,0:T(8,128)(2,1)S(1)} %copy-done.8), channel_id=1, source_target_pairs={{0,2},{2,0},{1,3},{3,1},{4,6},{6,4},{5,7},{7,5},{8,10},{10,8},{9,1... | collective-permute-start | bytes 393224 | tf_op jit(solution)/shard_map/ppermute | solution.py:24
  68.9 2.6 %collective-permute-done.10.wo.wo_other = bf16[128,512]{1,0:T(8,128)(2,1)S(1)} collective-permute-done((bf16[128,512]{1,0:T(8,128)(2,1)S(1)}, bf16[128,512]{1,0:T(8,128)(2,1)S(1)}, u32[]{:S(2)}, u32[]{:S(2)}) %collective-permute-start.10) | collective-permute-done | bytes 131104 | tf_op jit(solution)/shard_map/ppermute | solution.py:24
  71.5 4.9 %all-to-all-done.1.packed = f32[32,16,128]{2,1,0:T(8,128)S(1)} async-done(((f32[32,16,128]{2,1,0:T(8,128)}), f32[32,16,128]{2,1,0:T(8,128)S(1)}, u32[]{:S(2)}, u32[]{:S(2)}) %all-to-all-start.1) | async-done | bytes 262176 | tf_op jit(solution)/shard_map/all_to_all | solution.py:395
  77.2 6.7 %shard_map.189 = (f32[4,256]{1,0:T(4,128)}, f32[8,512]{1,0:T(8,128)}, bf16[2,256,512]{2,1,0:T(8,128)(2,1)}, bf16[2,256,384]{2,1,0:T(8,128)(2,1)}, bf16[512,512]{1,0:T(8,128)(2,1)}, /*index=5*/f32[1,128]{1,0:T(1,128)}) custom-call(f32[4]{0:T(128)} %pad_maximum_fusion.4.scale, f32[32,16,128]{2,1,0:T(8,128)} %copy-done.6, bf16[2,256,512]{2,1,0:T(8,128)(2,1)} %copy-done.1, ...), custom_call_target="tpu_custom_call" | custom-call | flops 5000000000 | bytes 5000000 | tf_op jit(solution)/shard_map/pallas_call | solution.py:300
  83.8 3.0 %collective-permute-start.12 = (bf16[512,512]{1,0:T(8,128)(2,1)}, bf16[512,512]{1,0:T(8,128)(2,1)S(1)}, u32[]{:S(2)}, u32[]{:S(2)}) collective-permute-start(bf16[512,512]{1,0:T(8,128)(2,1)} %get-tuple-element.50), channel_id=1, source_target_pairs={{0,2},{2,0},{1,3},{3,1},{4,6},{6,4},{5,7},{7,5},{8,10},{10,8},{9,1... | collective-permute-start | bytes 1572872 | tf_op jit(solution)/shard_map/ppermute | solution.py:24
  86.9 7.6 %shard_map.190 = (f32[512,512]{1,0:T(8,128)}, f32[4,16,128]{2,1,0:T(8,128)}, f32[256,512]{1,0:T(8,128)}, bf16[528,512]{1,0:T(8,128)(2,1)}, f32[256,512]{1,0:T(8,128)}) custom-call(f32[4]{0:T(128)} %pad_maximum_fusion.4.scale, s32[2]{0:T(128)} %pad_add_fusion.1.place, f32[8,512]{1,0:T(8,128)} %get-tuple-element.39.act_part, ...), custom_call_target="tpu_custom_call" | custom-call | flops 5000000000 | bytes 5000000 | tf_op jit(solution)/shard_map/pallas_call | solution.py:300
  95.7 2.8 %collective-permute-start.14 = (f32[16,128]{1,0:T(8,128)S(1)}, f32[16,128]{1,0:T(8,128)S(1)}, u32[]{:S(2)}, u32[]{:S(2)}) collective-permute-start(f32[16,128]{1,0:T(8,128)S(1)} %get-tuple-element.108), channel_id=1, source_target_pairs={{0,3},{1,2},{2,1},{3,0},{4,7},{5,6},{6,5},{7,4},{8,11},{9,10},{10,... | collective-permute-start | bytes 24584 | tf_op jit(solution)/shard_map/ppermute | solution.py:441
  98.5 1.4 add_convert_fusion
  100.8 2.8 %shard_map.191 = bf16[256,1024]{1,0:T(8,128)(2,1)} custom-call(bf16[2,256,512]{2,1,0:T(8,128)(2,1)} %copy-done.1, f32[1,512]{1,0:T(1,128)} %bitcast.124, f32[256,512]{1,0:T(8,128)} %get-tuple-element.46.grad_own, bf16[528,512]{1,0:T(8,128)(2,1)} %copy-done.3, bf16[2,256,512]{2,1,0:T(8,128)(2,1)} %get-tuple-element.40.up, f32[256,512]{1,0:T(8,128)} %get-tuple-element.48.enc_part), custom_call_target="tpu_custom_call" | custom-call | flops 1310720 | bytes 1310 | tf_op jit(solution)/shard_map/pallas_call | solution.py:300
  106.7 6.8 %all-to-all-start.2 = ((bf16[64,4,2176]{2,1,0:T(4,128)(2,1)}), bf16[64,4,2176]{2,1,0:T(4,128)(2,1)S(1)}, u32[]{:S(2)}, u32[]{:S(2)}) async-start(bf16[64,4,2176]{2,1,0:T(4,128)(2,1)} %reshape.138), calls=%async_computation.2 | async-start | bytes 2228224 | tf_op jit(solution)/shard_map/all_to_all | solution.py:446
  113.5 31.2 %all-to-all-done.2 = bf16[64,4,2176]{2,1,0:T(4,128)(2,1)S(1)} async-done(((bf16[64,4,2176]{2,1,0:T(4,128)(2,1)}), bf16[64,4,2176]{2,1,0:T(4,128)(2,1)S(1)}, u32[]{:S(2)}, u32[]{:S(2)}) %all-to-all-start.2) | async-done | bytes 1114144 | tf_op jit(solution)/shard_map/all_to_all | solution.py:446
  147.7 5.9 %all-to-all-start.3 = ((bf16[64,4,1152]{2,1,0:T(4,128)(2,1)}), bf16[64,4,1152]{2,1,0:T(4,128)(2,1)S(1)}, u32[]{:S(2)}, u32[]{:S(2)}) async-start(bf16[64,4,1152]{2,1,0:T(4,128)(2,1)} %broadcast_in_dim.51), calls=%async_computation.3 | async-start | bytes 1179648 | tf_op jit(solution)/shard_map/all_to_all | solution.py:449
  158.3 14.1 %all-to-all-done.3 = bf16[64,4,1152]{2,1,0:T(4,128)(2,1)S(1)} async-done(((bf16[64,4,1152]{2,1,0:T(4,128)(2,1)}), bf16[64,4,1152]{2,1,0:T(4,128)(2,1)S(1)}, u32[]{:S(2)}, u32[]{:S(2)}) %all-to-all-start.3) | async-done | bytes 589856 | tf_op jit(solution)/shard_map/all_to_all | solution.py:449
  (132 shorter events, 30.5 us)
Async XLA Ops:
  1.7 5.3 %collective-permute-start = (bf16[4,2,64,128]{3,2,1,0:T(8,128)(2,1)S(1)}, bf16[4,2,64,128]{3,2,1,0:T(8,128)(2,1)S(1)}, u32[]{:S(2)}, u32[]{:S(2)}) collective-permute-start(bf16[4,2,64,128]{3,2,1,0:T(8,128)(2,1)S(1)} %dynamic-slice_bitcast_fusion.1), channel_id=1, source_target_pairs={{0,1},{1,0},{2,3},{3,2},{4,5},{5,4},{6,7},{7,6},{8,9},{9,8},{10,11... | collective-permute-start | bytes 393224 | tf_op jit(solution)/shard_map/ppermute | solution.py:24
  2.5 20.5 %collective-permute-start.1 = (f32[16,128]{1,0:T(8,128)S(1)}, f32[16,128]{1,0:T(8,128)S(1)}, u32[]{:S(2)}, u32[]{:S(2)}) collective-permute-start(f32[16,128]{1,0:T(8,128)S(1)} %select_maximum_fusion), channel_id=1, source_target_pairs={{0,1},{1,0},{2,3},{3,2},{4,5},{5,4},{6,7},{7,6},{8,9},{9,8},{10,11... | collective-permute-start | bytes 24584 | tf_op jit(solution)/shard_map/ppermute | solution.py:24
  4.4 38.2 %collective-permute-start.4 = (bf16[512,384]{1,0:T(8,128)(2,1)S(1)}, bf16[512,384]{1,0:T(8,128)(2,1)S(1)}, u32[]{:S(2)}, u32[]{:S(2)}) collective-permute-start(bf16[512,384]{1,0:T(8,128)(2,1)S(1)} %copy.85.w_own), channel_id=1, source_target_pairs={{0,2},{2,0},{1,3},{3,1},{4,6},{6,4},{5,7},{7,5},{8,10},{10,8},{9,1... | collective-permute-start | bytes 1179656 | tf_op jit(solution)/shard_map/ppermute | solution.py:24
  7.1 15.8 %copy-start.10 = (f32[2,128,4]{1,2,0:T(4,128)S(1)}, f32[2,128,4]{1,2,0:T(4,128)}, u32[]{:S(2)}) copy-start(f32[2,128,4]{1,2,0:T(4,128)} %param.18) | copy-start | bytes 12292
  7.2 18.4 %copy-start.11 = (s32[256]{0:T(256)S(1)}, s32[256]{0:T(256)}, u32[]{:S(2)}) copy-start(s32[256]{0:T(256)} %param.20) | copy-start | bytes 3076
  7.2 21.4 %copy-start.8 = (bf16[128,512]{1,0:T(8,128)(2,1)S(1)}, bf16[128,512]{1,0:T(8,128)(2,1)}, u32[]{:S(2)}) copy-start(bf16[128,512]{1,0:T(8,128)(2,1)} %wo.1) | copy-start | bytes 393220
  8.4 32.6 %all-to-all-start = ((bf16[128,4,512]{2,1,0:T(4,128)(2,1)}), bf16[128,4,512]{2,1,0:T(4,128)(2,1)S(1)}, u32[]{:S(2)}, u32[]{:S(2)}) async-start(bf16[128,4,512]{2,1,0:T(4,128)(2,1)} %copy.82), calls=%async_computation | async-start | bytes 1048576 | tf_op jit(solution)/shard_map/all_to_all | solution.py:348
  23.0 5.5 %collective-permute-start.2 = (f32[2,16,128]{2,1,0:T(8,128)S(1)}, f32[2,16,128]{2,1,0:T(8,128)S(1)}, u32[]{:S(2)}, u32[]{:S(2)}) collective-permute-start(f32[2,16,128]{2,1,0:T(8,128)S(1)} %pad_maximum_fusion.2), channel_id=1, source_target_pairs={{0,2},{2,0},{1,3},{3,1},{4,6},{6,4},{5,7},{7,5},{8,10},{10,8},{9,1... | collective-permute-start | bytes 49160 | tf_op jit(solution)/shard_map/ppermute | solution.py:24
  28.7 13.9 %collective-permute-start.5 = (f32[8,128]{1,0:T(8,128)S(1)}, f32[8,128]{1,0:T(8,128)S(1)}, u32[]{:S(2)}, u32[]{:S(2)}) collective-permute-start(f32[8,128]{1,0:T(8,128)S(1)} %fusion.21.act_own), channel_id=1, source_target_pairs={{0,2},{2,0},{1,3},{3,1},{4,6},{6,4},{5,7},{7,5},{8,10},{10,8},{9,1... | collective-permute-start | bytes 12296 | tf_op jit(solution)/shard_map/ppermute | solution.py:24
  41.2 2.0 %collective-permute-start.3 = (bf16[2,256,512]{2,1,0:T(8,128)(2,1)S(1)}, bf16[2,256,512]{2,1,0:T(8,128)(2,1)S(1)}, u32[]{:S(2)}, u32[]{:S(2)}) collective-permute-start(bf16[2,256,512]{2,1,0:T(8,128)(2,1)S(1)} %reshape.131.in_own), channel_id=1, source_target_pairs={{0,1},{1,0},{2,3},{3,2},{4,5},{5,4},{6,7},{7,6},{8,9},{9,8},{10,11... | collective-permute-start | bytes 1572872 | tf_op jit(solution)/shard_map/ppermute | solution.py:24
  49.5 1.5 collective-permute-start.6
  51.6 8.5 %collective-permute-start.7 = (f32[16,128]{1,0:T(8,128)S(1)}, f32[16,128]{1,0:T(8,128)S(1)}, u32[]{:S(2)}, u32[]{:S(2)}) collective-permute-start(f32[16,128]{1,0:T(8,128)S(1)} %pad_maximum_fusion.3), channel_id=1, source_target_pairs={{0,128},{128,0},{1,129},{129,1},{2,130},{130,2},{3,131},{131,3},{4... | collective-permute-start | bytes 24584 | tf_op jit(solution)/shard_map/ppermute | solution.py:24
  55.0 5.1 %collective-permute-start.8 = (f32[8,128]{1,0:T(8,128)S(1)}, f32[8,128]{1,0:T(8,128)S(1)}, u32[]{:S(2)}, u32[]{:S(2)}) collective-permute-start(f32[8,128]{1,0:T(8,128)S(1)} %add.90), channel_id=1, source_target_pairs={{0,2},{2,0},{1,3},{3,1},{4,6},{6,4},{5,7},{7,5},{8,10},{10,8},{9,1... | collective-permute-start | bytes 12296 | tf_op jit(solution)/shard_map/ppermute | solution.py:24
  55.0 5.1 %collective-permute-start.9 = (f32[8,128]{1,0:T(8,128)S(1)}, f32[8,128]{1,0:T(8,128)S(1)}, u32[]{:S(2)}, u32[]{:S(2)}) collective-permute-start(f32[8,128]{1,0:T(8,128)S(1)} %add.90), channel_id=1, source_target_pairs={{0,130},{2,128},{128,2},{130,0},{1,131},{3,129},{129,3},{131,1},{4... | collective-permute-start | bytes 12296 | tf_op jit(solution)/shard_map/ppermute | solution.py:391
  60.9 15.5 %all-to-all-start.1 = ((f32[32,16,128]{2,1,0:T(8,128)}), f32[32,16,128]{2,1,0:T(8,128)S(1)}, u32[]{:S(2)}, u32[]{:S(2)}) async-start(f32[32,16,128]{2,1,0:T(8,128)} %broadcast_in_dim.50), calls=%async_computation.1 | async-start | bytes 524288 | tf_op jit(solution)/shard_map/all_to_all | solution.py:395
  65.0 6.6 %collective-permute-start.10 = (bf16[128,512]{1,0:T(8,128)(2,1)S(1)}, bf16[128,512]{1,0:T(8,128)(2,1)S(1)}, u32[]{:S(2)}, u32[]{:S(2)}) collective-permute-start(bf16[128,512]{1,0:T(8,128)(2,1)S(1)} %copy-done.8), channel_id=1, source_target_pairs={{0,2},{2,0},{1,3},{3,1},{4,6},{6,4},{5,7},{7,5},{8,10},{10,8},{9,1... | collective-permute-start | bytes 393224 | tf_op jit(solution)/shard_map/ppermute | solution.py:24
  83.8 14.7 %collective-permute-start.12 = (bf16[512,512]{1,0:T(8,128)(2,1)}, bf16[512,512]{1,0:T(8,128)(2,1)S(1)}, u32[]{:S(2)}, u32[]{:S(2)}) collective-permute-start(bf16[512,512]{1,0:T(8,128)(2,1)} %get-tuple-element.50), channel_id=1, source_target_pairs={{0,2},{2,0},{1,3},{3,1},{4,6},{6,4},{5,7},{7,5},{8,10},{10,8},{9,1... | collective-permute-start | bytes 1572872 | tf_op jit(solution)/shard_map/ppermute | solution.py:24
  94.5 5.5 %collective-permute-start.11 = (bf16[528,512]{1,0:T(8,128)(2,1)}, bf16[528,512]{1,0:T(8,128)(2,1)S(1)}, u32[]{:S(2)}, u32[]{:S(2)}) collective-permute-start(bf16[528,512]{1,0:T(8,128)(2,1)} %get-tuple-element.47), channel_id=1, source_target_pairs={{0,1},{1,0},{2,3},{3,2},{4,5},{5,4},{6,7},{7,6},{8,9},{9,8},{10,11... | collective-permute-start | bytes 1622024 | tf_op jit(solution)/shard_map/ppermute | solution.py:24
  95.2 8.4 %collective-permute-start.13 = (f32[16,128]{1,0:T(8,128)S(1)}, f32[16,128]{1,0:T(8,128)S(1)}, u32[]{:S(2)}, u32[]{:S(2)}) collective-permute-start(f32[16,128]{1,0:T(8,128)S(1)} %get-tuple-element.109), channel_id=1, source_target_pairs={{0,2},{2,0},{1,3},{3,1},{4,6},{6,4},{5,7},{7,5},{8,10},{10,8},{9,1... | collective-permute-start | bytes 24584 | tf_op jit(solution)/shard_map/ppermute | solution.py:24
  95.7 7.9 %collective-permute-start.14 = (f32[16,128]{1,0:T(8,128)S(1)}, f32[16,128]{1,0:T(8,128)S(1)}, u32[]{:S(2)}, u32[]{:S(2)}) collective-permute-start(f32[16,128]{1,0:T(8,128)S(1)} %get-tuple-element.108), channel_id=1, source_target_pairs={{0,3},{1,2},{2,1},{3,0},{4,7},{5,6},{6,5},{7,4},{8,11},{9,10},{10,... | collective-permute-start | bytes 24584 | tf_op jit(solution)/shard_map/ppermute | solution.py:441
  106.7 38.0 %all-to-all-start.2 = ((bf16[64,4,2176]{2,1,0:T(4,128)(2,1)}), bf16[64,4,2176]{2,1,0:T(4,128)(2,1)S(1)}, u32[]{:S(2)}, u32[]{:S(2)}) async-start(bf16[64,4,2176]{2,1,0:T(4,128)(2,1)} %reshape.138), calls=%async_computation.2 | async-start | bytes 2228224 | tf_op jit(solution)/shard_map/all_to_all | solution.py:446
  146.8 8.2 %collective-permute-start.15 = (bf16[64,4,2,2,128]{4,0,3,2,1:T(8,128)(2,1)S(1)}, bf16[64,4,2,2,128]{4,0,3,2,1:T(8,128)(2,1)S(1)}, u32[]{:S(2)}, u32[]{:S(2)}) collective-permute-start(bf16[64,4,2,2,128]{4,0,3,2,1:T(8,128)(2,1)S(1)} %bitcast.116), channel_id=1, source_target_pairs={{0,2},{2,0},{1,3},{3,1},{4,6},{6,4},{5,7},{7,5},{8,10},{10,8},{9,1... | collective-permute-start | bytes 786440 | tf_op jit(solution)/shard_map/ppermute | solution.py:24
  147.7 24.7 %all-to-all-start.3 = ((bf16[64,4,1152]{2,1,0:T(4,128)(2,1)}), bf16[64,4,1152]{2,1,0:T(4,128)(2,1)S(1)}, u32[]{:S(2)}, u32[]{:S(2)}) async-start(bf16[64,4,1152]{2,1,0:T(4,128)(2,1)} %broadcast_in_dim.51), calls=%async_computation.3 | async-start | bytes 1179648 | tf_op jit(solution)/shard_map/all_to_all | solution.py:449
  155.1 1.6 collective-permute-start.16
  (19 other events, 70.2 us)

commit v4 on v3

--- a/solution.py
+++ b/solution.py
@@ -178,12 +178,21 @@
     return jnp.where(lane == 0, sums[0], 0.0) + jnp.where(lane == 1, sums[1], 0.0)
 
 
-def weight_grads(target, normed, gp, up, attended):
+def prepare_kernel(normed, attended0, attended1, normed_t, attended0_t, attended1_t):
+    for p in range(2):
+        normed_t[p] = normed[p].T
+        attended0_t[p] = attended0[p].T
+        attended1_t[p] = attended1[p].T
+
+
+def weight_grads(target, normed_t, gp, up, attended_t):
     split = gp.shape[2]
-    qkv_part = dot(normed[0], gp[0], 0, 0) + dot(normed[1], gp[1], 0, 0)
-    out_part = dot(up[0], attended[0], 0, 0) + dot(up[1], attended[1], 0, 0)
-    target[:, :split] = qkv_part.astype(target.dtype)
-    target[:, split:] = out_part.astype(target.dtype)
+    half, share = normed_t.shape[1] // 2, attended_t.shape[1]
+    qkv_part = dot(normed_t[0], gp[0], 1, 0) + dot(normed_t[1], gp[1], 1, 0)
+    out_part = dot(attended_t[0], up[0], 1, 0) + dot(attended_t[1], up[1], 1, 0)
+    for k in range(2):
+        target[:, k * split : (k + 1) * split] = qkv_part[k * half : (k + 1) * half].astype(target.dtype)
+        target[k * share : (k + 1) * share, 2 * split :] = out_part[:, k * half : (k + 1) * half].astype(target.dtype)
 
 
 def frames_of(home):
@@ -196,7 +205,7 @@
 
 
 def other_kernel(
-    scale, packed, in_own, in_other, act, wo_own, wo, qkv, invs, probs, attended0, attended, normed,
+    scale, packed, in_own, in_other, act, wo_own, wo, qkv, invs, probs, attended0, attended, normed_t, attended_t,
     bounded_out, act_part, up, gp, grads, scale_row,
     pooled,
 ):
@@ -225,7 +234,7 @@
             cot = (in_own, in_other)[p][r, :, half:].astype(f32)
             up[p, :, cols] = (cot + pooled[:, cols]).astype(bf16)
     scale_row[...] = attention_back(1, scale, up, wo, qkv, invs, probs, gp, first_lanes(frames, share))
-    weight_grads(grads, normed, gp, up, attended)
+    weight_grads(grads, normed_t, gp, up, attended_t)
     part = dot_wide(eight, frames_of(in_own), 1, 0)
     for att, w in ((attended0, wo_own), (attended, wo)):
         mixed = dot_wide(eight, att[0], 1, 0) + dot_wide(eight, att[1], 1, 0)
@@ -234,9 +243,9 @@
 
 
 def own_kernel(
-    scale, place, act_part, up, wo, qkv, invs, probs, attended, normed, w_own, w_other, in_own, in_other,
+    scale, place, act_part, up, wo, qkv, invs, probs, attended, normed_t, attended_t, w_own, w_other, in_own, in_other,
     gp_other, scale_other, attended1, wo_other,
-    grads, small, normed_own, normed_other, enc_part,
+    grads, small, small2, small3, normed_own, normed_other, enc_part,
     gp,
 ):
     frames, width = up.shape[1:]
@@ -253,7 +262,7 @@
             normed_own[...] = grad
         else:
             normed_other[:frames] = grad.astype(bf16)
-    weight_grads(grads, normed, gp, up, attended)
+    weight_grads(grads, normed_t, gp, up, attended_t)
     for p in range(2):
         branch = dot(attended[p], wo[...], 1, 0) + dot(attended1[p], wo_other[...], 1, 0)
         if p == 0:
@@ -276,8 +285,7 @@
         if r == 1:
             normed_other[frames : frames + 16, :share] = rows.astype(bf16)
         else:
-            small[r] = rows
-    small[1] = jnp.zeros((16, share), f32)
+            (small, None, small2, small3)[r][...] = rows
     normed_other[frames : frames + 16, share:] = jnp.zeros((16, width - share), bf16)
 
 
@@ -390,38 +398,47 @@
     from_xl = swap(packed, "xl")
     from_both = lax.ppermute(part8, ("xl", "xh"), [(0, 3), (1, 2), (2, 1), (3, 0)])
     far = jnp.concatenate([from_xh + from_both, jnp.zeros_like(ac8)])
-    packed = (packed + from_xl) + far
-    packed = jnp.broadcast_to(packed[None], (n_yz, 16, frames // 2))
+    sums = (packed + from_xl) + far
+    packed = jnp.broadcast_to(sums[None], (n_yz, 16, frames // 2))
     packed = lax.all_to_all(packed, YZ, 0, 0, tiled=True)
 
+    normed_t, attended0_t, attended1_t = call(
+        prepare_kernel,
+        (),
+        (after(normed, sums), attended0, attended1),
+        (((2, width, frames), bf16), ((2, share, frames), bf16), ((2, share, frames), bf16)),
+        FORWARD_FLOPS,
+    )
     bounded, act_part, up, gp_other, grads_other, scale_other = call(
         other_kernel,
         (scale,),
         (
-            packed, in_own, in_other, act, w_out, wo_other, qkv1, invs1, probs1, attended0, attended1, normed,
+            packed, in_own, in_other, act, w_out, wo_other, qkv1, invs1, probs1, attended0, attended1, normed_t, attended1_t,
         ),
         (
             ((4, frames), f32),
             ((8, width), f32),
             ((2, frames, width), bf16),
             ((2, frames, 3 * share), bf16),
-            ((width, 4 * share), bf16),
+            ((width // 2, 2 * width), bf16),
             ((1, share), f32),
         ),
         BACKWARD_FLOPS,
         scratch=[pltpu.VMEM((frames, width), f32)],
     )
     grads_got = swap(grads_other, "xh")
-    grads_own, small, normed_own, normed_other, enc_part = call(
+    grads_own, small, small2, small3, normed_own, normed_other, enc_part = call(
         own_kernel,
         (scale, place),
         (
-            act_part, up, w_out, qkv0, invs0, probs0, attended0, normed, w_own, w_other, in_own, in_other,
+            act_part, up, w_out, qkv0, invs0, probs0, attended0, normed_t, attended0_t, w_own, w_other, in_own, in_other,
             gp_other, scale_other, attended1, wo_other,
         ),
         (
-            ((width, 4 * share), f32),
-            ((4, 16, share), f32),
+            ((width // 2, 2 * width), f32),
+            ((16, share), f32),
+            ((16, share), f32),
+            ((16, share), f32),
             ((frames, width), f32),
             ((2 * frames + 16, width), bf16),
             ((frames, width), f32),
@@ -438,21 +455,26 @@
         (((frames, 2 * width), bf16),),
         10 * frames * width,
     )
-    far = lax.ppermute(small[3], ("xh", "core"), [(0, 3), (1, 2), (2, 1), (3, 0)])
-    small = (small[0] + normed_got[frames : frames + 16, :share].astype(f32)) + (swap(small[2], "xh") + far)
+    far = lax.ppermute(small3, ("xh", "core"), [(0, 3), (1, 2), (2, 1), (3, 0)])
+    small = (small + normed_got[frames : frames + 16, :share].astype(f32)) + (swap(small2, "xh") + far)
     small = jnp.pad(small.astype(bf16), ((0, frames - 16), (0, 0)))
     grads = (grads_own + grads_got.astype(f32)).astype(bf16)
-    both_out = jnp.concatenate([both_out, grads[:frames], grads[frames:], small], axis=1)
+    both_out = jnp.concatenate([both_out, grads, small], axis=1)
     home = lax.all_to_all(both_out.reshape(n_tm, fl, 4 * width + share), TM, 0, 0, tiled=True)
     summed = jnp.sum(home[:, :, 2 * width :].astype(f32), axis=0).astype(bf16)
     copies = jnp.broadcast_to(summed[None], (n_tm, *summed.shape))
     summed = lax.all_to_all(copies, TM, 0, 0, tiled=True).reshape(frames, 2 * width + share)
     home = after(home[:, :, : 2 * width], copies)
     home = home.reshape(group, fl, 2, 2, 2, share)
-    got = swap(pick(home, 1 - xh, 3), "xh")
-    home = ordered(pick(home, xh, 3), got, xh, 0)
-    got = swap(pick(home, 1 - core, 4), "core")
-    home = ordered(pick(home, core, 4), got, core, 1)
+
+    def block_of(x_index, core_index):
+        return pick(pick(home, x_index, 3), core_index, 3)
+
+    from_core = swap(block_of(xh, 1 - core), "core")
+    from_xh = swap(block_of(1 - xh, core), "xh")
+    from_both = lax.ppermute(block_of(1 - xh, 1 - core), ("xh", "core"), [(0, 3), (1, 2), (2, 1), (3, 0)])
+    near = ordered(block_of(xh, core), from_core, core, 0)
+    home = ordered(near, ordered(from_xh, from_both, core, 0), xh, 0)
     home = home.transpose(4, 3, 0, 1, 2, 5).reshape(2, fl, patches, share)
     encoded, grad_frames = home[0], home[1]
 
@@ -463,10 +485,11 @@
     bounded_own = lax.dynamic_slice_in_dim(bounded, tm * fl, fl, 1)
     quant_gap = ((digits.astype(f32) - widths) / widths - bounded_own).T
 
-    both = jnp.concatenate([summed[:, :width], summed[:, width : 2 * width]]).astype(f32)
     norm_factor = 1.0 / math.sqrt(tokens)
-    grad_qkv = both[:, : 3 * share].reshape(width, 3, share) * norm_factor
-    grad_out = both[:, 3 * share : 4 * share].T * norm_factor
+    qkv_halves = jnp.concatenate([summed[:, : 3 * share], summed[:, 3 * share : 6 * share]])
+    grad_qkv = qkv_halves.astype(f32).reshape(width, 3, share) * norm_factor
+    out_halves = [summed[k * share : (k + 1) * share, 6 * share : 2 * width] for k in range(2)]
+    grad_out = jnp.concatenate(out_halves, axis=1).astype(f32) * norm_factor
     small = summed[:16, 2 * width :].astype(f32)
     grad_act = small[:8].reshape(2, 4, share).transpose(0, 2, 1) * (1.0 / math.sqrt(frames) / patches)
     grad_gain = small[8] * norm_factor

time: 178 us -> 175 us (0.983)
  waiting for transfers between devices: 71.9 us -> 65.9 us
  starting transfers between devices: 55.2 us -> 57.8 us
  Pallas kernels: 22.6 us -> 24.7 us
    all_to_all x1, waiting for transfers between devices: 14.1 us -> 3.44 us  [local(): lax.all_to_all(copies, TM, 0, 0, tiled=True)]
    ppermute x1 -> x2, starting transfers between devices: 2.83 us -> 5.87 us  [the longest x1 3.1 us: local(): lax.ppermute(block_of(1 - xh, 1 - core), ('xh', 'core'), [(0, 3), (1, 2),...]
    ppermute x1 -> x2, waiting for transfers between devices: 0.01 us -> 2.41 us  [the longest x1 2.41 us: local(): lax.ppermute(block_of(1 - xh, 1 - core), ('xh', 'core'), [(0, 3), (1, 2),...]
    ppermute x15, waiting for transfers between devices: 12 us -> 14.1 us  [swap(): return lax.ppermute(value, axis, [(0, 1), (1, 0)])]
    pallas_call x4 -> x5, Pallas kernels: 22.6 us -> 24.7 us  [call(): pl.pallas_call(kernel, out_shape=[jax.ShapeDtypeStruct(s, d) for s, d in...]
    unnamed x48 -> x49, local copies, waits for them, and re-layouts: 6.2 us -> 5.37 us
  transfers between devices with their start and end apart: 21 -> 22, of which waited for: 11 -> 11; matrix products, arithmetic and copies ran while one was open for 7% -> 7% of each run, Pallas kernels for 6% -> 7%
where the time goes in v4:
time: 175 us
  waiting for transfers between devices  65.9 us (38%)
  starting transfers between devices  57.8 us (33%)
  Pallas kernels  24.7 us (14%)
  local copies, waits for them, and re-layouts  15.6 us (9%)
  other arithmetic  9.14 us (5%)
    all_to_all x1, waiting for transfers between devices, local(): lax.all_to_all(both_out.reshape(n_tm, fl, 4 * width + share), TM, 0, 0, t...  31.1 us
    pallas_call x5, Pallas kernels, call(): pl.pallas_call(kernel, out_shape=[jax.ShapeDtypeStruct(s, d) for s, d in...  24.7 us
    ppermute x15, starting transfers between devices, swap(): return lax.ppermute(value, axis, [(0, 1), (1, 0)])  19.1 us
    all_to_all x1, starting transfers between devices, local(): lax.all_to_all(sent, ('xh',) + TM, 0, 0, tiled=True)  14.5 us
    ppermute x15, waiting for transfers between devices, swap(): return lax.ppermute(value, axis, [(0, 1), (1, 0)])  14.1 us
    all_to_all x1, waiting for transfers between devices, local(): lax.all_to_all(sent, ('xh',) + TM, 0, 0, tiled=True)  9.82 us
    all_to_all x1, starting transfers between devices, local(): lax.all_to_all(both_out.reshape(n_tm, fl, 4 * width + share), TM, 0, 0, t...  6.98 us
    all_to_all x1, starting transfers between devices, local(): lax.all_to_all(copies, TM, 0, 0, tiled=True)  5.7 us
  transfers between devices with their start and end apart: 22, of which 11 were waited for; matrix products, arithmetic and copies ran while one was open for 7% of the time, Pallas kernels for 7%

profile of v4, /device:TPU:2, one launch (start us, length us, event | category | flops | bytes accessed | tf_op | source)
XLA Modules:
  0.0 174.5 jit_solution(16873971551468375193)
XLA Ops:
  4.4 2.2 %collective-permute-start.4 = (bf16[512,384]{1,0:T(8,128)(2,1)S(1)}, bf16[512,384]{1,0:T(8,128)(2,1)S(1)}, u32[]{:S(2)}, u32[]{:S(2)}) collective-permute-start(bf16[512,384]{1,0:T(8,128)(2,1)S(1)} %copy.61.w_own), channel_id=1, source_target_pairs={{0,2},{2,0},{1,3},{3,1},{4,6},{6,4},{5,7},{7,5},{8,10},{10,8},{9,1... | collective-permute-start | bytes 1179656 | tf_op jit(solution)/shard_map/ppermute | solution.py:24
  8.4 14.5 %all-to-all-start = ((bf16[128,4,512]{2,1,0:T(4,128)(2,1)}), bf16[128,4,512]{2,1,0:T(4,128)(2,1)S(1)}, u32[]{:S(2)}, u32[]{:S(2)}) async-start(bf16[128,4,512]{2,1,0:T(4,128)(2,1)} %copy.58), calls=%async_computation | async-start | bytes 1048576 | tf_op jit(solution)/shard_map/all_to_all | solution.py:356
  23.0 2.6 %collective-permute-start.2 = (f32[2,16,128]{2,1,0:T(8,128)S(1)}, f32[2,16,128]{2,1,0:T(8,128)S(1)}, u32[]{:S(2)}, u32[]{:S(2)}) collective-permute-start(f32[2,16,128]{2,1,0:T(8,128)S(1)} %pad_maximum_fusion.4), channel_id=1, source_target_pairs={{0,2},{2,0},{1,3},{3,1},{4,6},{6,4},{5,7},{7,5},{8,10},{10,8},{9,1... | collective-permute-start | bytes 49160 | tf_op jit(solution)/shard_map/ppermute | solution.py:24
  28.7 2.5 %collective-permute-start.5 = (f32[8,128]{1,0:T(8,128)S(1)}, f32[8,128]{1,0:T(8,128)S(1)}, u32[]{:S(2)}, u32[]{:S(2)}) collective-permute-start(f32[8,128]{1,0:T(8,128)S(1)} %fusion.16.act_own), channel_id=1, source_target_pairs={{0,2},{2,0},{1,3},{3,1},{4,6},{6,4},{5,7},{7,5},{8,10},{10,8},{9,1... | collective-permute-start | bytes 12296 | tf_op jit(solution)/shard_map/ppermute | solution.py:24
  31.2 9.8 %all-to-all-done = bf16[128,4,512]{2,1,0:T(4,128)(2,1)S(1)} async-done(((bf16[128,4,512]{2,1,0:T(4,128)(2,1)}), bf16[128,4,512]{2,1,0:T(4,128)(2,1)S(1)}, u32[]{:S(2)}, u32[]{:S(2)}) %all-to-all-start) | async-done | bytes 524320 | tf_op jit(solution)/shard_map/all_to_all | solution.py:356
  44.0 5.5 %shard_map.188 = (bf16[2,256,512]{2,1,0:T(8,128)(2,1)}, bf16[2,3,256,128]{3,2,1,0:T(8,128)(2,1)}, bf16[2,3,256,128]{3,2,1,0:T(8,128)(2,1)}, f32[2,256,4]{2,1,0:T...) custom-call(f32[4]{0:T(128)} %pad_maximum_fusion.6.scale, ...), custom_call_target="tpu_custom_call" | custom-call | flops 1000 | bytes 1 | tf_op jit(solution)/shard_map/pallas_call | solution.py:308
  51.6 3.4 %collective-permute-start.7 = (f32[16,128]{1,0:T(8,128)S(1)}, f32[16,128]{1,0:T(8,128)S(1)}, u32[]{:S(2)}, u32[]{:S(2)}) collective-permute-start(f32[16,128]{1,0:T(8,128)S(1)} %pad_maximum_fusion.5), channel_id=1, source_target_pairs={{0,128},{128,0},{1,129},{129,1},{2,130},{130,2},{3,131},{131,3},{4... | collective-permute-start | bytes 24584 | tf_op jit(solution)/shard_map/ppermute | solution.py:24
  56.6 3.5 %collective-permute-done.8 = f32[8,128]{1,0:T(8,128)S(1)} collective-permute-done((f32[8,128]{1,0:T(8,128)S(1)}, f32[8,128]{1,0:T(8,128)S(1)}, u32[]{:S(2)}, u32[]{:S(2)}) %collective-permute-start.8) | collective-permute-done | bytes 4128 | tf_op jit(solution)/shard_map/ppermute | solution.py:24
  60.9 4.0 %all-to-all-start.1 = ((f32[32,16,128]{2,1,0:T(8,128)}), f32[32,16,128]{2,1,0:T(8,128)S(1)}, u32[]{:S(2)}, u32[]{:S(2)}) async-start(f32[32,16,128]{2,1,0:T(8,128)} %broadcast_in_dim.50), calls=%async_computation.1 | async-start | bytes 524288 | tf_op jit(solution)/shard_map/all_to_all | solution.py:403
  64.9 3.3 %collective-permute-start.10 = (bf16[128,512]{1,0:T(8,128)(2,1)S(1)}, bf16[128,512]{1,0:T(8,128)(2,1)S(1)}, u32[]{:S(2)}, u32[]{:S(2)}) collective-permute-start(bf16[128,512]{1,0:T(8,128)(2,1)S(1)} %copy-done.8), channel_id=1, source_target_pairs={{0,2},{2,0},{1,3},{3,1},{4,6},{6,4},{5,7},{7,5},{8,10},{10,8},{9,1... | collective-permute-start | bytes 393224 | tf_op jit(solution)/shard_map/ppermute | solution.py:24
  68.9 2.3 %shard_map.189 = (bf16[2,512,256]{2,1,0:T(8,128)(2,1)}, bf16[2,128,256]{2,1,0:T(8,128)(2,1)}, bf16[2,128,256]{2,1,0:T(8,128)(2,1)}) custom-call(bf16[2,256,512]{2,1,0:T(8,128)(2,1)} %get-tuple-element.45.normed, bf16[2,256,128]{2,1,0:T(8,128)(2,1)} %get-tuple-element.42.attended0.attended, bf16[2,256,128]{2,1,0:T(8,128)(2,1)} %get-tuple-element.43.attended1.attended), custom_call_target="tpu_custom_call" | custom-call | flops 1000 | bytes 1 | tf_op jit(solution)/shard_map/pallas_call | solution.py:308
  71.5 4.9 %all-to-all-done.1.packed = f32[32,16,128]{2,1,0:T(8,128)S(1)} async-done(((f32[32,16,128]{2,1,0:T(8,128)}), f32[32,16,128]{2,1,0:T(8,128)S(1)}, u32[]{:S(2)}, u32[]{:S(2)}) %all-to-all-start.1) | async-done | bytes 262176 | tf_op jit(solution)/shard_map/all_to_all | solution.py:403
  77.1 6.7 %shard_map.190 = (f32[4,256]{1,0:T(4,128)}, f32[8,512]{1,0:T(8,128)}, bf16[2,256,512]{2,1,0:T(8,128)(2,1)}, bf16[2,256,384]{2,1,0:T(8,128)(2,1)}, bf16[256,1024]{1,0:T(8,128)(2,1)}, /*index=5*/f32[1,128]{1,0:T(1,128)}) custom-call(f32[4]{0:T(128)} %pad_maximum_fusion.6.scale, f32[32,16,128]{2,1,0:T(8,128)} %copy-done.6, bf16[2,256,512]{2,1,0:T(8,128)(2,1)} %copy-done.1, ...), custom_call_target="tpu_custom_call" | custom-call | flops 5000000000 | bytes 5000000 | tf_op jit(solution)/shard_map/pallas_call | solution.py:308
  83.8 3.1 %collective-permute-start.12 = (bf16[256,1024]{1,0:T(8,128)(2,1)}, bf16[256,1024]{1,0:T(8,128)(2,1)S(1)}, u32[]{:S(2)}, u32[]{:S(2)}) collective-permute-start(bf16[256,1024]{1,0:T(8,128)(2,1)} %get-tuple-element.60), channel_id=1, source_target_pairs={{0,2},{2,0},{1,3},{3,1},{4,6},{6,4},{5,7},{7,5},{8,10},{10,8},{9,1... | collective-permute-start | bytes 1572872 | tf_op jit(solution)/shard_map/ppermute | solution.py:24
  86.9 7.4 %shard_map.191 = (f32[256,1024]{1,0:T(8,128)}, f32[16,128]{1,0:T(8,128)}, f32[16,128]{1,0:T(8,128)}, f32[16,128]{1,0:T(8,128)}, f32[256,512]{1,0:T(8,128)}, /*in...) custom-call(f32[4]{0:T(128)} %pad_maximum_fusion.6.scale, s32[2]{0:T(128)} %pad_add_fusion.1.place, ...), custom_call_target="tpu_custom_call" | custom-call | flops 5000000000 | bytes 5000000 | tf_op jit(solution)/shard_map/pallas_call | solution.py:308
  95.0 2.8 %collective-permute-start.14 = (f32[16,128]{1,0:T(8,128)}, f32[16,128]{1,0:T(8,128)S(1)}, u32[]{:S(2)}, u32[]{:S(2)}) collective-permute-start(f32[16,128]{1,0:T(8,128)} %get-tuple-element.63), channel_id=1, source_target_pairs={{0,3},{1,2},{2,1},{3,0},{4,7},{5,6},{6,5},{7,4},{8,11},{9,10},{10,... | collective-permute-start | bytes 24584 | tf_op jit(solution)/shard_map/ppermute | solution.py:458
  99.9 2.8 %shard_map.192 = bf16[256,1024]{1,0:T(8,128)(2,1)} custom-call(bf16[2,256,512]{2,1,0:T(8,128)(2,1)} %copy-done.1, f32[1,512]{1,0:T(1,128)} %bitcast.121, f32[256,512]{1,0:T(8,128)} %get-tuple-element.56.grad_own, bf16[528,512]{1,0:T(8,128)(2,1)} %copy-done.3, bf16[2,256,512]{2,1,0:T(8,128)(2,1)} %get-tuple-element.49.up, f32[256,512]{1,0:T(8,128)} %get-tuple-element.58.enc_part), custom_call_target="tpu_custom_call" | custom-call | flops 1310720 | bytes 1310 | tf_op jit(solution)/shard_map/pallas_call | solution.py:308
  105.8 7.0 %all-to-all-start.2 = ((bf16[64,4,2176]{2,1,0:T(4,128)(2,1)}), bf16[64,4,2176]{2,1,0:T(4,128)(2,1)S(1)}, u32[]{:S(2)}, u32[]{:S(2)}) async-start(bf16[64,4,2176]{2,1,0:T(4,128)(2,1)} %reshape.264), calls=%async_computation.2 | async-start | bytes 2228224 | tf_op jit(solution)/shard_map/all_to_all | solution.py:463
  112.8 31.1 %all-to-all-done.2 = bf16[64,4,2176]{2,1,0:T(4,128)(2,1)S(1)} async-done(((bf16[64,4,2176]{2,1,0:T(4,128)(2,1)}), bf16[64,4,2176]{2,1,0:T(4,128)(2,1)S(1)}, u32[]{:S(2)}, u32[]{:S(2)}) %all-to-all-start.2) | async-done | bytes 1114144 | tf_op jit(solution)/shard_map/all_to_all | solution.py:463
  145.2 5.7 %all-to-all-start.3 = ((bf16[64,4,1152]{2,1,0:T(4,128)(2,1)}), bf16[64,4,1152]{2,1,0:T(4,128)(2,1)S(1)}, u32[]{:S(2)}, u32[]{:S(2)}) async-start(bf16[64,4,1152]{2,1,0:T(4,128)(2,1)} %broadcast_in_dim.51), calls=%async_computation.3 | async-start | bytes 1179648 | tf_op jit(solution)/shard_map/all_to_all | solution.py:466
  154.2 3.1 %collective-permute-start.17 = (bf16[64,4,2,128]{3,0,1,2:T(8,128)(2,1)S(1)}, bf16[64,4,2,128]{3,0,1,2:T(8,128)(2,1)S(1)}, u32[]{:S(2)}, u32[]{:S(2)}) collective-permute-start(bf16[64,4,2,128]{3,0,1,2:T(8,128)(2,1)S(1)} %bitcast.115), channel_id=1, source_target_pairs={{0,3},{1,2},{2,1},{3,0},{4,7},{5,6},{6,5},{7,4},{8,11},{9,10},{10,... | collective-permute-start | bytes 393224 | tf_op jit(solution)/shard_map/ppermute | solution.py:475
  157.4 6.2 %collective-permute-done.16 = bf16[64,4,2,128]{3,0,1,2:T(8,128)(2,1)S(1)} collective-permute-done((bf16[64,4,2,128]{3,0,1,2:T(8,128)(2,1)S(1)}, bf16[64,4,2,128]{3,0,1,2:T(8,128)(2,1)S(1)}, u32[]{:S(2)}, u32[]{:S(2)}) %collective-permute-start.16) | collective-permute-done | bytes 131104 | tf_op jit(solution)/shard_map/ppermute | solution.py:24
  163.6 2.4 %collective-permute-done.17 = bf16[64,4,2,128]{3,0,1,2:T(8,128)(2,1)S(1)} collective-permute-done((bf16[64,4,2,128]{3,0,1,2:T(8,128)(2,1)S(1)}, bf16[64,4,2,128]{3,0,1,2:T(8,128)(2,1)S(1)}, u32[]{:S(2)}, u32[]{:S(2)}) %collective-permute-start.17) | collective-permute-done | bytes 131104 | tf_op jit(solution)/shard_map/ppermute | solution.py:475
  167.0 3.4 %all-to-all-done.3 = bf16[64,4,1152]{2,1,0:T(4,128)(2,1)S(1)} async-done(((bf16[64,4,1152]{2,1,0:T(4,128)(2,1)}), bf16[64,4,1152]{2,1,0:T(4,128)(2,1)S(1)}, u32[]{:S(2)}, u32[]{:S(2)}) %all-to-all-start.3) | async-done | bytes 589856 | tf_op jit(solution)/shard_map/all_to_all | solution.py:466
  (135 shorter events, 32.8 us)
Async XLA Ops:
  1.7 5.3 %collective-permute-start = (bf16[4,2,64,128]{3,2,1,0:T(8,128)(2,1)S(1)}, bf16[4,2,64,128]{3,2,1,0:T(8,128)(2,1)S(1)}, u32[]{:S(2)}, u32[]{:S(2)}) collective-permute-start(bf16[4,2,64,128]{3,2,1,0:T(8,128)(2,1)S(1)} %dynamic-slice_bitcast_fusion.1), channel_id=1, source_target_pairs={{0,1},{1,0},{2,3},{3,2},{4,5},{5,4},{6,7},{7,6},{8,9},{9,8},{10,11... | collective-permute-start | bytes 393224 | tf_op jit(solution)/shard_map/ppermute | solution.py:24
  2.5 20.5 %collective-permute-start.1 = (f32[16,128]{1,0:T(8,128)S(1)}, f32[16,128]{1,0:T(8,128)S(1)}, u32[]{:S(2)}, u32[]{:S(2)}) collective-permute-start(f32[16,128]{1,0:T(8,128)S(1)} %select_maximum_fusion), channel_id=1, source_target_pairs={{0,1},{1,0},{2,3},{3,2},{4,5},{5,4},{6,7},{7,6},{8,9},{9,8},{10,11... | collective-permute-start | bytes 24584 | tf_op jit(solution)/shard_map/ppermute | solution.py:24
  4.4 38.2 %collective-permute-start.4 = (bf16[512,384]{1,0:T(8,128)(2,1)S(1)}, bf16[512,384]{1,0:T(8,128)(2,1)S(1)}, u32[]{:S(2)}, u32[]{:S(2)}) collective-permute-start(bf16[512,384]{1,0:T(8,128)(2,1)S(1)} %copy.61.w_own), channel_id=1, source_target_pairs={{0,2},{2,0},{1,3},{3,1},{4,6},{6,4},{5,7},{7,5},{8,10},{10,8},{9,1... | collective-permute-start | bytes 1179656 | tf_op jit(solution)/shard_map/ppermute | solution.py:24
  7.2 18.4 %copy-start.12 = (s32[256]{0:T(256)S(1)}, s32[256]{0:T(256)}, u32[]{:S(2)}) copy-start(s32[256]{0:T(256)} %param.20) | copy-start | bytes 3076
  7.2 21.4 %copy-start.8 = (bf16[128,512]{1,0:T(8,128)(2,1)S(1)}, bf16[128,512]{1,0:T(8,128)(2,1)}, u32[]{:S(2)}) copy-start(bf16[128,512]{1,0:T(8,128)(2,1)} %wo.1) | copy-start | bytes 393220
  8.4 32.6 %all-to-all-start = ((bf16[128,4,512]{2,1,0:T(4,128)(2,1)}), bf16[128,4,512]{2,1,0:T(4,128)(2,1)S(1)}, u32[]{:S(2)}, u32[]{:S(2)}) async-start(bf16[128,4,512]{2,1,0:T(4,128)(2,1)} %copy.58), calls=%async_computation | async-start | bytes 1048576 | tf_op jit(solution)/shard_map/all_to_all | solution.py:356
  23.0 5.5 %collective-permute-start.2 = (f32[2,16,128]{2,1,0:T(8,128)S(1)}, f32[2,16,128]{2,1,0:T(8,128)S(1)}, u32[]{:S(2)}, u32[]{:S(2)}) collective-permute-start(f32[2,16,128]{2,1,0:T(8,128)S(1)} %pad_maximum_fusion.4), channel_id=1, source_target_pairs={{0,2},{2,0},{1,3},{3,1},{4,6},{6,4},{5,7},{7,5},{8,10},{10,8},{9,1... | collective-permute-start | bytes 49160 | tf_op jit(solution)/shard_map/ppermute | solution.py:24
  28.7 13.9 %collective-permute-start.5 = (f32[8,128]{1,0:T(8,128)S(1)}, f32[8,128]{1,0:T(8,128)S(1)}, u32[]{:S(2)}, u32[]{:S(2)}) collective-permute-start(f32[8,128]{1,0:T(8,128)S(1)} %fusion.16.act_own), channel_id=1, source_target_pairs={{0,2},{2,0},{1,3},{3,1},{4,6},{6,4},{5,7},{7,5},{8,10},{10,8},{9,1... | collective-permute-start | bytes 12296 | tf_op jit(solution)/shard_map/ppermute | solution.py:24
  41.2 2.0 %collective-permute-start.3 = (bf16[2,256,512]{2,1,0:T(8,128)(2,1)S(1)}, bf16[2,256,512]{2,1,0:T(8,128)(2,1)S(1)}, u32[]{:S(2)}, u32[]{:S(2)}) collective-permute-start(bf16[2,256,512]{2,1,0:T(8,128)(2,1)S(1)} %reshape.257.in_own), channel_id=1, source_target_pairs={{0,1},{1,0},{2,3},{3,2},{4,5},{5,4},{6,7},{7,6},{8,9},{9,8},{10,11... | collective-permute-start | bytes 1572872 | tf_op jit(solution)/shard_map/ppermute | solution.py:24
  49.5 1.5 collective-permute-start.6
  51.6 8.5 %collective-permute-start.7 = (f32[16,128]{1,0:T(8,128)S(1)}, f32[16,128]{1,0:T(8,128)S(1)}, u32[]{:S(2)}, u32[]{:S(2)}) collective-permute-start(f32[16,128]{1,0:T(8,128)S(1)} %pad_maximum_fusion.5), channel_id=1, source_target_pairs={{0,128},{128,0},{1,129},{129,1},{2,130},{130,2},{3,131},{131,3},{4... | collective-permute-start | bytes 24584 | tf_op jit(solution)/shard_map/ppermute | solution.py:24
  55.0 5.1 %collective-permute-start.8 = (f32[8,128]{1,0:T(8,128)S(1)}, f32[8,128]{1,0:T(8,128)S(1)}, u32[]{:S(2)}, u32[]{:S(2)}) collective-permute-start(f32[8,128]{1,0:T(8,128)S(1)} %add.118), channel_id=1, source_target_pairs={{0,2},{2,0},{1,3},{3,1},{4,6},{6,4},{5,7},{7,5},{8,10},{10,8},{9,1... | collective-permute-start | bytes 12296 | tf_op jit(solution)/shard_map/ppermute | solution.py:24
  55.0 5.1 %collective-permute-start.9 = (f32[8,128]{1,0:T(8,128)S(1)}, f32[8,128]{1,0:T(8,128)S(1)}, u32[]{:S(2)}, u32[]{:S(2)}) collective-permute-start(f32[8,128]{1,0:T(8,128)S(1)} %add.118), channel_id=1, source_target_pairs={{0,130},{2,128},{128,2},{130,0},{1,131},{3,129},{129,3},{131,1},{4... | collective-permute-start | bytes 12296 | tf_op jit(solution)/shard_map/ppermute | solution.py:399
  60.9 15.5 %all-to-all-start.1 = ((f32[32,16,128]{2,1,0:T(8,128)}), f32[32,16,128]{2,1,0:T(8,128)S(1)}, u32[]{:S(2)}, u32[]{:S(2)}) async-start(f32[32,16,128]{2,1,0:T(8,128)} %broadcast_in_dim.50), calls=%async_computation.1 | async-start | bytes 524288 | tf_op jit(solution)/shard_map/all_to_all | solution.py:403
  64.9 6.6 %collective-permute-start.10 = (bf16[128,512]{1,0:T(8,128)(2,1)S(1)}, bf16[128,512]{1,0:T(8,128)(2,1)S(1)}, u32[]{:S(2)}, u32[]{:S(2)}) collective-permute-start(bf16[128,512]{1,0:T(8,128)(2,1)S(1)} %copy-done.8), channel_id=1, source_target_pairs={{0,2},{2,0},{1,3},{3,1},{4,6},{6,4},{5,7},{7,5},{8,10},{10,8},{9,1... | collective-permute-start | bytes 393224 | tf_op jit(solution)/shard_map/ppermute | solution.py:24
  83.8 13.9 %collective-permute-start.12 = (bf16[256,1024]{1,0:T(8,128)(2,1)}, bf16[256,1024]{1,0:T(8,128)(2,1)S(1)}, u32[]{:S(2)}, u32[]{:S(2)}) collective-permute-start(bf16[256,1024]{1,0:T(8,128)(2,1)} %get-tuple-element.60), channel_id=1, source_target_pairs={{0,2},{2,0},{1,3},{3,1},{4,6},{6,4},{5,7},{7,5},{8,10},{10,8},{9,1... | collective-permute-start | bytes 1572872 | tf_op jit(solution)/shard_map/ppermute | solution.py:24
  94.3 4.8 %collective-permute-start.11 = (bf16[528,512]{1,0:T(8,128)(2,1)}, bf16[528,512]{1,0:T(8,128)(2,1)S(1)}, u32[]{:S(2)}, u32[]{:S(2)}) collective-permute-start(bf16[528,512]{1,0:T(8,128)(2,1)} %get-tuple-element.57), channel_id=1, source_target_pairs={{0,1},{1,0},{2,3},{3,2},{4,5},{5,4},{6,7},{7,6},{8,9},{9,8},{10,11... | collective-permute-start | bytes 1622024 | tf_op jit(solution)/shard_map/ppermute | solution.py:24
  94.4 8.4 %collective-permute-start.13 = (f32[16,128]{1,0:T(8,128)}, f32[16,128]{1,0:T(8,128)S(1)}, u32[]{:S(2)}, u32[]{:S(2)}) collective-permute-start(f32[16,128]{1,0:T(8,128)} %get-tuple-element.62), channel_id=1, source_target_pairs={{0,2},{2,0},{1,3},{3,1},{4,6},{6,4},{5,7},{7,5},{8,10},{10,8},{9,1... | collective-permute-start | bytes 24584 | tf_op jit(solution)/shard_map/ppermute | solution.py:24
  95.0 7.8 %collective-permute-start.14 = (f32[16,128]{1,0:T(8,128)}, f32[16,128]{1,0:T(8,128)S(1)}, u32[]{:S(2)}, u32[]{:S(2)}) collective-permute-start(f32[16,128]{1,0:T(8,128)} %get-tuple-element.63), channel_id=1, source_target_pairs={{0,3},{1,2},{2,1},{3,0},{4,7},{5,6},{6,5},{7,4},{8,11},{9,10},{10,... | collective-permute-start | bytes 24584 | tf_op jit(solution)/shard_map/ppermute | solution.py:458
  105.8 38.2 %all-to-all-start.2 = ((bf16[64,4,2176]{2,1,0:T(4,128)(2,1)}), bf16[64,4,2176]{2,1,0:T(4,128)(2,1)S(1)}, u32[]{:S(2)}, u32[]{:S(2)}) async-start(bf16[64,4,2176]{2,1,0:T(4,128)(2,1)} %reshape.264), calls=%async_computation.2 | async-start | bytes 2228224 | tf_op jit(solution)/shard_map/all_to_all | solution.py:463
  145.2 25.2 %all-to-all-start.3 = ((bf16[64,4,1152]{2,1,0:T(4,128)(2,1)}), bf16[64,4,1152]{2,1,0:T(4,128)(2,1)S(1)}, u32[]{:S(2)}, u32[]{:S(2)}) async-start(bf16[64,4,1152]{2,1,0:T(4,128)(2,1)} %broadcast_in_dim.51), calls=%async_computation.3 | async-start | bytes 1179648 | tf_op jit(solution)/shard_map/all_to_all | solution.py:466
  152.5 4.8 %collective-permute-start.15 = (bf16[64,4,2,128]{3,0,1,2:T(8,128)(2,1)S(1)}, bf16[64,4,2,128]{3,0,1,2:T(8,128)(2,1)S(1)}, u32[]{:S(2)}, u32[]{:S(2)}) collective-permute-start(bf16[64,4,2,128]{3,0,1,2:T(8,128)(2,1)S(1)} %bitcast.113), channel_id=1, source_target_pairs={{0,1},{1,0},{2,3},{3,2},{4,5},{5,4},{6,7},{7,6},{8,9},{9,8},{10,11... | collective-permute-start | bytes 393224 | tf_op jit(solution)/shard_map/ppermute | solution.py:24
  153.7 9.8 %collective-permute-start.16 = (bf16[64,4,2,128]{3,0,1,2:T(8,128)(2,1)S(1)}, bf16[64,4,2,128]{3,0,1,2:T(8,128)(2,1)S(1)}, u32[]{:S(2)}, u32[]{:S(2)}) collective-permute-start(bf16[64,4,2,128]{3,0,1,2:T(8,128)(2,1)S(1)} %bitcast.114), channel_id=1, source_target_pairs={{0,2},{2,0},{1,3},{3,1},{4,6},{6,4},{5,7},{7,5},{8,10},{10,8},{9,1... | collective-permute-start | bytes 393224 | tf_op jit(solution)/shard_map/ppermute | solution.py:24
  154.2 11.8 %collective-permute-start.17 = (bf16[64,4,2,128]{3,0,1,2:T(8,128)(2,1)S(1)}, bf16[64,4,2,128]{3,0,1,2:T(8,128)(2,1)S(1)}, u32[]{:S(2)}, u32[]{:S(2)}) collective-permute-start(bf16[64,4,2,128]{3,0,1,2:T(8,128)(2,1)S(1)} %bitcast.115), channel_id=1, source_target_pairs={{0,3},{1,2},{2,1},{3,0},{4,7},{5,6},{6,5},{7,4},{8,11},{9,10},{10,... | collective-permute-start | bytes 393224 | tf_op jit(solution)/shard_map/ppermute | solution.py:475
  (21 other events, 92.7 us)

commit v5 on v4

--- a/solution.py
+++ b/solution.py
@@ -458,10 +458,17 @@
     far = lax.ppermute(small3, ("xh", "core"), [(0, 3), (1, 2), (2, 1), (3, 0)])
     small = (small + normed_got[frames : frames + 16, :share].astype(f32)) + (swap(small2, "xh") + far)
     small = jnp.pad(small.astype(bf16), ((0, frames - 16), (0, 0)))
-    grads = (grads_own + grads_got.astype(f32)).astype(bf16)
+    def half_of(index):
+        own = lax.dynamic_slice_in_dim(grads_own, index * width, width, 1)
+        return own + lax.dynamic_slice_in_dim(grads_got, index * width, width, 1).astype(f32)
+
+    from_xl = swap(half_of(1 - xl).astype(bf16), "xl")
+    grads = (half_of(xl) + from_xl.astype(f32)).astype(bf16)
     both_out = jnp.concatenate([both_out, grads, small], axis=1)
-    home = lax.all_to_all(both_out.reshape(n_tm, fl, 4 * width + share), TM, 0, 0, tiled=True)
-    summed = jnp.sum(home[:, :, 2 * width :].astype(f32), axis=0).astype(bf16)
+    home = lax.all_to_all(both_out.reshape(n_tm, fl, 3 * width + share), TM, 0, 0, tiled=True)
+    summed = jnp.sum(home[:, :, 2 * width :].astype(f32).reshape(2, n_yz, fl, width + share), axis=1)
+    few = summed[0, :, width:] + summed[1, :, width:]
+    summed = jnp.concatenate([summed[0, :, :width], summed[1, :, :width], few], axis=1).astype(bf16)
     copies = jnp.broadcast_to(summed[None], (n_tm, *summed.shape))
     summed = lax.all_to_all(copies, TM, 0, 0, tiled=True).reshape(frames, 2 * width + share)
     home = after(home[:, :, : 2 * width], copies)

time: 175 us -> 174 us (level)
  waiting for transfers between devices: 65.9 us -> 63.4 us
    all_to_all x1, waiting for transfers between devices: 31.1 us -> 25.8 us  [local(): lax.all_to_all(both_out.reshape(n_tm, fl, 3 * width + share), TM, 0, 0, t...]
    ppermute x15 -> x16, starting transfers between devices: 19.1 us -> 23.2 us  [swap(): return lax.ppermute(value, axis, [(0, 1), (1, 0)])]
    ppermute x15 -> x16, waiting for transfers between devices: 14.1 us -> 17.6 us  [swap(): return lax.ppermute(value, axis, [(0, 1), (1, 0)])]
    ppermute x1, starting transfers between devices: 2.76 us -> 0.01 us  [local(): far = lax.ppermute(small3, ('xh', 'core'), [(0, 3), (1, 2), (2, 1), (3, 0)])]
    all_to_all x1, waiting for transfers between devices: 3.44 us -> 1.5 us  [local(): lax.all_to_all(copies, TM, 0, 0, tiled=True)]
    unnamed x49 -> x57, local copies, waits for them, and re-layouts: 5.37 us -> 5.37 us
  transfers between devices with their start and end apart: 22 -> 23, of which waited for: 11 -> 13; matrix products, arithmetic and copies ran while one was open for 7% -> 7% of each run, Pallas kernels for 7% -> 7%
where the time goes in v5:
time: 174 us; the launch traced here: 172 us
  waiting for transfers between devices  63.4 us (36%)
  starting transfers between devices  58.7 us (34%)
  Pallas kernels  24.8 us (14%)
  local copies, waits for them, and re-layouts  15.6 us (9%)
  other arithmetic  8.55 us (5%)
    all_to_all x1, waiting for transfers between devices, local(): lax.all_to_all(both_out.reshape(n_tm, fl, 3 * width + share), TM, 0, 0, t...  25.8 us
    pallas_call x5, Pallas kernels, call(): pl.pallas_call(kernel, out_shape=[jax.ShapeDtypeStruct(s, d) for s, d in...  24.8 us
    ppermute x16, starting transfers between devices, swap(): return lax.ppermute(value, axis, [(0, 1), (1, 0)])  23.2 us
    ppermute x16, waiting for transfers between devices, swap(): return lax.ppermute(value, axis, [(0, 1), (1, 0)])  17.6 us
    all_to_all x1, starting transfers between devices, local(): lax.all_to_all(sent, ('xh',) + TM, 0, 0, tiled=True)  14.5 us
    all_to_all x1, waiting for transfers between devices, local(): lax.all_to_all(sent, ('xh',) + TM, 0, 0, tiled=True)  9.82 us
    all_to_all x1, starting transfers between devices, local(): lax.all_to_all(both_out.reshape(n_tm, fl, 3 * width + share), TM, 0, 0, t...  8.61 us
    unnamed x57, local copies, waits for them, and re-layouts  5.37 us
  transfers between devices with their start and end apart: 23, of which 13 were waited for; matrix products, arithmetic and copies ran while one was open for 7% of the time, Pallas kernels for 7%

profile of v5, /device:TPU:2, one launch (start us, length us, event | category | flops | bytes accessed | tf_op | source)
XLA Modules:
  0.0 172.4 jit_solution(10696019586227329519)
XLA Ops:
  4.4 2.2 %collective-permute-start.4 = (bf16[512,384]{1,0:T(8,128)(2,1)S(1)}, bf16[512,384]{1,0:T(8,128)(2,1)S(1)}, u32[]{:S(2)}, u32[]{:S(2)}) collective-permute-start(bf16[512,384]{1,0:T(8,128)(2,1)S(1)} %copy.61.w_own), channel_id=1, source_target_pairs={{0,2},{2,0},{1,3},{3,1},{4,6},{6,4},{5,7},{7,5},{8,10},{10,8},{9,1... | collective-permute-start | bytes 1179656 | tf_op jit(solution)/shard_map/ppermute | solution.py:24
  8.4 14.5 %all-to-all-start = ((bf16[128,4,512]{2,1,0:T(4,128)(2,1)}), bf16[128,4,512]{2,1,0:T(4,128)(2,1)S(1)}, u32[]{:S(2)}, u32[]{:S(2)}) async-start(bf16[128,4,512]{2,1,0:T(4,128)(2,1)} %copy.58), calls=%async_computation | async-start | bytes 1048576 | tf_op jit(solution)/shard_map/all_to_all | solution.py:356
  23.0 2.6 %collective-permute-start.2 = (f32[2,16,128]{2,1,0:T(8,128)S(1)}, f32[2,16,128]{2,1,0:T(8,128)S(1)}, u32[]{:S(2)}, u32[]{:S(2)}) collective-permute-start(f32[2,16,128]{2,1,0:T(8,128)S(1)} %pad_maximum_fusion.4), channel_id=1, source_target_pairs={{0,2},{2,0},{1,3},{3,1},{4,6},{6,4},{5,7},{7,5},{8,10},{10,8},{9,1... | collective-permute-start | bytes 49160 | tf_op jit(solution)/shard_map/ppermute | solution.py:24
  26.4 2.1 %collective-permute-done.2 = f32[2,16,128]{2,1,0:T(8,128)S(1)} collective-permute-done((f32[2,16,128]{2,1,0:T(8,128)S(1)}, f32[2,16,128]{2,1,0:T(8,128)S(1)}, u32[]{:S(2)}, u32[]{:S(2)}) %collective-permute-start.2) | collective-permute-done | bytes 16416 | tf_op jit(solution)/shard_map/ppermute | solution.py:24
  28.7 2.5 %collective-permute-start.5 = (f32[8,128]{1,0:T(8,128)S(1)}, f32[8,128]{1,0:T(8,128)S(1)}, u32[]{:S(2)}, u32[]{:S(2)}) collective-permute-start(f32[8,128]{1,0:T(8,128)S(1)} %fusion.18.act_own), channel_id=1, source_target_pairs={{0,2},{2,0},{1,3},{3,1},{4,6},{6,4},{5,7},{7,5},{8,10},{10,8},{9,1... | collective-permute-start | bytes 12296 | tf_op jit(solution)/shard_map/ppermute | solution.py:24
  31.2 9.8 %all-to-all-done = bf16[128,4,512]{2,1,0:T(4,128)(2,1)S(1)} async-done(((bf16[128,4,512]{2,1,0:T(4,128)(2,1)}), bf16[128,4,512]{2,1,0:T(4,128)(2,1)S(1)}, u32[]{:S(2)}, u32[]{:S(2)}) %all-to-all-start) | async-done | bytes 524320 | tf_op jit(solution)/shard_map/all_to_all | solution.py:356
  44.0 5.5 %shard_map.188 = (bf16[2,256,512]{2,1,0:T(8,128)(2,1)}, bf16[2,3,256,128]{3,2,1,0:T(8,128)(2,1)}, bf16[2,3,256,128]{3,2,1,0:T(8,128)(2,1)}, f32[2,256,4]{2,1,0:T...) custom-call(f32[4]{0:T(128)} %pad_maximum_fusion.7.scale, ...), custom_call_target="tpu_custom_call" | custom-call | flops 1000 | bytes 1 | tf_op jit(solution)/shard_map/pallas_call | solution.py:308
  51.6 3.4 %collective-permute-start.7 = (f32[16,128]{1,0:T(8,128)S(1)}, f32[16,128]{1,0:T(8,128)S(1)}, u32[]{:S(2)}, u32[]{:S(2)}) collective-permute-start(f32[16,128]{1,0:T(8,128)S(1)} %pad_maximum_fusion.6), channel_id=1, source_target_pairs={{0,128},{128,0},{1,129},{129,1},{2,130},{130,2},{3,131},{131,3},{4... | collective-permute-start | bytes 24584 | tf_op jit(solution)/shard_map/ppermute | solution.py:24
  56.6 3.5 %collective-permute-done.8 = f32[8,128]{1,0:T(8,128)S(1)} collective-permute-done((f32[8,128]{1,0:T(8,128)S(1)}, f32[8,128]{1,0:T(8,128)S(1)}, u32[]{:S(2)}, u32[]{:S(2)}) %collective-permute-start.8) | collective-permute-done | bytes 4128 | tf_op jit(solution)/shard_map/ppermute | solution.py:24
  60.9 4.0 %all-to-all-start.1 = ((f32[32,16,128]{2,1,0:T(8,128)}), f32[32,16,128]{2,1,0:T(8,128)S(1)}, u32[]{:S(2)}, u32[]{:S(2)}) async-start(f32[32,16,128]{2,1,0:T(8,128)} %broadcast_in_dim.50), calls=%async_computation.1 | async-start | bytes 524288 | tf_op jit(solution)/shard_map/all_to_all | solution.py:403
  64.9 3.3 %collective-permute-start.10 = (bf16[128,512]{1,0:T(8,128)(2,1)S(1)}, bf16[128,512]{1,0:T(8,128)(2,1)S(1)}, u32[]{:S(2)}, u32[]{:S(2)}) collective-permute-start(bf16[128,512]{1,0:T(8,128)(2,1)S(1)} %copy-done.10), channel_id=1, source_target_pairs={{0,2},{2,0},{1,3},{3,1},{4,6},{6,4},{5,7},{7,5},{8,10},{10,8},{9,1... | collective-permute-start | bytes 393224 | tf_op jit(solution)/shard_map/ppermute | solution.py:24
  68.8 2.2 %shard_map.189 = (bf16[2,512,256]{2,1,0:T(8,128)(2,1)}, bf16[2,128,256]{2,1,0:T(8,128)(2,1)}, bf16[2,128,256]{2,1,0:T(8,128)(2,1)}) custom-call(bf16[2,256,512]{2,1,0:T(8,128)(2,1)} %get-tuple-element.45.normed, bf16[2,256,128]{2,1,0:T(8,128)(2,1)} %get-tuple-element.42.attended0.attended, bf16[2,256,128]{2,1,0:T(8,128)(2,1)} %get-tuple-element.43.attended1.attended), custom_call_target="tpu_custom_call" | custom-call | flops 1000 | bytes 1 | tf_op jit(solution)/shard_map/pallas_call | solution.py:308
  71.5 4.9 %all-to-all-done.1.packed = f32[32,16,128]{2,1,0:T(8,128)S(1)} async-done(((f32[32,16,128]{2,1,0:T(8,128)}), f32[32,16,128]{2,1,0:T(8,128)S(1)}, u32[]{:S(2)}, u32[]{:S(2)}) %all-to-all-start.1) | async-done | bytes 262176 | tf_op jit(solution)/shard_map/all_to_all | solution.py:403
  77.1 6.7 %shard_map.190 = (f32[4,256]{1,0:T(4,128)}, f32[8,512]{1,0:T(8,128)}, bf16[2,256,512]{2,1,0:T(8,128)(2,1)}, bf16[2,256,384]{2,1,0:T(8,128)(2,1)}, bf16[256,1024]{1,0:T(8,128)(2,1)}, /*index=5*/f32[1,128]{1,0:T(1,128)}) custom-call(f32[4]{0:T(128)} %pad_maximum_fusion.7.scale, f32[32,16,128]{2,1,0:T(8,128)} %copy-done.8, bf16[2,256,512]{2,1,0:T(8,128)(2,1)} %copy-done.1, ...), custom_call_target="tpu_custom_call" | custom-call | flops 5000000000 | bytes 5000000 | tf_op jit(solution)/shard_map/pallas_call | solution.py:308
  83.9 3.1 %collective-permute-start.12 = (bf16[256,1024]{1,0:T(8,128)(2,1)}, bf16[256,1024]{1,0:T(8,128)(2,1)S(1)}, u32[]{:S(2)}, u32[]{:S(2)}) collective-permute-start(bf16[256,1024]{1,0:T(8,128)(2,1)} %get-tuple-element.60), channel_id=1, source_target_pairs={{0,2},{2,0},{1,3},{3,1},{4,6},{6,4},{5,7},{7,5},{8,10},{10,8},{9,1... | collective-permute-start | bytes 1572872 | tf_op jit(solution)/shard_map/ppermute | solution.py:24
  86.9 7.4 %shard_map.191 = (f32[256,1024]{1,0:T(8,128)}, f32[16,128]{1,0:T(8,128)}, f32[16,128]{1,0:T(8,128)}, f32[16,128]{1,0:T(8,128)}, f32[256,512]{1,0:T(8,128)}, /*in...) custom-call(f32[4]{0:T(128)} %pad_maximum_fusion.7.scale, s32[2]{0:T(128)} %pad_add_fusion.1.place, ...), custom_call_target="tpu_custom_call" | custom-call | flops 5000000000 | bytes 5000000 | tf_op jit(solution)/shard_map/pallas_call | solution.py:308
  94.5 1.9 %collective-permute-done.12 = bf16[256,1024]{1,0:T(8,128)(2,1)S(1)} collective-permute-done((bf16[256,1024]{1,0:T(8,128)(2,1)}, bf16[256,1024]{1,0:T(8,128)(2,1)S(1)}, u32[]{:S(2)}, u32[]{:S(2)}) %collective-permute-start.12) | collective-permute-done | bytes 524320 | tf_op jit(solution)/shard_map/ppermute | solution.py:24
  102.0 2.9 %shard_map.192 = bf16[256,1024]{1,0:T(8,128)(2,1)} custom-call(bf16[2,256,512]{2,1,0:T(8,128)(2,1)} %copy-done.1, f32[1,512]{1,0:T(1,128)} %bitcast.130, f32[256,512]{1,0:T(8,128)} %get-tuple-element.56.grad_own, bf16[528,512]{1,0:T(8,128)(2,1)} %copy-done.5, bf16[2,256,512]{2,1,0:T(8,128)(2,1)} %get-tuple-element.49.up, f32[256,512]{1,0:T(8,128)} %get-tuple-element.58.enc_part), custom_call_target="tpu_custom_call" | custom-call | flops 1310720 | bytes 1310 | tf_op jit(solution)/shard_map/pallas_call | solution.py:308
  108.0 8.6 %all-to-all-start.2 = ((bf16[64,4,1664]{2,1,0:T(4,128)(2,1)}), bf16[64,4,1664]{2,1,0:T(4,128)(2,1)S(1)}, u32[]{:S(2)}, u32[]{:S(2)}) async-start(bf16[64,4,1664]{2,1,0:T(4,128)(2,1)} %reshape.293), calls=%async_computation.2 | async-start | bytes 1703936 | tf_op jit(solution)/shard_map/all_to_all | solution.py:468
  116.6 25.8 %all-to-all-done.2 = bf16[64,4,1664]{2,1,0:T(4,128)(2,1)S(1)} async-done(((bf16[64,4,1664]{2,1,0:T(4,128)(2,1)}), bf16[64,4,1664]{2,1,0:T(4,128)(2,1)S(1)}, u32[]{:S(2)}, u32[]{:S(2)}) %all-to-all-start.2) | async-done | bytes 852000 | tf_op jit(solution)/shard_map/all_to_all | solution.py:468
  143.6 5.3 %all-to-all-start.3 = ((bf16[64,4,1152]{2,1,0:T(4,128)(2,1)}), bf16[64,4,1152]{2,1,0:T(4,128)(2,1)S(1)}, u32[]{:S(2)}, u32[]{:S(2)}) async-start(bf16[64,4,1152]{2,1,0:T(4,128)(2,1)} %broadcast_in_dim.51), calls=%async_computation.3 | async-start | bytes 1179648 | tf_op jit(solution)/shard_map/all_to_all | solution.py:473
  151.7 2.0 %collective-permute-start.17 = (bf16[64,4,2,128]{3,0,1,2:T(8,128)(2,1)S(1)}, bf16[64,4,2,128]{3,0,1,2:T(8,128)(2,1)S(1)}, u32[]{:S(2)}, u32[]{:S(2)}) collective-permute-start(bf16[64,4,2,128]{3,0,1,2:T(8,128)(2,1)S(1)} %bitcast.123), channel_id=1, source_target_pairs={{0,2},{2,0},{1,3},{3,1},{4,6},{6,4},{5,7},{7,5},{8,10},{10,8},{9,1... | collective-permute-start | bytes 393224 | tf_op jit(solution)/shard_map/ppermute | solution.py:24
  155.3 6.7 %collective-permute-done.17 = bf16[64,4,2,128]{3,0,1,2:T(8,128)(2,1)S(1)} collective-permute-done((bf16[64,4,2,128]{3,0,1,2:T(8,128)(2,1)S(1)}, bf16[64,4,2,128]{3,0,1,2:T(8,128)(2,1)S(1)}, u32[]{:S(2)}, u32[]{:S(2)}) %collective-permute-start.17) | collective-permute-done | bytes 131104 | tf_op jit(solution)/shard_map/ppermute | solution.py:24
  162.0 3.8 %collective-permute-done.18 = bf16[64,4,2,128]{3,0,1,2:T(8,128)(2,1)S(1)} collective-permute-done((bf16[64,4,2,128]{3,0,1,2:T(8,128)(2,1)S(1)}, bf16[64,4,2,128]{3,0,1,2:T(8,128)(2,1)S(1)}, u32[]{:S(2)}, u32[]{:S(2)}) %collective-permute-start.18) | collective-permute-done | bytes 131104 | tf_op jit(solution)/shard_map/ppermute | solution.py:482
  (150 shorter events, 36.1 us)
Async XLA Ops:
  1.7 5.3 %collective-permute-start = (bf16[4,2,64,128]{3,2,1,0:T(8,128)(2,1)S(1)}, bf16[4,2,64,128]{3,2,1,0:T(8,128)(2,1)S(1)}, u32[]{:S(2)}, u32[]{:S(2)}) collective-permute-start(bf16[4,2,64,128]{3,2,1,0:T(8,128)(2,1)S(1)} %dynamic-slice_bitcast_fusion.1), channel_id=1, source_target_pairs={{0,1},{1,0},{2,3},{3,2},{4,5},{5,4},{6,7},{7,6},{8,9},{9,8},{10,11... | collective-permute-start | bytes 393224 | tf_op jit(solution)/shard_map/ppermute | solution.py:24
  2.5 20.5 %collective-permute-start.1 = (f32[16,128]{1,0:T(8,128)S(1)}, f32[16,128]{1,0:T(8,128)S(1)}, u32[]{:S(2)}, u32[]{:S(2)}) collective-permute-start(f32[16,128]{1,0:T(8,128)S(1)} %select_maximum_fusion), channel_id=1, source_target_pairs={{0,1},{1,0},{2,3},{3,2},{4,5},{5,4},{6,7},{7,6},{8,9},{9,8},{10,11... | collective-permute-start | bytes 24584 | tf_op jit(solution)/shard_map/ppermute | solution.py:24
  4.4 38.2 %collective-permute-start.4 = (bf16[512,384]{1,0:T(8,128)(2,1)S(1)}, bf16[512,384]{1,0:T(8,128)(2,1)S(1)}, u32[]{:S(2)}, u32[]{:S(2)}) collective-permute-start(bf16[512,384]{1,0:T(8,128)(2,1)S(1)} %copy.61.w_own), channel_id=1, source_target_pairs={{0,2},{2,0},{1,3},{3,1},{4,6},{6,4},{5,7},{7,5},{8,10},{10,8},{9,1... | collective-permute-start | bytes 1179656 | tf_op jit(solution)/shard_map/ppermute | solution.py:24
  7.2 21.4 %copy-start.10 = (bf16[128,512]{1,0:T(8,128)(2,1)S(1)}, bf16[128,512]{1,0:T(8,128)(2,1)}, u32[]{:S(2)}) copy-start(bf16[128,512]{1,0:T(8,128)(2,1)} %wo.1) | copy-start | bytes 393220
  8.4 32.6 %all-to-all-start = ((bf16[128,4,512]{2,1,0:T(4,128)(2,1)}), bf16[128,4,512]{2,1,0:T(4,128)(2,1)S(1)}, u32[]{:S(2)}, u32[]{:S(2)}) async-start(bf16[128,4,512]{2,1,0:T(4,128)(2,1)} %copy.58), calls=%async_computation | async-start | bytes 1048576 | tf_op jit(solution)/shard_map/all_to_all | solution.py:356
  23.0 5.5 %collective-permute-start.2 = (f32[2,16,128]{2,1,0:T(8,128)S(1)}, f32[2,16,128]{2,1,0:T(8,128)S(1)}, u32[]{:S(2)}, u32[]{:S(2)}) collective-permute-start(f32[2,16,128]{2,1,0:T(8,128)S(1)} %pad_maximum_fusion.4), channel_id=1, source_target_pairs={{0,2},{2,0},{1,3},{3,1},{4,6},{6,4},{5,7},{7,5},{8,10},{10,8},{9,1... | collective-permute-start | bytes 49160 | tf_op jit(solution)/shard_map/ppermute | solution.py:24
  28.7 13.9 %collective-permute-start.5 = (f32[8,128]{1,0:T(8,128)S(1)}, f32[8,128]{1,0:T(8,128)S(1)}, u32[]{:S(2)}, u32[]{:S(2)}) collective-permute-start(f32[8,128]{1,0:T(8,128)S(1)} %fusion.18.act_own), channel_id=1, source_target_pairs={{0,2},{2,0},{1,3},{3,1},{4,6},{6,4},{5,7},{7,5},{8,10},{10,8},{9,1... | collective-permute-start | bytes 12296 | tf_op jit(solution)/shard_map/ppermute | solution.py:24
  41.2 2.0 %collective-permute-start.3 = (bf16[2,256,512]{2,1,0:T(8,128)(2,1)S(1)}, bf16[2,256,512]{2,1,0:T(8,128)(2,1)S(1)}, u32[]{:S(2)}, u32[]{:S(2)}) collective-permute-start(bf16[2,256,512]{2,1,0:T(8,128)(2,1)S(1)} %reshape.286.in_own), channel_id=1, source_target_pairs={{0,1},{1,0},{2,3},{3,2},{4,5},{5,4},{6,7},{7,6},{8,9},{9,8},{10,11... | collective-permute-start | bytes 1572872 | tf_op jit(solution)/shard_map/ppermute | solution.py:24
  49.5 1.5 collective-permute-start.6
  51.6 8.5 %collective-permute-start.7 = (f32[16,128]{1,0:T(8,128)S(1)}, f32[16,128]{1,0:T(8,128)S(1)}, u32[]{:S(2)}, u32[]{:S(2)}) collective-permute-start(f32[16,128]{1,0:T(8,128)S(1)} %pad_maximum_fusion.6), channel_id=1, source_target_pairs={{0,128},{128,0},{1,129},{129,1},{2,130},{130,2},{3,131},{131,3},{4... | collective-permute-start | bytes 24584 | tf_op jit(solution)/shard_map/ppermute | solution.py:24
  55.0 5.1 %collective-permute-start.8 = (f32[8,128]{1,0:T(8,128)S(1)}, f32[8,128]{1,0:T(8,128)S(1)}, u32[]{:S(2)}, u32[]{:S(2)}) collective-permute-start(f32[8,128]{1,0:T(8,128)S(1)} %add.136), channel_id=1, source_target_pairs={{0,2},{2,0},{1,3},{3,1},{4,6},{6,4},{5,7},{7,5},{8,10},{10,8},{9,1... | collective-permute-start | bytes 12296 | tf_op jit(solution)/shard_map/ppermute | solution.py:24
  55.0 5.1 %collective-permute-start.9 = (f32[8,128]{1,0:T(8,128)S(1)}, f32[8,128]{1,0:T(8,128)S(1)}, u32[]{:S(2)}, u32[]{:S(2)}) collective-permute-start(f32[8,128]{1,0:T(8,128)S(1)} %add.136), channel_id=1, source_target_pairs={{0,130},{2,128},{128,2},{130,0},{1,131},{3,129},{129,3},{131,1},{4... | collective-permute-start | bytes 12296 | tf_op jit(solution)/shard_map/ppermute | solution.py:399
  60.9 15.5 %all-to-all-start.1 = ((f32[32,16,128]{2,1,0:T(8,128)}), f32[32,16,128]{2,1,0:T(8,128)S(1)}, u32[]{:S(2)}, u32[]{:S(2)}) async-start(f32[32,16,128]{2,1,0:T(8,128)} %broadcast_in_dim.50), calls=%async_computation.1 | async-start | bytes 524288 | tf_op jit(solution)/shard_map/all_to_all | solution.py:403
  64.9 6.6 %collective-permute-start.10 = (bf16[128,512]{1,0:T(8,128)(2,1)S(1)}, bf16[128,512]{1,0:T(8,128)(2,1)S(1)}, u32[]{:S(2)}, u32[]{:S(2)}) collective-permute-start(bf16[128,512]{1,0:T(8,128)(2,1)S(1)} %copy-done.10), channel_id=1, source_target_pairs={{0,2},{2,0},{1,3},{3,1},{4,6},{6,4},{5,7},{7,5},{8,10},{10,8},{9,1... | collective-permute-start | bytes 393224 | tf_op jit(solution)/shard_map/ppermute | solution.py:24
  83.9 12.5 %collective-permute-start.12 = (bf16[256,1024]{1,0:T(8,128)(2,1)}, bf16[256,1024]{1,0:T(8,128)(2,1)S(1)}, u32[]{:S(2)}, u32[]{:S(2)}) collective-permute-start(bf16[256,1024]{1,0:T(8,128)(2,1)} %get-tuple-element.60), channel_id=1, source_target_pairs={{0,2},{2,0},{1,3},{3,1},{4,6},{6,4},{5,7},{7,5},{8,10},{10,8},{9,1... | collective-permute-start | bytes 1572872 | tf_op jit(solution)/shard_map/ppermute | solution.py:24
  94.4 6.8 %collective-permute-start.11 = (bf16[528,512]{1,0:T(8,128)(2,1)}, bf16[528,512]{1,0:T(8,128)(2,1)S(1)}, u32[]{:S(2)}, u32[]{:S(2)}) collective-permute-start(bf16[528,512]{1,0:T(8,128)(2,1)} %get-tuple-element.57), channel_id=1, source_target_pairs={{0,1},{1,0},{2,3},{3,2},{4,5},{5,4},{6,7},{7,6},{8,9},{9,8},{10,11... | collective-permute-start | bytes 1622024 | tf_op jit(solution)/shard_map/ppermute | solution.py:24
  98.2 8.4 %collective-permute-start.13 = (bf16[256,512]{1,0:T(8,128)(2,1)}, bf16[256,512]{1,0:T(8,128)(2,1)S(1)}, u32[]{:S(2)}, u32[]{:S(2)}) collective-permute-start(bf16[256,512]{1,0:T(8,128)(2,1)} %add_convert_fusion.1), channel_id=1, source_target_pairs={{0,128},{128,0},{1,129},{129,1},{2,130},{130,2},{3,131},{131,3},{4... | collective-permute-start | bytes 786440 | tf_op jit(solution)/shard_map/ppermute | solution.py:24
  99.7 6.1 %collective-permute-start.14 = (f32[16,128]{1,0:T(8,128)S(1)}, f32[16,128]{1,0:T(8,128)S(1)}, u32[]{:S(2)}, u32[]{:S(2)}) collective-permute-start(f32[16,128]{1,0:T(8,128)S(1)} %copy-done.26), channel_id=1, source_target_pairs={{0,2},{2,0},{1,3},{3,1},{4,6},{6,4},{5,7},{7,5},{8,10},{10,8},{9,1... | collective-permute-start | bytes 24584 | tf_op jit(solution)/shard_map/ppermute | solution.py:24
  101.2 4.7 %collective-permute-start.15 = (f32[16,128]{1,0:T(8,128)S(1)}, f32[16,128]{1,0:T(8,128)S(1)}, u32[]{:S(2)}, u32[]{:S(2)}) collective-permute-start(f32[16,128]{1,0:T(8,128)S(1)} %copy-done.25), channel_id=1, source_target_pairs={{0,3},{1,2},{2,1},{3,0},{4,7},{5,6},{6,5},{7,4},{8,11},{9,10},{10,... | collective-permute-start | bytes 24584 | tf_op jit(solution)/shard_map/ppermute | solution.py:458
  108.0 34.5 %all-to-all-start.2 = ((bf16[64,4,1664]{2,1,0:T(4,128)(2,1)}), bf16[64,4,1664]{2,1,0:T(4,128)(2,1)S(1)}, u32[]{:S(2)}, u32[]{:S(2)}) async-start(bf16[64,4,1664]{2,1,0:T(4,128)(2,1)} %reshape.293), calls=%async_computation.2 | async-start | bytes 1703936 | tf_op jit(solution)/shard_map/all_to_all | solution.py:468
  143.6 24.7 %all-to-all-start.3 = ((bf16[64,4,1152]{2,1,0:T(4,128)(2,1)}), bf16[64,4,1152]{2,1,0:T(4,128)(2,1)S(1)}, u32[]{:S(2)}, u32[]{:S(2)}) async-start(bf16[64,4,1152]{2,1,0:T(4,128)(2,1)} %broadcast_in_dim.51), calls=%async_computation.3 | async-start | bytes 1179648 | tf_op jit(solution)/shard_map/all_to_all | solution.py:473
  150.5 4.8 %collective-permute-start.16 = (bf16[64,4,2,128]{3,0,1,2:T(8,128)(2,1)S(1)}, bf16[64,4,2,128]{3,0,1,2:T(8,128)(2,1)S(1)}, u32[]{:S(2)}, u32[]{:S(2)}) collective-permute-start(bf16[64,4,2,128]{3,0,1,2:T(8,128)(2,1)S(1)} %bitcast.122), channel_id=1, source_target_pairs={{0,1},{1,0},{2,3},{3,2},{4,5},{5,4},{6,7},{7,6},{8,9},{9,8},{10,11... | collective-permute-start | bytes 393224 | tf_op jit(solution)/shard_map/ppermute | solution.py:24
  151.7 10.3 %collective-permute-start.17 = (bf16[64,4,2,128]{3,0,1,2:T(8,128)(2,1)S(1)}, bf16[64,4,2,128]{3,0,1,2:T(8,128)(2,1)S(1)}, u32[]{:S(2)}, u32[]{:S(2)}) collective-permute-start(bf16[64,4,2,128]{3,0,1,2:T(8,128)(2,1)S(1)} %bitcast.123), channel_id=1, source_target_pairs={{0,2},{2,0},{1,3},{3,1},{4,6},{6,4},{5,7},{7,5},{8,10},{10,8},{9,1... | collective-permute-start | bytes 393224 | tf_op jit(solution)/shard_map/ppermute | solution.py:24
  153.8 12.0 %collective-permute-start.18 = (bf16[64,4,2,128]{3,0,1,2:T(8,128)(2,1)S(1)}, bf16[64,4,2,128]{3,0,1,2:T(8,128)(2,1)S(1)}, u32[]{:S(2)}, u32[]{:S(2)}) collective-permute-start(bf16[64,4,2,128]{3,0,1,2:T(8,128)(2,1)S(1)} %bitcast.124), channel_id=1, source_target_pairs={{0,3},{1,2},{2,1},{3,0},{4,7},{5,6},{6,5},{7,4},{8,11},{9,10},{10,... | collective-permute-start | bytes 393224 | tf_op jit(solution)/shard_map/ppermute | solution.py:482
  (26 other events, 132.5 us)

commit v6 on v5

--- a/solution.py
+++ b/solution.py
@@ -435,7 +435,7 @@
             gp_other, scale_other, attended1, wo_other,
         ),
         (
-            ((width // 2, 2 * width), f32),
+            ((width // 2, 2 * width), bf16),
             ((16, share), f32),
             ((16, share), f32),
             ((16, share), f32),
@@ -460,7 +460,7 @@
     small = jnp.pad(small.astype(bf16), ((0, frames - 16), (0, 0)))
     def half_of(index):
         own = lax.dynamic_slice_in_dim(grads_own, index * width, width, 1)
-        return own + lax.dynamic_slice_in_dim(grads_got, index * width, width, 1).astype(f32)
+        return own.astype(f32) + lax.dynamic_slice_in_dim(grads_got, index * width, width, 1).astype(f32)
 
     from_xl = swap(half_of(1 - xl).astype(bf16), "xl")
     grads = (half_of(xl) + from_xl.astype(f32)).astype(bf16)

time: 174 us -> 173 us (level)
    unnamed x57 -> x53, local copies, waits for them, and re-layouts: 5.37 us -> 5.38 us
  transfers between devices with their start and end apart: 23 -> 23, of which waited for: 13 -> 14; matrix products, arithmetic and copies ran while one was open for 7% -> 7% of each run, Pallas kernels for 7% -> 7%
where the time goes in v6:
time: 173 us; the launch traced here: 172 us
  waiting for transfers between devices  63.6 us (37%)
  starting transfers between devices  58.8 us (34%)
  Pallas kernels  24.6 us (14%)
  local copies, waits for them, and re-layouts  15.6 us (9%)
  other arithmetic  7.71 us (4%)
    all_to_all x1, waiting for transfers between devices, local(): lax.all_to_all(both_out.reshape(n_tm, fl, 3 * width + share), TM, 0, 0, t...  25.7 us
    pallas_call x5, Pallas kernels, call(): pl.pallas_call(kernel, out_shape=[jax.ShapeDtypeStruct(s, d) for s, d in...  24.6 us
    ppermute x16, starting transfers between devices, swap(): return lax.ppermute(value, axis, [(0, 1), (1, 0)])  23.4 us
    ppermute x16, waiting for transfers between devices, swap(): return lax.ppermute(value, axis, [(0, 1), (1, 0)])  17.5 us
    all_to_all x1, starting transfers between devices, local(): lax.all_to_all(sent, ('xh',) + TM, 0, 0, tiled=True)  14.5 us
    all_to_all x1, waiting for transfers between devices, local(): lax.all_to_all(sent, ('xh',) + TM, 0, 0, tiled=True)  9.82 us
    all_to_all x1, starting transfers between devices, local(): lax.all_to_all(both_out.reshape(n_tm, fl, 3 * width + share), TM, 0, 0, t...  8.53 us
    unnamed x53, local copies, waits for them, and re-layouts  5.38 us
  transfers between devices with their start and end apart: 23, of which 14 were waited for; matrix products, arithmetic and copies ran while one was open for 7% of the time, Pallas kernels for 7%

profile of v6, /device:TPU:2, one launch (start us, length us, event | category | flops | bytes accessed | tf_op | source)
XLA Modules:
  0.0 171.7 jit_solution(17467454595587920169)
XLA Ops:
  4.4 2.2 %collective-permute-start.4 = (bf16[512,384]{1,0:T(8,128)(2,1)S(1)}, bf16[512,384]{1,0:T(8,128)(2,1)S(1)}, u32[]{:S(2)}, u32[]{:S(2)}) collective-permute-start(bf16[512,384]{1,0:T(8,128)(2,1)S(1)} %copy.61.w_own), channel_id=1, source_target_pairs={{0,2},{2,0},{1,3},{3,1},{4,6},{6,4},{5,7},{7,5},{8,10},{10,8},{9,1... | collective-permute-start | bytes 1179656 | tf_op jit(solution)/shard_map/ppermute | solution.py:24
  8.4 14.5 %all-to-all-start = ((bf16[128,4,512]{2,1,0:T(4,128)(2,1)}), bf16[128,4,512]{2,1,0:T(4,128)(2,1)S(1)}, u32[]{:S(2)}, u32[]{:S(2)}) async-start(bf16[128,4,512]{2,1,0:T(4,128)(2,1)} %copy.58), calls=%async_computation | async-start | bytes 1048576 | tf_op jit(solution)/shard_map/all_to_all | solution.py:356
  23.0 2.6 %collective-permute-start.2 = (f32[2,16,128]{2,1,0:T(8,128)S(1)}, f32[2,16,128]{2,1,0:T(8,128)S(1)}, u32[]{:S(2)}, u32[]{:S(2)}) collective-permute-start(f32[2,16,128]{2,1,0:T(8,128)S(1)} %pad_maximum_fusion.4), channel_id=1, source_target_pairs={{0,2},{2,0},{1,3},{3,1},{4,6},{6,4},{5,7},{7,5},{8,10},{10,8},{9,1... | collective-permute-start | bytes 49160 | tf_op jit(solution)/shard_map/ppermute | solution.py:24
  26.4 2.1 %collective-permute-done.2 = f32[2,16,128]{2,1,0:T(8,128)S(1)} collective-permute-done((f32[2,16,128]{2,1,0:T(8,128)S(1)}, f32[2,16,128]{2,1,0:T(8,128)S(1)}, u32[]{:S(2)}, u32[]{:S(2)}) %collective-permute-start.2) | collective-permute-done | bytes 16416 | tf_op jit(solution)/shard_map/ppermute | solution.py:24
  28.7 2.5 %collective-permute-start.5 = (f32[8,128]{1,0:T(8,128)S(1)}, f32[8,128]{1,0:T(8,128)S(1)}, u32[]{:S(2)}, u32[]{:S(2)}) collective-permute-start(f32[8,128]{1,0:T(8,128)S(1)} %fusion.18.act_own), channel_id=1, source_target_pairs={{0,2},{2,0},{1,3},{3,1},{4,6},{6,4},{5,7},{7,5},{8,10},{10,8},{9,1... | collective-permute-start | bytes 12296 | tf_op jit(solution)/shard_map/ppermute | solution.py:24
  31.2 9.8 %all-to-all-done = bf16[128,4,512]{2,1,0:T(4,128)(2,1)S(1)} async-done(((bf16[128,4,512]{2,1,0:T(4,128)(2,1)}), bf16[128,4,512]{2,1,0:T(4,128)(2,1)S(1)}, u32[]{:S(2)}, u32[]{:S(2)}) %all-to-all-start) | async-done | bytes 524320 | tf_op jit(solution)/shard_map/all_to_all | solution.py:356
  44.0 5.5 %shard_map.188 = (bf16[2,256,512]{2,1,0:T(8,128)(2,1)}, bf16[2,3,256,128]{3,2,1,0:T(8,128)(2,1)}, bf16[2,3,256,128]{3,2,1,0:T(8,128)(2,1)}, f32[2,256,4]{2,1,0:T...) custom-call(f32[4]{0:T(128)} %pad_maximum_fusion.7.scale, ...), custom_call_target="tpu_custom_call" | custom-call | flops 1000 | bytes 1 | tf_op jit(solution)/shard_map/pallas_call | solution.py:308
  51.6 3.4 %collective-permute-start.7 = (f32[16,128]{1,0:T(8,128)S(1)}, f32[16,128]{1,0:T(8,128)S(1)}, u32[]{:S(2)}, u32[]{:S(2)}) collective-permute-start(f32[16,128]{1,0:T(8,128)S(1)} %pad_maximum_fusion.6), channel_id=1, source_target_pairs={{0,128},{128,0},{1,129},{129,1},{2,130},{130,2},{3,131},{131,3},{4... | collective-permute-start | bytes 24584 | tf_op jit(solution)/shard_map/ppermute | solution.py:24
  56.6 3.5 %collective-permute-done.8 = f32[8,128]{1,0:T(8,128)S(1)} collective-permute-done((f32[8,128]{1,0:T(8,128)S(1)}, f32[8,128]{1,0:T(8,128)S(1)}, u32[]{:S(2)}, u32[]{:S(2)}) %collective-permute-start.8) | collective-permute-done | bytes 4128 | tf_op jit(solution)/shard_map/ppermute | solution.py:24
  60.9 4.0 %all-to-all-start.1 = ((f32[32,16,128]{2,1,0:T(8,128)}), f32[32,16,128]{2,1,0:T(8,128)S(1)}, u32[]{:S(2)}, u32[]{:S(2)}) async-start(f32[32,16,128]{2,1,0:T(8,128)} %broadcast_in_dim.50), calls=%async_computation.1 | async-start | bytes 524288 | tf_op jit(solution)/shard_map/all_to_all | solution.py:403
  64.9 3.3 %collective-permute-start.10 = (bf16[128,512]{1,0:T(8,128)(2,1)S(1)}, bf16[128,512]{1,0:T(8,128)(2,1)S(1)}, u32[]{:S(2)}, u32[]{:S(2)}) collective-permute-start(bf16[128,512]{1,0:T(8,128)(2,1)S(1)} %copy-done.10), channel_id=1, source_target_pairs={{0,2},{2,0},{1,3},{3,1},{4,6},{6,4},{5,7},{7,5},{8,10},{10,8},{9,1... | collective-permute-start | bytes 393224 | tf_op jit(solution)/shard_map/ppermute | solution.py:24
  68.8 2.3 %shard_map.189 = (bf16[2,512,256]{2,1,0:T(8,128)(2,1)}, bf16[2,128,256]{2,1,0:T(8,128)(2,1)}, bf16[2,128,256]{2,1,0:T(8,128)(2,1)}) custom-call(bf16[2,256,512]{2,1,0:T(8,128)(2,1)} %get-tuple-element.45.normed, bf16[2,256,128]{2,1,0:T(8,128)(2,1)} %get-tuple-element.42.attended0.attended, bf16[2,256,128]{2,1,0:T(8,128)(2,1)} %get-tuple-element.43.attended1.attended), custom_call_target="tpu_custom_call" | custom-call | flops 1000 | bytes 1 | tf_op jit(solution)/shard_map/pallas_call | solution.py:308
  71.5 4.9 %all-to-all-done.1.packed = f32[32,16,128]{2,1,0:T(8,128)S(1)} async-done(((f32[32,16,128]{2,1,0:T(8,128)}), f32[32,16,128]{2,1,0:T(8,128)S(1)}, u32[]{:S(2)}, u32[]{:S(2)}) %all-to-all-start.1) | async-done | bytes 262176 | tf_op jit(solution)/shard_map/all_to_all | solution.py:403
  77.1 6.7 %shard_map.190 = (f32[4,256]{1,0:T(4,128)}, f32[8,512]{1,0:T(8,128)}, bf16[2,256,512]{2,1,0:T(8,128)(2,1)}, bf16[2,256,384]{2,1,0:T(8,128)(2,1)}, bf16[256,1024]{1,0:T(8,128)(2,1)}, /*index=5*/f32[1,128]{1,0:T(1,128)}) custom-call(f32[4]{0:T(128)} %pad_maximum_fusion.7.scale, f32[32,16,128]{2,1,0:T(8,128)} %copy-done.8, bf16[2,256,512]{2,1,0:T(8,128)(2,1)} %copy-done.1, ...), custom_call_target="tpu_custom_call" | custom-call | flops 5000000000 | bytes 5000000 | tf_op jit(solution)/shard_map/pallas_call | solution.py:308
  83.9 3.1 %collective-permute-start.12 = (bf16[256,1024]{1,0:T(8,128)(2,1)}, bf16[256,1024]{1,0:T(8,128)(2,1)S(1)}, u32[]{:S(2)}, u32[]{:S(2)}) collective-permute-start(bf16[256,1024]{1,0:T(8,128)(2,1)} %get-tuple-element.60), channel_id=1, source_target_pairs={{0,2},{2,0},{1,3},{3,1},{4,6},{6,4},{5,7},{7,5},{8,10},{10,8},{9,1... | collective-permute-start | bytes 1572872 | tf_op jit(solution)/shard_map/ppermute | solution.py:24
  87.0 7.2 %shard_map.191 = (bf16[256,1024]{1,0:T(8,128)(2,1)}, f32[16,128]{1,0:T(8,128)}, f32[16,128]{1,0:T(8,128)}, f32[16,128]{1,0:T(8,128)}, f32[256,512]{1,0:T(8,128)}...) custom-call(f32[4]{0:T(128)} %pad_maximum_fusion.7.scale, s32[2]{0:T(128)} %pad_add_fusion.1.place, ...), custom_call_target="tpu_custom_call" | custom-call | flops 5000000000 | bytes 5000000 | tf_op jit(solution)/shard_map/pallas_call | solution.py:308
  94.2 2.2 %collective-permute-done.12 = bf16[256,1024]{1,0:T(8,128)(2,1)S(1)} collective-permute-done((bf16[256,1024]{1,0:T(8,128)(2,1)}, bf16[256,1024]{1,0:T(8,128)(2,1)S(1)}, u32[]{:S(2)}, u32[]{:S(2)}) %collective-permute-start.12) | collective-permute-done | bytes 524320 | tf_op jit(solution)/shard_map/ppermute | solution.py:24
  101.4 2.9 %shard_map.192 = bf16[256,1024]{1,0:T(8,128)(2,1)} custom-call(bf16[2,256,512]{2,1,0:T(8,128)(2,1)} %copy-done.1, f32[1,512]{1,0:T(1,128)} %bitcast.130, f32[256,512]{1,0:T(8,128)} %get-tuple-element.56.grad_own, bf16[528,512]{1,0:T(8,128)(2,1)} %copy-done.4, bf16[2,256,512]{2,1,0:T(8,128)(2,1)} %get-tuple-element.49.up, f32[256,512]{1,0:T(8,128)} %get-tuple-element.58.enc_part), custom_call_target="tpu_custom_call" | custom-call | flops 1310720 | bytes 1310 | tf_op jit(solution)/shard_map/pallas_call | solution.py:308
  107.4 8.5 %all-to-all-start.2 = ((bf16[64,4,1664]{2,1,0:T(4,128)(2,1)}), bf16[64,4,1664]{2,1,0:T(4,128)(2,1)S(1)}, u32[]{:S(2)}, u32[]{:S(2)}) async-start(bf16[64,4,1664]{2,1,0:T(4,128)(2,1)} %reshape.293), calls=%async_computation.2 | async-start | bytes 1703936 | tf_op jit(solution)/shard_map/all_to_all | solution.py:468
  116.0 25.7 %all-to-all-done.2 = bf16[64,4,1664]{2,1,0:T(4,128)(2,1)S(1)} async-done(((bf16[64,4,1664]{2,1,0:T(4,128)(2,1)}), bf16[64,4,1664]{2,1,0:T(4,128)(2,1)S(1)}, u32[]{:S(2)}, u32[]{:S(2)}) %all-to-all-start.2) | async-done | bytes 852000 | tf_op jit(solution)/shard_map/all_to_all | solution.py:468
  142.9 5.3 %all-to-all-start.3 = ((bf16[64,4,1152]{2,1,0:T(4,128)(2,1)}), bf16[64,4,1152]{2,1,0:T(4,128)(2,1)S(1)}, u32[]{:S(2)}, u32[]{:S(2)}) async-start(bf16[64,4,1152]{2,1,0:T(4,128)(2,1)} %broadcast_in_dim.51), calls=%async_computation.3 | async-start | bytes 1179648 | tf_op jit(solution)/shard_map/all_to_all | solution.py:473
  151.0 2.1 %collective-permute-start.17 = (bf16[64,4,2,128]{3,0,1,2:T(8,128)(2,1)S(1)}, bf16[64,4,2,128]{3,0,1,2:T(8,128)(2,1)S(1)}, u32[]{:S(2)}, u32[]{:S(2)}) collective-permute-start(bf16[64,4,2,128]{3,0,1,2:T(8,128)(2,1)S(1)} %bitcast.123), channel_id=1, source_target_pairs={{0,2},{2,0},{1,3},{3,1},{4,6},{6,4},{5,7},{7,5},{8,10},{10,8},{9,1... | collective-permute-start | bytes 393224 | tf_op jit(solution)/shard_map/ppermute | solution.py:24
  154.6 6.7 %collective-permute-done.17 = bf16[64,4,2,128]{3,0,1,2:T(8,128)(2,1)S(1)} collective-permute-done((bf16[64,4,2,128]{3,0,1,2:T(8,128)(2,1)S(1)}, bf16[64,4,2,128]{3,0,1,2:T(8,128)(2,1)S(1)}, u32[]{:S(2)}, u32[]{:S(2)}) %collective-permute-start.17) | collective-permute-done | bytes 131104 | tf_op jit(solution)/shard_map/ppermute | solution.py:24
  161.3 3.7 %collective-permute-done.18 = bf16[64,4,2,128]{3,0,1,2:T(8,128)(2,1)S(1)} collective-permute-done((bf16[64,4,2,128]{3,0,1,2:T(8,128)(2,1)S(1)}, bf16[64,4,2,128]{3,0,1,2:T(8,128)(2,1)S(1)}, u32[]{:S(2)}, u32[]{:S(2)}) %collective-permute-start.18) | collective-permute-done | bytes 131104 | tf_op jit(solution)/shard_map/ppermute | solution.py:482
  (146 shorter events, 35.4 us)
Async XLA Ops:
  1.7 5.3 %collective-permute-start = (bf16[4,2,64,128]{3,2,1,0:T(8,128)(2,1)S(1)}, bf16[4,2,64,128]{3,2,1,0:T(8,128)(2,1)S(1)}, u32[]{:S(2)}, u32[]{:S(2)}) collective-permute-start(bf16[4,2,64,128]{3,2,1,0:T(8,128)(2,1)S(1)} %dynamic-slice_bitcast_fusion.1), channel_id=1, source_target_pairs={{0,1},{1,0},{2,3},{3,2},{4,5},{5,4},{6,7},{7,6},{8,9},{9,8},{10,11... | collective-permute-start | bytes 393224 | tf_op jit(solution)/shard_map/ppermute | solution.py:24
  2.5 20.5 %collective-permute-start.1 = (f32[16,128]{1,0:T(8,128)S(1)}, f32[16,128]{1,0:T(8,128)S(1)}, u32[]{:S(2)}, u32[]{:S(2)}) collective-permute-start(f32[16,128]{1,0:T(8,128)S(1)} %select_maximum_fusion), channel_id=1, source_target_pairs={{0,1},{1,0},{2,3},{3,2},{4,5},{5,4},{6,7},{7,6},{8,9},{9,8},{10,11... | collective-permute-start | bytes 24584 | tf_op jit(solution)/shard_map/ppermute | solution.py:24
  4.4 38.2 %collective-permute-start.4 = (bf16[512,384]{1,0:T(8,128)(2,1)S(1)}, bf16[512,384]{1,0:T(8,128)(2,1)S(1)}, u32[]{:S(2)}, u32[]{:S(2)}) collective-permute-start(bf16[512,384]{1,0:T(8,128)(2,1)S(1)} %copy.61.w_own), channel_id=1, source_target_pairs={{0,2},{2,0},{1,3},{3,1},{4,6},{6,4},{5,7},{7,5},{8,10},{10,8},{9,1... | collective-permute-start | bytes 1179656 | tf_op jit(solution)/shard_map/ppermute | solution.py:24
  7.2 21.4 %copy-start.10 = (bf16[128,512]{1,0:T(8,128)(2,1)S(1)}, bf16[128,512]{1,0:T(8,128)(2,1)}, u32[]{:S(2)}) copy-start(bf16[128,512]{1,0:T(8,128)(2,1)} %wo.1) | copy-start | bytes 393220
  8.4 32.6 %all-to-all-start = ((bf16[128,4,512]{2,1,0:T(4,128)(2,1)}), bf16[128,4,512]{2,1,0:T(4,128)(2,1)S(1)}, u32[]{:S(2)}, u32[]{:S(2)}) async-start(bf16[128,4,512]{2,1,0:T(4,128)(2,1)} %copy.58), calls=%async_computation | async-start | bytes 1048576 | tf_op jit(solution)/shard_map/all_to_all | solution.py:356
  23.0 5.5 %collective-permute-start.2 = (f32[2,16,128]{2,1,0:T(8,128)S(1)}, f32[2,16,128]{2,1,0:T(8,128)S(1)}, u32[]{:S(2)}, u32[]{:S(2)}) collective-permute-start(f32[2,16,128]{2,1,0:T(8,128)S(1)} %pad_maximum_fusion.4), channel_id=1, source_target_pairs={{0,2},{2,0},{1,3},{3,1},{4,6},{6,4},{5,7},{7,5},{8,10},{10,8},{9,1... | collective-permute-start | bytes 49160 | tf_op jit(solution)/shard_map/ppermute | solution.py:24
  28.7 13.8 %collective-permute-start.5 = (f32[8,128]{1,0:T(8,128)S(1)}, f32[8,128]{1,0:T(8,128)S(1)}, u32[]{:S(2)}, u32[]{:S(2)}) collective-permute-start(f32[8,128]{1,0:T(8,128)S(1)} %fusion.18.act_own), channel_id=1, source_target_pairs={{0,2},{2,0},{1,3},{3,1},{4,6},{6,4},{5,7},{7,5},{8,10},{10,8},{9,1... | collective-permute-start | bytes 12296 | tf_op jit(solution)/shard_map/ppermute | solution.py:24
  41.2 2.0 %collective-permute-start.3 = (bf16[2,256,512]{2,1,0:T(8,128)(2,1)S(1)}, bf16[2,256,512]{2,1,0:T(8,128)(2,1)S(1)}, u32[]{:S(2)}, u32[]{:S(2)}) collective-permute-start(bf16[2,256,512]{2,1,0:T(8,128)(2,1)S(1)} %reshape.286.in_own), channel_id=1, source_target_pairs={{0,1},{1,0},{2,3},{3,2},{4,5},{5,4},{6,7},{7,6},{8,9},{9,8},{10,11... | collective-permute-start | bytes 1572872 | tf_op jit(solution)/shard_map/ppermute | solution.py:24
  49.5 1.5 collective-permute-start.6
  51.6 8.5 %collective-permute-start.7 = (f32[16,128]{1,0:T(8,128)S(1)}, f32[16,128]{1,0:T(8,128)S(1)}, u32[]{:S(2)}, u32[]{:S(2)}) collective-permute-start(f32[16,128]{1,0:T(8,128)S(1)} %pad_maximum_fusion.6), channel_id=1, source_target_pairs={{0,128},{128,0},{1,129},{129,1},{2,130},{130,2},{3,131},{131,3},{4... | collective-permute-start | bytes 24584 | tf_op jit(solution)/shard_map/ppermute | solution.py:24
  55.0 5.1 %collective-permute-start.8 = (f32[8,128]{1,0:T(8,128)S(1)}, f32[8,128]{1,0:T(8,128)S(1)}, u32[]{:S(2)}, u32[]{:S(2)}) collective-permute-start(f32[8,128]{1,0:T(8,128)S(1)} %add.136), channel_id=1, source_target_pairs={{0,2},{2,0},{1,3},{3,1},{4,6},{6,4},{5,7},{7,5},{8,10},{10,8},{9,1... | collective-permute-start | bytes 12296 | tf_op jit(solution)/shard_map/ppermute | solution.py:24
  55.0 5.1 %collective-permute-start.9 = (f32[8,128]{1,0:T(8,128)S(1)}, f32[8,128]{1,0:T(8,128)S(1)}, u32[]{:S(2)}, u32[]{:S(2)}) collective-permute-start(f32[8,128]{1,0:T(8,128)S(1)} %add.136), channel_id=1, source_target_pairs={{0,130},{2,128},{128,2},{130,0},{1,131},{3,129},{129,3},{131,1},{4... | collective-permute-start | bytes 12296 | tf_op jit(solution)/shard_map/ppermute | solution.py:399
  60.9 15.5 %all-to-all-start.1 = ((f32[32,16,128]{2,1,0:T(8,128)}), f32[32,16,128]{2,1,0:T(8,128)S(1)}, u32[]{:S(2)}, u32[]{:S(2)}) async-start(f32[32,16,128]{2,1,0:T(8,128)} %broadcast_in_dim.50), calls=%async_computation.1 | async-start | bytes 524288 | tf_op jit(solution)/shard_map/all_to_all | solution.py:403
  64.9 6.6 %collective-permute-start.10 = (bf16[128,512]{1,0:T(8,128)(2,1)S(1)}, bf16[128,512]{1,0:T(8,128)(2,1)S(1)}, u32[]{:S(2)}, u32[]{:S(2)}) collective-permute-start(bf16[128,512]{1,0:T(8,128)(2,1)S(1)} %copy-done.10), channel_id=1, source_target_pairs={{0,2},{2,0},{1,3},{3,1},{4,6},{6,4},{5,7},{7,5},{8,10},{10,8},{9,1... | collective-permute-start | bytes 393224 | tf_op jit(solution)/shard_map/ppermute | solution.py:24
  83.9 12.5 %collective-permute-start.12 = (bf16[256,1024]{1,0:T(8,128)(2,1)}, bf16[256,1024]{1,0:T(8,128)(2,1)S(1)}, u32[]{:S(2)}, u32[]{:S(2)}) collective-permute-start(bf16[256,1024]{1,0:T(8,128)(2,1)} %get-tuple-element.60), channel_id=1, source_target_pairs={{0,2},{2,0},{1,3},{3,1},{4,6},{6,4},{5,7},{7,5},{8,10},{10,8},{9,1... | collective-permute-start | bytes 1572872 | tf_op jit(solution)/shard_map/ppermute | solution.py:24
  94.2 6.4 %collective-permute-start.11 = (bf16[528,512]{1,0:T(8,128)(2,1)}, bf16[528,512]{1,0:T(8,128)(2,1)S(1)}, u32[]{:S(2)}, u32[]{:S(2)}) collective-permute-start(bf16[528,512]{1,0:T(8,128)(2,1)} %get-tuple-element.57), channel_id=1, source_target_pairs={{0,1},{1,0},{2,3},{3,2},{4,5},{5,4},{6,7},{7,6},{8,9},{9,8},{10,11... | collective-permute-start | bytes 1622024 | tf_op jit(solution)/shard_map/ppermute | solution.py:24
  97.4 8.6 %collective-permute-start.13 = (bf16[256,512]{1,0:T(8,128)(2,1)S(1)}, bf16[256,512]{1,0:T(8,128)(2,1)S(1)}, u32[]{:S(2)}, u32[]{:S(2)}) collective-permute-start(bf16[256,512]{1,0:T(8,128)(2,1)S(1)} %add_convert_fusion.1), channel_id=1, source_target_pairs={{0,128},{128,0},{1,129},{129,1},{2,130},{130,2},{3,131},{131,3},{4... | collective-permute-start | bytes 786440 | tf_op jit(solution)/shard_map/ppermute | solution.py:24
  99.0 5.9 %collective-permute-start.14 = (f32[16,128]{1,0:T(8,128)}, f32[16,128]{1,0:T(8,128)S(1)}, u32[]{:S(2)}, u32[]{:S(2)}) collective-permute-start(f32[16,128]{1,0:T(8,128)} %get-tuple-element.62), channel_id=1, source_target_pairs={{0,2},{2,0},{1,3},{3,1},{4,6},{6,4},{5,7},{7,5},{8,10},{10,8},{9,1... | collective-permute-start | bytes 24584 | tf_op jit(solution)/shard_map/ppermute | solution.py:24
  100.5 4.8 %collective-permute-start.15 = (f32[16,128]{1,0:T(8,128)}, f32[16,128]{1,0:T(8,128)S(1)}, u32[]{:S(2)}, u32[]{:S(2)}) collective-permute-start(f32[16,128]{1,0:T(8,128)} %get-tuple-element.63), channel_id=1, source_target_pairs={{0,3},{1,2},{2,1},{3,0},{4,7},{5,6},{6,5},{7,4},{8,11},{9,10},{10,... | collective-permute-start | bytes 24584 | tf_op jit(solution)/shard_map/ppermute | solution.py:458
  107.4 34.3 %all-to-all-start.2 = ((bf16[64,4,1664]{2,1,0:T(4,128)(2,1)}), bf16[64,4,1664]{2,1,0:T(4,128)(2,1)S(1)}, u32[]{:S(2)}, u32[]{:S(2)}) async-start(bf16[64,4,1664]{2,1,0:T(4,128)(2,1)} %reshape.293), calls=%async_computation.2 | async-start | bytes 1703936 | tf_op jit(solution)/shard_map/all_to_all | solution.py:468
  142.9 24.7 %all-to-all-start.3 = ((bf16[64,4,1152]{2,1,0:T(4,128)(2,1)}), bf16[64,4,1152]{2,1,0:T(4,128)(2,1)S(1)}, u32[]{:S(2)}, u32[]{:S(2)}) async-start(bf16[64,4,1152]{2,1,0:T(4,128)(2,1)} %broadcast_in_dim.51), calls=%async_computation.3 | async-start | bytes 1179648 | tf_op jit(solution)/shard_map/all_to_all | solution.py:473
  149.8 4.8 %collective-permute-start.16 = (bf16[64,4,2,128]{3,0,1,2:T(8,128)(2,1)S(1)}, bf16[64,4,2,128]{3,0,1,2:T(8,128)(2,1)S(1)}, u32[]{:S(2)}, u32[]{:S(2)}) collective-permute-start(bf16[64,4,2,128]{3,0,1,2:T(8,128)(2,1)S(1)} %bitcast.122), channel_id=1, source_target_pairs={{0,1},{1,0},{2,3},{3,2},{4,5},{5,4},{6,7},{7,6},{8,9},{9,8},{10,11... | collective-permute-start | bytes 393224 | tf_op jit(solution)/shard_map/ppermute | solution.py:24
  151.0 10.3 %collective-permute-start.17 = (bf16[64,4,2,128]{3,0,1,2:T(8,128)(2,1)S(1)}, bf16[64,4,2,128]{3,0,1,2:T(8,128)(2,1)S(1)}, u32[]{:S(2)}, u32[]{:S(2)}) collective-permute-start(bf16[64,4,2,128]{3,0,1,2:T(8,128)(2,1)S(1)} %bitcast.123), channel_id=1, source_target_pairs={{0,2},{2,0},{1,3},{3,1},{4,6},{6,4},{5,7},{7,5},{8,10},{10,8},{9,1... | collective-permute-start | bytes 393224 | tf_op jit(solution)/shard_map/ppermute | solution.py:24
  153.1 11.9 %collective-permute-start.18 = (bf16[64,4,2,128]{3,0,1,2:T(8,128)(2,1)S(1)}, bf16[64,4,2,128]{3,0,1,2:T(8,128)(2,1)S(1)}, u32[]{:S(2)}, u32[]{:S(2)}) collective-permute-start(bf16[64,4,2,128]{3,0,1,2:T(8,128)(2,1)S(1)} %bitcast.124), channel_id=1, source_target_pairs={{0,3},{1,2},{2,1},{3,0},{4,7},{5,6},{6,5},{7,4},{8,11},{9,10},{10,... | collective-permute-start | bytes 393224 | tf_op jit(solution)/shard_map/ppermute | solution.py:482
  (24 other events, 120.4 us)
